TPU v7x, 32 devices: a whole 2x2x4 slice. The times are simulated.
32 devices in a mesh: dp: 4 (over y, core), expert: 8 (over z, x).
Axes of the slice: x: 2, y: 2, z: 4, core: 2. Of those that a mesh axis runs over, the one named last changes fastest.
Arguments:
- block_input: bfloat16 [192, 196, 384], P(('dp', 'expert')), may hold values from -6 to 6
- routes: int32 [2, 192, 196, 1], P(None, ('dp', 'expert')), may hold values from 0 to 7, as said below
- first_gain: float32 [2, 384], replicated, may hold values from 0.5 to 1.5
- first_shift: float32 [2, 384], replicated, may hold values from -2.5 to 2.5
- attend_weight: bfloat16 [2, 384, 1152], replicated, may hold values from -0.3125 to 0.3125
- bias_table: float32 [2, 169, 12], replicated, may hold values from -4 to 4
- output_weight: bfloat16 [2, 384, 384], replicated, may hold values from -1.25 to 1.25
- second_gain: float32 [2, 384], replicated, may hold values from 0.5 to 1.5
- second_shift: float32 [2, 384], replicated, may hold values from -2.5 to 2.5
- router_weight: bfloat16 [2, 384, 8], replicated, may hold values from -0.21875 to 0.21875
- core_up: bfloat16 [2, 384, 1536], replicated, may hold values from -0.3125 to 0.3125
- core_down: bfloat16 [2, 1536, 384], replicated, may hold values from -2.5 to 2.5
- residual_up: bfloat16 [2, 384, 12288], P(None, None, 'expert'), may hold values from -0.15625 to 0.15625
- residual_down: bfloat16 [2, 12288, 384], P(None, 'expert'), may hold values from -1.25 to 1.25
- cotangent: bfloat16 [192, 196, 384], P(('dp', 'expert')), may hold values from -6 to 6
Outputs:
- block_output: bfloat16 [192, 196, 384], P(('dp', 'expert'))
- input_grad: bfloat16 [192, 196, 384], P(('dp', 'expert'))
- first_gain_grad: float32 [2, 384], replicated
- first_shift_grad: float32 [2, 384], replicated
- attend_weight_grad: float32 [2, 384, 1152], replicated
- bias_table_grad: float32 [2, 169, 12], replicated
- output_weight_grad: float32 [2, 384, 384], replicated
- second_gain_grad: float32 [2, 384], replicated
- second_shift_grad: float32 [2, 384], replicated
- router_weight_grad: float32 [2, 384, 8], replicated
- core_up_grad: float32 [2, 384, 1536], replicated
- core_down_grad: float32 [2, 1536, 384], replicated
- residual_up_grad: float32 [2, 384, 12288], P(None, None, 'expert')
- residual_down_grad: float32 [2, 12288, 384], P(None, 'expert')
Inputs may be any that keep to these rules, and one draw needn't show every extreme that they name: `routes`: each token's expert in each block; every expert is named by some token; in each block one expert, drawn from the seed, is named by about two fifths of all tokens.
All inputs are finite; a program needn't handle non-finite values.
Results may differ from a plain program's by a relative error of at most 0.022.
Values may be sent and summed in bfloat16 or wider, within the bound.
No kernel may reach another device: no remote copies, remote signals or barrier semaphores. Data moves between devices by JAX's collectives and lax.ppermute only.
A program may use at most 256 MiB of HBM per device.

v0:
```python
from functools import partial

import jax
import jax.numpy as jnp
from jax import lax
from jax.sharding import PartitionSpec as P

D = 384
HEADS = 12
HD = 32
FF = 1536
EXPERTS = 8
WIN = 7
SIDE = 14
SHIFT = 3
LAYERS = 2
HW = 196
CAP = 184
OFFSETS = 169


eps_norm = 1e-05
mask_fill = -100.0
precise = lax.Precision.HIGHEST


def layer_norm(values, norm_gain, norm_shift):
    middle = jnp.mean(values, axis=-1, keepdims=True)
    centred = values - middle
    spread = jnp.mean(centred * centred, axis=-1, keepdims=True)
    return centred * lax.rsqrt(spread + eps_norm) * norm_gain + norm_shift


def to_windows(grid_in, window):
    images = grid_in.shape[0]
    grid_side = grid_in.shape[1]
    channels = grid_in.shape[3]
    per_side = grid_side // window
    pieces = grid_in.reshape(images, per_side, window, per_side, window, channels)
    return pieces.transpose(0, 1, 3, 2, 4, 5).reshape(
        images * per_side * per_side, window * window, channels
    )


def from_windows(blocks, images, grid_side, window):
    per_side = grid_side // window
    channels = blocks.shape[-1]
    pieces = blocks.reshape(images, per_side, per_side, window, window, channels)
    return pieces.transpose(0, 1, 3, 2, 4, 5).reshape(images, grid_side, grid_side, channels)


def relative_index(window):
    places = jnp.arange(window * window, dtype=jnp.int32)
    rows_at = places // window
    cols_at = places % window
    row_delta = rows_at[:, None] - rows_at[None, :] + window - 1
    col_delta = cols_at[:, None] - cols_at[None, :] + window - 1
    return row_delta * (2 * window - 1) + col_delta


def band_mask(grid_side, window, offset):
    coords = jnp.arange(grid_side, dtype=jnp.int32)
    bands = (coords >= grid_side - window).astype(jnp.int32) + (
        coords >= grid_side - offset
    ).astype(jnp.int32)
    labels = bands[:, None] * 3 + bands[None, :]
    pieces = to_windows(labels[None, :, :, None], window)[:, :, 0]
    return jnp.where(pieces[:, :, None] == pieces[:, None, :], 0.0, mask_fill).astype(jnp.float32)


def window_scores(queries, key_heads, position, mask_rows, images):
    scores = (
        jnp.einsum("wqhd,wkhd->whqk", queries, key_heads, preferred_element_type=jnp.float32)
        * HD ** (-0.5)
        + position[None]
    )
    count_windows = scores.shape[0]
    length = scores.shape[2]
    masked = scores.reshape(images, -1, HEADS, length, length) + mask_rows[None, :, None]
    return masked.reshape(count_windows, HEADS, length, length)


def expert_apply(up_sum, down_sum, received):
    inner_act = jnp.einsum("ncd,df->ncf", received, up_sum, preferred_element_type=jnp.float32)
    hidden = jax.nn.gelu(inner_act, approximate=False).astype(jnp.bfloat16)
    part_out = jnp.einsum(
        "ncf,fd->ncd", hidden, down_sum, preferred_element_type=jnp.float32
    ).astype(jnp.bfloat16)
    returned = lax.all_to_all(part_out, "expert", split_axis=0, concat_axis=0, tiled=True)
    return (returned, received)


def spread_columns(piece, start, axis_at, full_width):
    shape_full = list(piece.shape)
    shape_full[axis_at] = full_width
    empty = jnp.zeros(tuple(shape_full), jnp.float32)
    return lax.dynamic_update_slice_in_dim(empty, piece, start, axis_at)


def body(
    block_input,
    routes,
    first_gain,
    first_shift,
    attend_weight,
    bias_table,
    output_weight,
    second_gain,
    second_shift,
    router_weight,
    core_up,
    core_down,
    residual_up,
    residual_down,
    cotangent,
):
    groups = lax.axis_size("expert")
    slices = groups // EXPERTS
    group_part = lax.axis_index("expert") % slices
    images = block_input.shape[0]
    rows_total = images * HW
    length = WIN * WIN
    hidden_part = residual_up.shape[2]
    slot_count = EXPERTS * CAP
    count_windows = images * (SIDE // WIN) * (SIDE // WIN)
    picker = (
        relative_index(WIN).reshape(-1)[:, None] == jnp.arange(OFFSETS, dtype=jnp.int32)[None, :]
    ).astype(jnp.float32)
    expert_ids = jnp.arange(EXPERTS, dtype=jnp.int32)
    slot_ids = jnp.arange(slot_count, dtype=jnp.int32)
    empty_row = jnp.zeros((1, D), jnp.float32)
    carried = block_input.astype(jnp.float32).reshape(images, SIDE, SIDE, D)
    kept = []
    for depth in range(LAYERS):
        offset = SHIFT * (depth % 2)
        mask_rows = band_mask(SIDE, WIN, offset)
        position = (
            jnp.dot(picker, bias_table[depth], precision=precise)
            .reshape(length, length, HEADS)
            .transpose(2, 0, 1)
        )
        normed = layer_norm(carried, first_gain[depth], first_shift[depth])
        blocks = to_windows(jnp.roll(normed, (-offset, -offset), axis=(1, 2)), WIN).astype(
            jnp.bfloat16
        )
        joined = jnp.einsum(
            "wld,de->wle", blocks, attend_weight[depth], preferred_element_type=jnp.float32
        ).astype(jnp.bfloat16)
        head_split = joined.reshape(count_windows, length, 3, HEADS, HD)
        scores = window_scores(
            head_split[:, :, 0], head_split[:, :, 1], position, mask_rows, images
        )
        top_score = jnp.max(scores, axis=-1, keepdims=True)
        raised = jnp.exp(scores - top_score)
        total_mass = jnp.sum(raised, axis=-1, keepdims=True)
        log_mass = top_score + jnp.log(total_mass)
        weights = (raised / total_mass).astype(jnp.bfloat16)
        mixed = jnp.einsum(
            "whqk,wkhd->wqhd", weights, head_split[:, :, 2], preferred_element_type=jnp.float32
        )
        mixed = mixed.astype(jnp.bfloat16).reshape(count_windows, length, D)
        projected = jnp.einsum(
            "wld,de->wle", mixed, output_weight[depth], preferred_element_type=jnp.float32
        )
        middle = carried + jnp.roll(
            from_windows(projected, images, SIDE, WIN), (offset, offset), axis=(1, 2)
        )
        tokens = middle.reshape(rows_total, D)
        normed_two = layer_norm(tokens, second_gain[depth], second_shift[depth]).astype(
            jnp.bfloat16
        )
        logits = jnp.dot(normed_two, router_weight[depth], preferred_element_type=jnp.float32)
        router_probs = jax.nn.softmax(logits, axis=-1)
        route_ids = routes[depth].reshape(rows_total)
        chosen = route_ids[:, None] == expert_ids[None, :]
        gate_values = jnp.sum(jnp.where(chosen, router_probs, 0.0), axis=-1)
        rank_counts = jnp.cumsum(chosen.astype(jnp.int32), axis=0) - 1
        slot_index = jnp.sum(jnp.where(chosen, rank_counts, 0), axis=-1)
        target = jnp.where(slot_index < CAP, route_ids * CAP + slot_index, slot_count)
        placing = (target[:, None] == slot_ids[None, :]).astype(jnp.bfloat16)
        buffers = jnp.einsum(
            "ts,td->sd", placing, normed_two, preferred_element_type=jnp.float32
        ).astype(jnp.bfloat16)
        outgoing = jnp.repeat(buffers.reshape(EXPERTS, CAP, D), slices, axis=0)
        up_slice = lax.dynamic_slice_in_dim(
            core_up[depth], group_part * hidden_part, hidden_part, 1
        )
        down_slice = lax.dynamic_slice_in_dim(
            core_down[depth], group_part * hidden_part, hidden_part, 0
        )
        up_sum = (up_slice.astype(jnp.float32) + residual_up[depth].astype(jnp.float32)).astype(
            jnp.bfloat16
        )
        down_sum = (
            down_slice.astype(jnp.float32) + residual_down[depth].astype(jnp.float32)
        ).astype(jnp.bfloat16)
        returned, arrived = expert_apply(
            up_sum,
            down_sum,
            lax.all_to_all(outgoing, "expert", split_axis=0, concat_axis=0, tiled=True),
        )
        expert_out = jnp.sum(
            returned.astype(jnp.float32).reshape(EXPERTS, slices, CAP, D), axis=1
        ).reshape(slot_count, D)
        gathered = jnp.take(jnp.concatenate([expert_out, empty_row], axis=0), target, axis=0)
        kept.append(
            (
                carried,
                offset,
                mask_rows,
                position,
                blocks,
                head_split,
                log_mass,
                mixed,
                tokens,
                normed_two,
                router_probs,
                chosen,
                gate_values,
                target,
                placing,
                gathered,
                arrived,
                up_sum,
                down_sum,
            )
        )
        carried = (tokens + gate_values[:, None] * gathered).reshape(images, SIDE, SIDE, D)
    block_output = carried.reshape(images, HW, D).astype(jnp.bfloat16)
    grad_carried = cotangent.astype(jnp.float32).reshape(rows_total, D)
    collected = [None] * LAYERS
    for depth in reversed(range(LAYERS)):
        (
            grid_before,
            offset,
            mask_rows,
            position,
            blocks,
            head_split,
            log_mass,
            mixed,
            tokens,
            normed_two,
            router_probs,
            chosen,
            gate_values,
            target,
            placing,
            gathered,
            arrived,
            up_sum,
            down_sum,
        ) = kept[depth]
        gate_grad = jnp.sum(grad_carried * gathered, axis=-1)
        logit_grad = (
            (gate_values * gate_grad)[:, None] * (chosen.astype(jnp.float32) - router_probs)
        ).astype(jnp.bfloat16)
        router_grad = jnp.einsum(
            "td,te->de", normed_two, logit_grad, preferred_element_type=jnp.float32
        )
        scaled = (gate_values[:, None] * grad_carried).astype(jnp.bfloat16)
        grad_buffers = jnp.einsum(
            "ts,td->sd", placing, scaled, preferred_element_type=jnp.float32
        ).astype(jnp.bfloat16)
        incoming = lax.all_to_all(
            jnp.repeat(grad_buffers.reshape(EXPERTS, CAP, D), slices, axis=0),
            "expert",
            split_axis=0,
            concat_axis=0,
            tiled=True,
        )
        inner_act = jnp.einsum("ncd,df->ncf", arrived, up_sum, preferred_element_type=jnp.float32)
        hidden, gelu_pull = jax.vjp(partial(jax.nn.gelu, approximate=False), inner_act)
        hidden_low = hidden.astype(jnp.bfloat16)
        grad_hidden = jnp.einsum(
            "ncd,fd->ncf", incoming, down_sum, preferred_element_type=jnp.float32
        )
        grad_inner = gelu_pull(grad_hidden)[0].astype(jnp.bfloat16)
        down_local = jnp.einsum(
            "ncf,ncd->fd", hidden_low, incoming, preferred_element_type=jnp.float32
        )
        up_local = jnp.einsum(
            "ncd,ncf->df", arrived, grad_inner, preferred_element_type=jnp.float32
        )
        grad_rows = jnp.einsum(
            "ncf,df->ncd", grad_inner, up_sum, preferred_element_type=jnp.float32
        ).astype(jnp.bfloat16)
        grad_back = lax.all_to_all(grad_rows, "expert", split_axis=0, concat_axis=0, tiled=True)
        grad_slots = jnp.sum(
            grad_back.astype(jnp.float32).reshape(EXPERTS, slices, CAP, D), axis=1
        ).reshape(slot_count, D)
        grad_normed = jnp.take(jnp.concatenate([grad_slots, empty_row], axis=0), target, axis=0)
        grad_normed = grad_normed + jnp.einsum(
            "te,de->td", logit_grad, router_weight[depth], preferred_element_type=jnp.float32
        )
        second_pull = jax.vjp(layer_norm, tokens, second_gain[depth], second_shift[depth])[1]
        grad_tokens, gain_two_grad, shift_two_grad = second_pull(grad_normed)
        grad_middle = (grad_carried + grad_tokens).reshape(images, SIDE, SIDE, D)
        grad_z = to_windows(jnp.roll(grad_middle, (-offset, -offset), axis=(1, 2)), WIN).astype(
            jnp.bfloat16
        )
        output_grad = jnp.einsum("wld,wle->de", mixed, grad_z, preferred_element_type=jnp.float32)
        grad_mixed = jnp.einsum(
            "wle,de->wld", grad_z, output_weight[depth], preferred_element_type=jnp.float32
        )
        grad_mixed = grad_mixed.astype(jnp.bfloat16).reshape(count_windows, length, HEADS, HD)
        queries = head_split[:, :, 0]
        key_heads = head_split[:, :, 1]
        value_heads = head_split[:, :, 2]
        scores = window_scores(queries, key_heads, position, mask_rows, images)
        weights_full = jnp.exp(scores - log_mass)
        grad_weights = jnp.einsum(
            "wqhd,wkhd->whqk", grad_mixed, value_heads, preferred_element_type=jnp.float32
        )
        grad_values = jnp.einsum(
            "whqk,wqhd->wkhd",
            weights_full.astype(jnp.bfloat16),
            grad_mixed,
            preferred_element_type=jnp.float32,
        )
        row_dot = jnp.sum(weights_full * grad_weights, axis=-1, keepdims=True)
        grad_scores = (weights_full * (grad_weights - row_dot)).astype(jnp.bfloat16)
        grad_queries = jnp.einsum(
            "whqk,wkhd->wqhd", grad_scores, key_heads, preferred_element_type=jnp.float32
        ) * HD ** (-0.5)
        grad_keys = jnp.einsum(
            "whqk,wqhd->wkhd", grad_scores, queries, preferred_element_type=jnp.float32
        ) * HD ** (-0.5)
        score_total = jnp.sum(grad_scores.astype(jnp.float32), axis=0).reshape(
            HEADS, length * length
        )
        table_grad = jnp.dot(score_total, picker, precision=precise).T
        grad_joined = (
            jnp.stack([grad_queries, grad_keys, grad_values], axis=2)
            .reshape(count_windows, length, 3 * D)
            .astype(jnp.bfloat16)
        )
        attend_grad = jnp.einsum(
            "wld,wle->de", blocks, grad_joined, preferred_element_type=jnp.float32
        )
        grad_blocks = jnp.einsum(
            "wle,de->wld", grad_joined, attend_weight[depth], preferred_element_type=jnp.float32
        )
        grad_normed_one = jnp.roll(
            from_windows(grad_blocks, images, SIDE, WIN), (offset, offset), axis=(1, 2)
        )
        first_pull = jax.vjp(layer_norm, grid_before, first_gain[depth], first_shift[depth])[1]
        grad_before, gain_one_grad, shift_one_grad = first_pull(grad_normed_one)
        grad_carried = (grad_middle + grad_before).reshape(rows_total, D)
        collected[depth] = (
            gain_one_grad,
            shift_one_grad,
            attend_grad,
            table_grad,
            output_grad,
            gain_two_grad,
            shift_two_grad,
            router_grad,
            up_local,
            down_local,
        )
    input_grad = grad_carried.reshape(images, HW, D).astype(jnp.bfloat16)
    stacked = [
        jnp.stack([collected[depth][member] for depth in range(LAYERS)]) for member in range(10)
    ]
    (
        local_gain_one,
        local_shift_one,
        local_attend,
        local_table,
        local_output,
        local_gain_two,
        local_shift_two,
        local_router,
        local_up,
        local_down,
    ) = stacked
    residual_up_grad, residual_down_grad = (
        lax.psum(local_up.astype(jnp.bfloat16), "dp").astype(jnp.float32),
        lax.psum(local_down.astype(jnp.bfloat16), "dp").astype(jnp.float32),
    )
    start = group_part * hidden_part
    (
        first_gain_grad,
        first_shift_grad,
        attend_weight_grad,
        bias_table_grad,
        output_weight_grad,
        second_gain_grad,
        second_shift_grad,
        router_weight_grad,
    ) = lax.psum(
        (
            local_gain_one,
            local_shift_one,
            local_attend,
            local_table,
            local_output,
            local_gain_two,
            local_shift_two,
            local_router,
        ),
        ("dp", "expert"),
    )
    core_up_grad, core_down_grad = (
        lax.psum(
            spread_columns(residual_up_grad, start, 2, FF).astype(jnp.bfloat16), "expert"
        ).astype(jnp.float32),
        lax.psum(
            spread_columns(residual_down_grad, start, 1, FF).astype(jnp.bfloat16), "expert"
        ).astype(jnp.float32),
    )
    return (
        block_output,
        input_grad,
        first_gain_grad,
        first_shift_grad,
        attend_weight_grad,
        bias_table_grad,
        output_weight_grad,
        second_gain_grad,
        second_shift_grad,
        router_weight_grad,
        core_up_grad,
        core_down_grad,
        residual_up_grad,
        residual_down_grad,
    )


def solution(mesh):
    placed = (
        P(("dp", "expert"), None, None),
        P(None, ("dp", "expert"), None, None),
        P(),
        P(),
        P(),
        P(),
        P(),
        P(),
        P(),
        P(),
        P(),
        P(),
        P(None, None, "expert"),
        P(None, "expert", None),
        P(("dp", "expert"), None, None),
    )
    return jax.shard_map(
        body,
        mesh=mesh,
        in_specs=placed,
        out_specs=(
            P(("dp", "expert"), None, None),
            P(("dp", "expert"), None, None),
            P(),
            P(),
            P(),
            P(),
            P(),
            P(),
            P(),
            P(),
            P(),
            P(),
            P(None, None, "expert"),
            P(None, "expert", None),
        ),
        check_vma=False,
    )
```

profile of v0, /device:TPU:1, one launch (start us, length us, event | category | flops | bytes accessed | tf_op | source)
XLA Modules:
  0.0 1043.0 jit_solution(3037288531431009640)
XLA Ops:
  24.2 5.1 convolution_convert_fusion.1
  29.2 8.0 copy.183
  37.3 5.0 fusion.161
  50.6 6.5 copy.255
  57.1 6.6 reshape.877
  82.3 6.6 all-to-all-start
  92.4 23.2 %all-to-all-done = bf16[8,184,384]{2,1,0:T(8,128)(2,1)} async-done(((bf16[8,184,384]{2,1,0:T(8,128)(2,1)}), bf16[8,184,384]{2,1,0:T(8,128)(2,1)}, u32[]{:S(2)}, u32[]{:S(2)}) %all-to-all-start) | async-done | bytes 1130528 | tf_op jit(solution)/shard_map/all_to_all | solution.py:200
  115.5 6.6 fusion.59
  122.1 21.4 %multiply_convert_fusion.1 = (bf16[8,184,1536]{2,1,0:T(8,128)(2,1)S(1)}, f32[8,184,1536]{2,1,0:T(8,128)}) fusion(f32[8,184,1536]{2,1,0:T(8,128)S(1)} %get-tuple-element.149, u8[184,1536]{1,0:T(8,128)(4,1)S(1)} %get-tuple-element.74, u8[184,1536]{1,0:T(8,128)(4,1)S(1)} %get-tuple-element.73), kind=kLoop, calls=%fused_computation.34 | loop fusion | flops 158269440 | bytes 23175168 | tf_op jit(solution)/shard_map/convert_element_type | solution.py:85
  149.3 5.1 all-to-all-start.1
  161.9 18.8 %all-to-all-done.1 = bf16[8,184,384]{2,1,0:T(8,128)(2,1)} async-done(((bf16[8,184,384]{2,1,0:T(8,128)(2,1)}), bf16[8,184,384]{2,1,0:T(8,128)(2,1)}, u32[]{:S(2)}, u32[]{:S(2)}) %all-to-all-start.1) | async-done | bytes 1130528 | tf_op jit(solution)/shard_map/all_to_all | solution.py:89
  182.1 4.2 gather_fusion
  198.4 5.0 convolution_convert_fusion
  203.5 8.2 copy.197
  211.7 5.0 fusion.163
  220.1 4.9 fusion.69
  225.0 7.0 copy.256
  232.0 6.1 reshape.878
  255.9 5.0 all-to-all-start.2
  266.3 21.0 %all-to-all-done.2 = bf16[8,184,384]{2,1,0:T(8,128)(2,1)} async-done(((bf16[8,184,384]{2,1,0:T(8,128)(2,1)}), bf16[8,184,384]{2,1,0:T(8,128)(2,1)}, u32[]{:S(2)}, u32[]{:S(2)}) %all-to-all-start.2) | async-done | bytes 1130528 | tf_op jit(solution)/shard_map/all_to_all | solution.py:200
  287.3 5.2 all-to-all-start.4
  292.5 6.6 fusion.60
  302.5 21.4 %multiply_convert_fusion = (bf16[8,184,1536]{2,1,0:T(8,128)(2,1)}, f32[8,184,1536]{2,1,0:T(8,128)}) fusion(f32[8,184,1536]{2,1,0:T(8,128)S(1)} %get-tuple-element.154, u8[184,1536]{1,0:T(8,128)(4,1)S(1)} %get-tuple-element.72, u8[184,1536]{1,0:T(8,128)(4,1)S(1)} %get-tuple-element.71), kind=kLoop, calls=%fused_computation.21 | loop fusion | flops 158269440 | bytes 23175168 | tf_op jit(solution)/shard_map/convert_element_type | solution.py:85
  323.9 9.7 add_convert_fusion.1
  339.4 5.6 all-to-all-start.5
  346.4 6.5 convolution_convert_fusion.4
  352.9 18.3 %all-to-all-done.5 = bf16[8,184,384]{2,1,0:T(8,128)(2,1)S(1)} async-done(((bf16[8,184,384]{2,1,0:T(8,128)(2,1)}), bf16[8,184,384]{2,1,0:T(8,128)(2,1)S(1)}, u32[]{:S(2)}, u32[]{:S(2)}) %all-to-all-start.5) | async-done | bytes 1130528 | tf_op jit(solution)/shard_map/all_to_all | solution.py:289
  371.2 5.3 all-to-all-start.3
  377.3 6.4 fusion.45
  383.7 4.3 fusion.47
  388.1 14.6 %all-to-all-done.3 = bf16[8,184,384]{2,1,0:T(8,128)(2,1)} async-done(((bf16[8,184,384]{2,1,0:T(8,128)(2,1)}), bf16[8,184,384]{2,1,0:T(8,128)(2,1)}, u32[]{:S(2)}, u32[]{:S(2)}) %all-to-all-start.3) | async-done | bytes 1130528 | tf_op jit(solution)/shard_map/all_to_all | solution.py:89
  405.5 4.2 gather_fusion.2
  409.7 6.3 gather_fusion.1
  430.5 4.1 copy.210
  434.7 7.9 fusion.51
  442.6 7.2 multiply_reduce_fusion.1
  449.8 5.3 convert_reduce_fusion
  463.8 4.0 copy.231
  467.9 18.0 %copy.257 = bf16[24,49,3,12,32]{4,3,2,1,0:T(8,128)(2,1)} copy(bf16[24,49,3,12,32]{1,4,3,0,2:T(8,128)(2,1)} %copy-done.8) | data formatting | bytes 5419008 | tf_op jit(solution)/shard_map/convert_element_type | solution.py:337
  485.9 16.0 %reshape.879 = bf16[6,2,2,7,7,1152]{5,4,3,2,1,0:T(8,128)(2,1)S(1)} reshape(bf16[24,49,3,12,32]{4,3,2,1,0:T(8,128)(2,1)} %copy.257) | data formatting | bytes 5419008 | tf_op jit(solution)/shard_map/convert_element_type | solution.py:337
  501.9 3.8 convolution_bitcast_fusion.8
  510.5 8.8 copy.232
  532.6 5.7 all-to-all-start.6
  546.5 18.0 %all-to-all-done.6 = bf16[8,184,384]{2,1,0:T(8,128)(2,1)} async-done(((bf16[8,184,384]{2,1,0:T(8,128)(2,1)}), bf16[8,184,384]{2,1,0:T(8,128)(2,1)}, u32[]{:S(2)}, u32[]{:S(2)}) %all-to-all-start.6) | async-done | bytes 1130528 | tf_op jit(solution)/shard_map/all_to_all | solution.py:266
  564.5 10.7 %add_convert_fusion = bf16[8,184,1536]{2,1,0:T(8,128)(2,1)S(1)} fusion(f32[8,184,1536]{2,1,0:T(8,128)} %get-tuple-element.134, f32[8,184,1536]{2,1,0:T(8,128)} %copy-done.26, bf16[8,184,384]{2,1,0:T(8,128)(2,1)} %all-to-all-done.6, bf16[2,1536,384]{2,1,0:T(8,128)(2,1)S(1)} %copy-done.138, bf16[2,1536,384]{2,1,0:T(8,128)(2,1)} %param.28), kind=kOutput, calls=%fused_computation.19 | convolution fusion | flops 1770455040 | bytes 26099712 | tf_op jit(solution)/shard_map/ncd,fd->ncf/dot_general | solution.py:276
  581.0 5.2 all-to-all-start.7
  590.0 5.4 fusion.46
  602.2 10.7 %all-to-all-done.7 = bf16[8,184,384]{2,1,0:T(8,128)(2,1)S(1)} async-done(((bf16[8,184,384]{2,1,0:T(8,128)(2,1)}), bf16[8,184,384]{2,1,0:T(8,128)(2,1)S(1)}, u32[]{:S(2)}, u32[]{:S(2)}) %all-to-all-start.7) | async-done | bytes 1130528 | tf_op jit(solution)/shard_map/all_to_all | solution.py:289
  613.1 4.2 gather_fusion.3
  628.6 10.9 %multiply_reduce_fusion = (f32[24,12,49]{2,1,0:T(8,128)S(1)}, f32[24,12,49,49]{2,3,1,0:T(8,128)}) fusion(f32[24,12,49,49]{2,3,1,0:T(8,128)} %copy-done, f32[24,12,49]{2,1,0:T(8,128)} %log_add_fusion, bf16[24,49,12,32]{1,3,2,0:T(8,128)(2,1)S(1)} %bitcast.370, bf16[24,49,3,12,32]{1,4,3,2,0:T(8,128)(2,1)} %bitcast.356), kind=kOutput, calls=%fused_computation.50 | convolution fusion | flops 46315584 | bytes 14539008 | tf_op jit(solution)/shard_map/wqhd,wkhd->whqk/dot_general | solution.py:313
  639.5 58.6 %all-reduce.18.cloned.1.call-done = (bf16[2,384,1536]{2,1,0:T(8,128)(2,1)}, bf16[2,1536,384]{2,1,0:T(8,128)(2,1)}) async-done(((bf16[2,384,1536]{2,1,0:T(8,128)(2,1)}, bf16[2,1536,384]{2,1,0:T(8,128)(2,1)}), (bf16[2,384,1536]{2,1,0:T(8,128)(2,1)}, bf16[2,1536,384]{2,1,0:T(8,128)(2,1)})) %all-reduce.18.cloned.1.call-update) | async-done | bytes 4718608 | tf_op jit(solution)/shard_map/psum | solution.py:380
  698.0 4.5 convert_element_type.425
  702.5 4.3 convert_element_type.426
  707.8 8.3 convert_reduce_fusion.1
  730.4 4.1 copy.229
  734.5 18.1 %copy.258 = bf16[24,49,3,12,32]{4,3,2,1,0:T(8,128)(2,1)} copy(bf16[24,49,3,12,32]{1,4,3,0,2:T(8,128)(2,1)} %copy-done.9) | data formatting | bytes 5419008 | tf_op jit(solution)/shard_map/convert_element_type | solution.py:337
  755.6 7.7 copy.230
  763.3 17.4 %reshape.880 = bf16[6,2,2,7,7,1152]{5,4,3,2,1,0:T(8,128)(2,1)} reshape(bf16[24,49,3,12,32]{4,3,2,1,0:T(8,128)(2,1)} %copy.258) | data formatting | bytes 5419008 | tf_op jit(solution)/shard_map/convert_element_type | solution.py:337
  780.7 4.7 fusion.165
  806.4 43.6 %all-reduce.6 = (f32[2,384]{1,0:T(2,128)}, f32[2,384]{1,0:T(2,128)}, f32[2,169,12]{1,2,0:T(8,128)S(1)}, f32[2,384]{1,0:T(2,128)}, f32[2,384]{1,0:T(2,128)}, /*index=5*/f32[2,384,8]{1,2,0:T(8,128)}) all-reduce(f32[2,384]{1,0:T(2,128)S(1)} %pad_maximum_fusion.13, ...), channel_id=1, replica_groups=mesh['dp'=4,'expert'=8] {'dp','expert'}, use_global_device_ids=true, to_apply=%region_38.40 | all-reduce | flops 13272 | bytes 106176 | tf_op jit(solution)/shard_map/psum | solution.py:393
  854.1 28.4 %all-reduce.16.cloned.1.call-done = (bf16[2,384,1536]{2,1,0:T(8,128)(2,1)}, bf16[2,1536,384]{2,1,0:T(8,128)(2,1)}) async-done(((bf16[2,384,1536]{2,1,0:T(8,128)(2,1)}, bf16[2,1536,384]{2,1,0:T(8,128)(2,1)}), (bf16[2,384,1536]{2,1,0:T(8,128)(2,1)}, bf16[2,1536,384]{2,1,0:T(8,128)(2,1)})) %all-reduce.16.cloned.1.call-update) | async-done | bytes 4718608 | tf_op jit(solution)/shard_map/psum | solution.py:407
  882.5 4.6 convert_element_type.423
  889.7 141.4 %all-reduce.14.cloned.1.call-done = (f32[2,384,1152]{2,1,0:T(8,128)}, f32[2,384,384]{2,1,0:T(8,128)}) async-done(((f32[2,384,1152]{2,1,0:T(8,128)}, f32[2,384,384]{2,1,0:T(8,128)}), (f32[2,384,1152]{2,1,0:T(8,128)}, f32[2,384,384]{2,1,0:T(8,128)})) %all-reduce.14.cloned.1.call-update) | async-done | bytes 4718608 | tf_op jit(solution)/shard_map/psum | solution.py:393
  1031.1 4.1 copy.315
  (551 shorter events, 237.5 us)
Async XLA Ops:
  12.3 9.4 copy-start.14
  13.5 8.2 copy-start.59
  13.5 8.1 copy-start.61
  29.2 8.0 copy-start.72
  57.1 6.6 copy-start.45
  69.8 8.8 copy-start.79
  70.6 91.2 %copy-start.73 = (s32[1176]{0:T(1024)}, s32[1176]{0:T(1024)S(1)}, u32[]{:S(2)}) copy-start(s32[1176]{0:T(1024)S(1)} %eq.174) | copy-start | bytes 14116
  74.1 87.1 %copy-start.107 = (s32[1176]{0:T(1024)}, s32[1176]{0:T(1024)S(1)}, u32[]{:S(2)}) copy-start(s32[1176]{0:T(1024)S(1)} %get-tuple-element.132) | copy-start | bytes 14116
  74.8 83.7 %copy-start.101 = (f32[384]{0:T(512)}, f32[384]{0:T(512)S(1)}, u32[]{:S(2)}) copy-start(f32[384]{0:T(512)S(1)} %get-tuple-element.171) | copy-start | bytes 4612
  82.3 33.3 %all-to-all-start = ((bf16[8,184,384]{2,1,0:T(8,128)(2,1)}), bf16[8,184,384]{2,1,0:T(8,128)(2,1)}, u32[]{:S(2)}, u32[]{:S(2)}) async-start(bf16[8,184,384]{2,1,0:T(8,128)(2,1)} %bitcast.386), calls=%async_computation | async-start | bytes 2260992 | tf_op jit(solution)/shard_map/all_to_all | solution.py:200
  122.1 21.5 %copy-start.26 = (f32[8,184,1536]{2,1,0:T(8,128)}, f32[8,184,1536]{2,1,0:T(8,128)S(1)}, u32[]{:S(2)}) copy-start(f32[8,184,1536]{2,1,0:T(8,128)S(1)} %get-tuple-element.149) | copy-start | bytes 27131908
  122.1 23.6 %copy-start.137 = (bf16[2,1536,384]{2,1,0:T(8,128)(2,1)S(1)}, bf16[2,1536,384]{2,1,0:T(8,128)(2,1)}, u32[]{:S(2)}) copy-start(bf16[2,1536,384]{2,1,0:T(8,128)(2,1)} %param.30) | copy-start | bytes 7077892
  122.1 23.6 %copy-start.139 = (bf16[2,1536,384]{2,1,0:T(8,128)(2,1)S(1)}, bf16[2,1536,384]{2,1,0:T(8,128)(2,1)}, u32[]{:S(2)}) copy-start(bf16[2,1536,384]{2,1,0:T(8,128)(2,1)} %param.28) | copy-start | bytes 7077892
  145.7 8.7 copy-start.133
  145.7 8.7 copy-start.134
  149.3 9.2 copy-start.115
  149.3 31.4 %all-to-all-start.1 = ((bf16[8,184,384]{2,1,0:T(8,128)(2,1)}), bf16[8,184,384]{2,1,0:T(8,128)(2,1)}, u32[]{:S(2)}, u32[]{:S(2)}) async-start(bf16[8,184,384]{2,1,0:T(8,128)(2,1)} %convolution_convert_fusion.5), calls=%async_computation.1 | async-start | bytes 2260992 | tf_op jit(solution)/shard_map/all_to_all | solution.py:89
  161.3 25.0 %copy-start.87 = (s32[2048]{0:T(1024)}, s32[2048]{0:T(1024)S(1)}, u32[]{:S(2)}) copy-start(s32[2048]{0:T(1024)S(1)} %pad_clamp_fusion.1) | copy-start | bytes 24580
  161.6 19.1 %copy-start.69 = (f32[1176,8]{0,1:T(8,128)}, f32[1176,8]{0,1:T(8,128)S(1)}, u32[]{:S(2)}) copy-start(f32[1176,8]{0,1:T(8,128)S(1)} %get-tuple-element.151) | copy-start | bytes 112900
  161.6 24.7 %copy-start.85 = (f32[1176]{0:T(1024)}, f32[1176]{0:T(1024)S(1)}, u32[]{:S(2)}) copy-start(f32[1176]{0:T(1024)S(1)} %get-tuple-element.150) | copy-start | bytes 14116
  161.7 24.6 %copy-start.95 = (f32[1176]{0:T(1024)}, f32[1176]{0:T(1024)S(1)}, u32[]{:S(2)}) copy-start(f32[1176]{0:T(1024)S(1)} %fusion.131) | copy-start | bytes 14116
  161.8 24.5 %copy-start.89 = (f32[1176]{0:T(1024)}, f32[1176]{0:T(1024)S(1)}, u32[]{:S(2)}) copy-start(f32[1176]{0:T(1024)S(1)} %select_reduce_fusion.1) | copy-start | bytes 14116
  161.8 90.4 %copy-start.109 = (s32[1176]{0:T(1024)}, s32[1176]{0:T(1024)S(1)}, u32[]{:S(2)}) copy-start(s32[1176]{0:T(1024)S(1)} %get-tuple-element.124) | copy-start | bytes 14116
  161.8 254.2 %copy-start.116 = (pred[1176]{0:T(1024)(128)(4,1)}, pred[1176]{0:T(1024)(128)(4,1)S(1)}, u32[]{:S(2)}) copy-start(pred[1176]{0:T(1024)(128)(4,1)S(1)} %get-tuple-element.123) | copy-start | bytes 3532
  188.9 60.6 %copy-start.4 = (f32[1176,384]{1,0:T(8,128)}, f32[1176,384]{1,0:T(8,128)S(1)}, u32[]{:S(2)}) copy-start(f32[1176,384]{1,0:T(8,128)S(1)} %get-tuple-element.130) | copy-start | bytes 5419012
  252.2 10.0 copy-start.29
  255.9 31.4 %all-to-all-start.2 = ((bf16[8,184,384]{2,1,0:T(8,128)(2,1)}), bf16[8,184,384]{2,1,0:T(8,128)(2,1)}, u32[]{:S(2)}, u32[]{:S(2)}) async-start(bf16[8,184,384]{2,1,0:T(8,128)(2,1)} %bitcast.47), calls=%async_computation.2 | async-start | bytes 2260992 | tf_op jit(solution)/shard_map/all_to_all | solution.py:200
  287.3 36.6 %all-to-all-start.4 = ((bf16[8,184,384]{2,1,0:T(8,128)(2,1)}), bf16[8,184,384]{2,1,0:T(8,128)(2,1)S(1)}, u32[]{:S(2)}, u32[]{:S(2)}) async-start(bf16[8,184,384]{2,1,0:T(8,128)(2,1)} %bitcast.53), calls=%async_computation.4 | async-start | bytes 2260992 | tf_op jit(solution)/shard_map/all_to_all | solution.py:266
  323.9 11.8 %copy-start.140 = (bf16[2,384,1536]{2,1,0:T(8,128)(2,1)S(1)}, bf16[2,384,1536]{2,1,0:T(8,128)(2,1)}, u32[]{:S(2)}) copy-start(bf16[2,384,1536]{2,1,0:T(8,128)(2,1)} %param.29) | copy-start | bytes 7077892
  323.9 11.8 %copy-start.142 = (bf16[2,384,1536]{2,1,0:T(8,128)(2,1)S(1)}, bf16[2,384,1536]{2,1,0:T(8,128)(2,1)}, u32[]{:S(2)}) copy-start(bf16[2,384,1536]{2,1,0:T(8,128)(2,1)} %param.27) | copy-start | bytes 7077892
  339.4 31.8 %all-to-all-start.5 = ((bf16[8,184,384]{2,1,0:T(8,128)(2,1)}), bf16[8,184,384]{2,1,0:T(8,128)(2,1)S(1)}, u32[]{:S(2)}, u32[]{:S(2)}) async-start(bf16[8,184,384]{2,1,0:T(8,128)(2,1)} %convolution_convert_fusion.3), calls=%async_computation.5 | async-start | bytes 2260992 | tf_op jit(solution)/shard_map/all_to_all | solution.py:289
  352.9 23.7 %copy-start.52 = (f32[24,12,49]{2,1,0:T(8,128)S(1)}, f32[24,12,49]{2,1,0:T(8,128)}, u32[]{:S(2)}) copy-start(f32[24,12,49]{2,1,0:T(8,128)} %copy-done.51) | copy-start | bytes 169348
  352.9 23.7 %copy-start.66 = (f32[24,12,49]{2,1,0:T(8,128)S(1)}, f32[24,12,49]{2,1,0:T(8,128)}, u32[]{:S(2)}) copy-start(f32[24,12,49]{2,1,0:T(8,128)} %copy-done.65) | copy-start | bytes 169348
  371.2 31.6 %all-to-all-start.3 = ((bf16[8,184,384]{2,1,0:T(8,128)(2,1)}), bf16[8,184,384]{2,1,0:T(8,128)(2,1)}, u32[]{:S(2)}, u32[]{:S(2)}) async-start(bf16[8,184,384]{2,1,0:T(8,128)(2,1)} %convolution_convert_fusion.4), calls=%async_computation.3 | async-start | bytes 2260992 | tf_op jit(solution)/shard_map/all_to_all | solution.py:89
  376.5 7.1 slice-start.12
  427.2 7.4 copy-start.43
  427.2 15.3 %slice-start.6 = ((s8[7077888]{0:T(1024)(128)(4,1)}), s8[2883584]{0:T(1024)(128)(4,1)S(1)}, s32[]{:S(2)}) async-start(s8[7077888]{0:T(1024)(128)(4,1)} %bitcast.363), calls=%async_computation.17 | async-start | bytes 5767168
  434.6 7.9 slice-start.7
  434.6 7.9 copy-start.13
  434.6 15.1 %slice-start.2 = ((s8[8257536]{0:T(1024)(128)(4,1)}), s8[4194304]{0:T(1024)(128)(4,1)S(1)}, s32[]{:S(2)}) async-start(s8[8257536]{0:T(1024)(128)(4,1)} %bitcast.352), calls=%async_computation.13 | async-start | bytes 8388608
  442.5 7.2 slice-start.3
  528.9 9.4 copy-start.119
  532.6 7.2 copy-start.30
  532.6 7.4 copy-start.40
  532.6 7.7 copy-start.36
  532.6 31.9 %all-to-all-start.6 = ((bf16[8,184,384]{2,1,0:T(8,128)(2,1)}), bf16[8,184,384]{2,1,0:T(8,128)(2,1)}, u32[]{:S(2)}, u32[]{:S(2)}) async-start(bf16[8,184,384]{2,1,0:T(8,128)(2,1)} %bitcast.387), calls=%async_computation.6 | async-start | bytes 2260992 | tf_op jit(solution)/shard_map/all_to_all | solution.py:266
  543.8 20.7 %copy-start.138 = (bf16[2,1536,384]{2,1,0:T(8,128)(2,1)S(1)}, bf16[2,1536,384]{2,1,0:T(8,128)(2,1)}, u32[]{:S(2)}) copy-start(bf16[2,1536,384]{2,1,0:T(8,128)(2,1)} %param.30) | copy-start | bytes 7077892
  564.5 12.8 %copy-start.141 = (bf16[2,384,1536]{2,1,0:T(8,128)(2,1)S(1)}, bf16[2,384,1536]{2,1,0:T(8,128)(2,1)}, u32[]{:S(2)}) copy-start(bf16[2,384,1536]{2,1,0:T(8,128)(2,1)} %param.29) | copy-start | bytes 7077892
  564.5 12.8 %copy-start.143 = (bf16[2,384,1536]{2,1,0:T(8,128)(2,1)S(1)}, bf16[2,384,1536]{2,1,0:T(8,128)(2,1)}, u32[]{:S(2)}) copy-start(bf16[2,384,1536]{2,1,0:T(8,128)(2,1)} %param.27) | copy-start | bytes 7077892
  577.3 9.3 copy-start.124
  581.0 6.8 copy-start.41
  581.0 7.9 copy-start.125
  581.0 32.0 %all-to-all-start.7 = ((bf16[8,184,384]{2,1,0:T(8,128)(2,1)}), bf16[8,184,384]{2,1,0:T(8,128)(2,1)S(1)}, u32[]{:S(2)}, u32[]{:S(2)}) async-start(bf16[8,184,384]{2,1,0:T(8,128)(2,1)} %convolution_convert_fusion.2), calls=%async_computation.7 | async-start | bytes 2260992 | tf_op jit(solution)/shard_map/all_to_all | solution.py:289
  586.2 111.8 %all-reduce.18.cloned.1.call-start = ((), (), s32[]{:S(2)}) async-start(), calls=%async_computation.10 | async-start | bytes 9437184 | tf_op jit(solution)/shard_map/psum | solution.py:380
  587.8 9.3 slice-start.10
  590.0 7.1 slice-start.11
  602.2 10.9 %copy-start.88 = (s32[2048]{0:T(1024)S(1)}, s32[2048]{0:T(1024)}, u32[]{:S(2)}) copy-start(s32[2048]{0:T(1024)} %copy-done.87) | copy-start | bytes 24580
  628.5 10.9 %copy-start.11 = (bf16[24,49,384]{1,2,0:T(8,128)(2,1)}, bf16[24,49,384]{1,2,0:T(8,128)(2,1)S(1)}, u32[]{:S(2)}) copy-start(bf16[24,49,384]{1,2,0:T(8,128)(2,1)S(1)} %copy.219) | copy-start | bytes 2709508
  702.5 13.5 %slice-start.4 = ((s8[7077888]{0:T(1024)(128)(4,1)}), s8[2883584]{0:T(1024)(128)(4,1)S(1)}, s32[]{:S(2)}) async-start(s8[7077888]{0:T(1024)(128)(4,1)} %bitcast.357), calls=%async_computation.15 | async-start | bytes 5767168
  706.8 175.7 %all-reduce.16.cloned.1.call-start = ((), (), s32[]{:S(2)}) async-start(), calls=%async_computation.9 | async-start | bytes 9437184 | tf_op jit(solution)/shard_map/psum | solution.py:407
  707.6 323.5 %all-reduce.14.cloned.1.call-start = ((), (), s32[]{:S(2)}) async-start(), calls=%async_computation.8 | async-start | bytes 9437184 | tf_op jit(solution)/shard_map/psum | solution.py:393
  707.7 8.3 slice-start.5
  734.5 19.3 %copy-start.33 = (f32[1176,384]{1,0:T(8,128)S(1)}, f32[1176,384]{1,0:T(8,128)}, u32[]{:S(2)}) copy-start(f32[1176,384]{1,0:T(8,128)} %get-tuple-element.114) | copy-start | bytes 5419012
  802.8 48.1 %copy-start.94 = (f32[6,196]{1,0:T(8,128)S(1)}, f32[6,196]{1,0:T(8,128)}, u32[]{:S(2)}) copy-start(f32[6,196]{1,0:T(8,128)} %copy-done.93) | copy-start | bytes 14116
  (107 other events, 302.1 us)
Sparse Core Ops, SparseCore 0:
  602.3 95.6 all-reduce.17
  711.3 171.1 all-reduce.15
  888.9 142.1 all-reduce.13
where the time goes:
time: 1050 us; the launch traced here: 1040 us
  waiting for transfers between devices  354 us (34%)
  local copies, waits for them, and re-layouts  249 us (24%)
  matrix products  193 us (18%)
  other arithmetic  143 us (14%)
  starting transfers between devices  44.1 us (4%)
  blocking collectives  43.6 us (4%)
  between operations  16.4 us (2%)
    psum x1, waiting for transfers between devices, body(): lax.psum((local_gain_one, local_shift_one, local_attend, local_table, loc...  141 us
    convert_element_type x8, local copies, waits for them, and re-layouts, body(): grad_joined = jnp.stack([grad_queries, grad_keys, grad_values], axis=2).r...  94.2 us
    psum x1, waiting for transfers between devices, body(): lax.psum(local_up.astype(jnp.bfloat16), 'dp').astype(jnp.float32)  58.6 us
    all_to_all x2, waiting for transfers between devices, body(): lax.all_to_all(outgoing, 'expert', split_axis=0, concat_axis=0, tiled=True)  44.1 us
    psum x1, blocking collectives, body(): lax.psum((local_gain_one, local_shift_one, local_attend, local_table, loc...  43.6 us
    convert_element_type x2, other arithmetic, expert_apply(): hidden = jax.nn.gelu(inner_act, approximate=False).astype(jnp.bfloat16)  42.8 us
    unnamed x321, local copies, waits for them, and re-layouts  35.5 us
    all_to_all x2, waiting for transfers between devices, expert_apply(): lax.all_to_all(part_out, 'expert', split_axis=0, concat_axis=0, tiled=True)  33.4 us
  transfers between devices with their start and end apart: 11, of which 10 were waited for; matrix products, arithmetic and copies ran while one was open for 21% of the time, Pallas kernels for 0%

commit v1 on v0

v1 whole, which is shorter than its diff:
```python
from functools import partial

import jax
import jax.numpy as jnp
import numpy as np
from jax import lax
from jax.experimental import pallas as pl
from jax.experimental.pallas import tpu as pltpu
from jax.sharding import PartitionSpec as P

D = 384
HEADS = 12
HD = 32
FF = 1536
EXPERTS = 8
WIN = 7
SIDE = 14
SHIFT = 3
LAYERS = 2
HW = 196
CAP = 184
OFFSETS = 169
SLOTS = EXPERTS * CAP

WINDOWS = (SIDE // WIN) * (SIDE // WIN)
LENGTH = WIN * WIN
LPAD = 64
WROWS = WINDOWS * LPAD
TPAD = 256
LANES = 128
GROUP = LANES // HD
GROUPS = HEADS // GROUP
GW = GROUP * LPAD
FCHUNK = 384

F32 = jnp.float32
BF16 = jnp.bfloat16
eps_norm = 1e-05
mask_fill = -100.0
pad_fill = -1e30
score_scale = HD ** (-0.5)
VMEM_BYTES = 56 * 1024 * 1024

NN = (((1,), (0,)), ((), ()))
NT = (((1,), (1,)), ((), ()))
TN = (((0,), (0,)), ((), ()))


def mm(a, b, dims=NN):
    return lax.dot_general(a, b, dims, preferred_element_type=F32)


def window_tokens(offset):
    rows = np.full((WINDOWS, LPAD), -1, np.int64)
    per_side = SIDE // WIN
    for w in range(WINDOWS):
        for i in range(LENGTH):
            r = (w // per_side) * WIN + i // WIN
            c = (w % per_side) * WIN + i % WIN
            rows[w, i] = ((r + offset) % SIDE) * SIDE + (c + offset) % SIDE
    return rows.reshape(-1)


def permutation(offset):
    rows = window_tokens(offset)
    return (rows[:, None] == np.arange(HW)[None, :]).astype(np.float32)


def score_mask(offset):
    coords = np.arange(SIDE)
    bands = (coords >= SIDE - WIN).astype(int) + (coords >= SIDE - offset).astype(int)
    labels = bands[:, None] * 3 + bands[None, :]
    per_side = SIDE // WIN
    out = np.zeros((WINDOWS, LPAD, LPAD), np.float32)
    for w in range(WINDOWS):
        r0, c0 = (w // per_side) * WIN, (w % per_side) * WIN
        flat = labels[r0 : r0 + WIN, c0 : c0 + WIN].reshape(-1)
        out[w, :LENGTH, :LENGTH] = np.where(flat[:, None] == flat[None, :], 0.0, mask_fill)
        out[w, LENGTH:, :] = pad_fill
    return np.tile(out, (1, 1, GROUP))


def offset_table():
    i = np.arange(LENGTH)
    r, c = i // WIN, i % WIN
    index = np.full((LPAD, LPAD), -1, np.int64)
    index[:LENGTH, :LENGTH] = (
        (r[None, :] - r[:, None] + WIN - 1) * (2 * WIN - 1) + c[None, :] - c[:, None] + WIN - 1
    )
    return index.reshape(-1)


def norm_parts(x):
    centred = x - jnp.mean(x, axis=-1, keepdims=True)
    inverse = lax.rsqrt(jnp.mean(centred * centred, axis=-1, keepdims=True) + eps_norm)
    return centred * inverse, inverse


def norm_back(grad, unit, inverse, gain):
    scaled = grad * gain
    return inverse * (
        scaled
        - jnp.mean(scaled, axis=-1, keepdims=True)
        - unit * jnp.mean(scaled * unit, axis=-1, keepdims=True)
    )


def one_hot(cond):
    return jnp.where(cond, 1.0, 0.0).astype(BF16)


def head_masks():
    lane = lax.broadcasted_iota(jnp.int32, (1, LANES), 1) // HD
    return [jnp.where(lane == h, 1.0, 0.0) for h in range(GROUP)]


def spread_heads(block, masks):
    return jnp.concatenate([block * m.astype(BF16) for m in masks], axis=0)


def fold_heads(tall, masks):
    total = tall[0:LPAD] * masks[0]
    for h in range(1, GROUP):
        total = total + tall[h * LPAD : (h + 1) * LPAD] * masks[h]
    return total


def as_column(row, count):
    wide = jnp.broadcast_to(row.astype(F32), (8, TPAD))
    return wide.T[:count, 0:1].astype(jnp.int32)


def pick_rows(target_row, parts):
    column = as_column(target_row, HW)
    place = one_hot(lax.broadcasted_iota(jnp.int32, (HW, SLOTS), 1) == column)
    total = mm(place, parts[0])
    for k in range(1, parts.shape[0]):
        total = total + mm(place, parts[k])
    return total


def send_rows(out_ref, target_all, rows):
    step = SLOTS // 4
    for c in range(4):
        slot = lax.broadcasted_iota(jnp.int32, (step, rows.shape[0]), 0) + c * step
        out_ref[c * step : (c + 1) * step] = mm(one_hot(slot == target_all), rows).astype(BF16)


def gelu_parts(u):
    x = jnp.abs(u) * (0.5**0.5)
    t = 1.0 / (1.0 + 0.3275911 * x)
    bell = jnp.exp(-0.5 * u * u)
    poly = t * (
        0.254829592
        + t * (-0.284496736 + t * (1.421413741 + t * (-1.453152027 + t * 1.061405429)))
    )
    tail = 0.5 * poly * bell
    cdf = jnp.where(u >= 0.0, 1.0 - tail, tail)
    return u * cdf, cdf + u * bell * 0.3989422804014327


def routing_kernel(routes_ref, target_ref):
    before = one_hot(
        lax.broadcasted_iota(jnp.int32, (TPAD, TPAD), 0)
        <= lax.broadcasted_iota(jnp.int32, (TPAD, TPAD), 1)
    )
    expert = lax.broadcasted_iota(jnp.int32, (16, TPAD), 0)
    for depth in range(LAYERS):
        carry = jnp.zeros((16, 1), F32)
        for i in range(routes_ref.shape[1]):
            row = routes_ref[depth, i : i + 1, :]
            chosen = jnp.where(expert == row, 1.0, 0.0)
            counts = mm(chosen.astype(BF16), before) + carry
            carry = counts[:, TPAD - 1 : TPAD]
            slot = jnp.sum(chosen * counts, axis=0, keepdims=True).astype(jnp.int32) - 1
            kept = (slot >= 0) & (slot < CAP)
            target_ref[depth, i : i + 1, :] = jnp.where(kept, row * CAP + slot, -1)


def run_routing(routes):
    return pl.pallas_call(
        routing_kernel,
        out_shape=jax.ShapeDtypeStruct(routes.shape, jnp.int32),
        name="routing",
    )(routes)


def transposed_scores(qkv, w, g, bias_ref, mask_ref, masks):
    rows = slice(w * LPAD, (w + 1) * LPAD)
    q = qkv[rows, g * LANES : (g + 1) * LANES]
    k = qkv[rows, D + g * LANES : D + (g + 1) * LANES]
    v = qkv[rows, 2 * D + g * LANES : 2 * D + (g + 1) * LANES]
    q_wide = spread_heads(q, masks)
    scores = (
        mm(k, q_wide, NT) * score_scale
        + bias_ref[:, g * GW : (g + 1) * GW]
        + mask_ref[w]
    )
    raised = jnp.exp(scores - jnp.max(scores, axis=0, keepdims=True))
    return q_wide, k, v, raised * (1.0 / jnp.sum(raised, axis=0, keepdims=True))


def forward_kernel(depth, images, *refs):
    last = depth == LAYERS - 1
    refs = list(refs)
    take = lambda: refs.pop(0)
    x_ref = take()
    if depth:
        back_ref, gate_in_ref, target_in_ref = take(), take(), take()
    if last:
        cot_ref = take()
    (route_ref, target_ref, g1_ref, s1_ref, g2_ref, s2_ref, attend_ref, out_w_ref) = refs[:8]
    (router_ref, bias_ref, mask_ref, perm_ref, perm_back_ref) = refs[8:13]
    refs = refs[13:]
    (qkv_ref, a_ref, mixed_ref, mid_ref, n_ref, probs_ref, gate_ref, buf_ref) = refs[:8]
    refs = refs[8:]
    if depth:
        x_out_ref, picked_ref = take(), take()
    if last:
        dy_buf_ref = take()
    rows_ref = take()
    if last:
        dy_rows_ref = take()

    step = pl.program_id(0)

    @pl.when(step == 0)
    def _():
        rows_ref[...] = jnp.zeros_like(rows_ref)
        if last:
            dy_rows_ref[...] = jnp.zeros_like(dy_rows_ref)

    x = x_ref[0].astype(F32)
    if depth:
        picked = pick_rows(target_in_ref[0], back_ref)
        picked_ref[0] = picked.astype(picked_ref.dtype)
        x = x + gate_in_ref[0][:, 0:1] * picked
        x_out_ref[0] = x
    unit, _ = norm_parts(x)
    normed = (unit * g1_ref[depth : depth + 1] + s1_ref[depth : depth + 1]).astype(BF16)
    a = mm(perm_ref[...], normed).astype(BF16)
    a_ref[0] = a
    qkv_ref[0] = mm(a, attend_ref[0]).astype(BF16)
    masks = head_masks()
    for w in range(WINDOWS):
        for g in range(GROUPS):
            _, _, v, probs = transposed_scores(qkv_ref.at[0], w, g, bias_ref, mask_ref, masks)
            mixed = fold_heads(mm(probs.astype(BF16), v, TN), masks)
            mixed_ref[0, w * LPAD : (w + 1) * LPAD, g * LANES : (g + 1) * LANES] = mixed.astype(
                BF16
            )
    mixed = mm(perm_back_ref[...], mixed_ref[0]).astype(BF16)
    mid = x + mm(mixed, out_w_ref[0])
    mid_ref[0] = mid
    unit, _ = norm_parts(mid)
    n = (unit * g2_ref[depth : depth + 1] + s2_ref[depth : depth + 1]).astype(BF16)
    n_ref[0] = n
    lane = lax.broadcasted_iota(jnp.int32, (HW, LANES), 1)
    logits = jnp.where(lane < EXPERTS, mm(n, router_ref[0]), pad_fill)
    raised = jnp.exp(logits - jnp.max(logits, axis=-1, keepdims=True))
    router = raised / jnp.sum(raised, axis=-1, keepdims=True)
    probs_ref[0] = router
    chosen = lane == as_column(route_ref[0], HW)
    gate = jnp.sum(jnp.where(chosen, router, 0.0), axis=-1, keepdims=True)
    gate_ref[0] = jnp.broadcast_to(gate, (HW, LANES))
    rows_ref[pl.ds(step, 1), 0:HW, :] = n[None]
    if last:
        dy_rows_ref[pl.ds(step, 1), 0:HW, :] = (gate * cot_ref[0].astype(F32)).astype(BF16)[None]

    @pl.when(step == images - 1)
    def _():
        target_all = target_ref[...]
        send_rows(buf_ref, target_all, rows_ref[...].reshape(images * TPAD, D))
        if last:
            send_rows(dy_buf_ref, target_all, dy_rows_ref[...].reshape(images * TPAD, D))


def whole(shape):
    return pl.BlockSpec(shape, lambda i: (0,) * len(shape))


def by_image(shape):
    return pl.BlockSpec((1,) + shape[1:], lambda i: (i,) + (0,) * (len(shape) - 1))


def layer_of(shape, depth):
    return pl.BlockSpec((1,) + shape[1:], lambda i: (depth,) + (0,) * (len(shape) - 1))


def run_forward(depth, x, earlier, cotangent, route_rows, target_rows, target_all, shared):
    images = x.shape[0]
    last = depth == LAYERS - 1
    args, specs = [x], [by_image(x.shape)]
    if depth:
        back, gate_in, target_in, picked_type = earlier
        args += [back, gate_in, target_in]
        specs += [whole(back.shape), by_image(gate_in.shape), by_image(target_in.shape)]
    if last:
        args.append(cotangent)
        specs.append(by_image(cotangent.shape))
    args += [route_rows, target_all]
    specs += [by_image(route_rows.shape), whole(target_all.shape)]
    for name in ("first_gain", "first_shift", "second_gain", "second_shift"):
        args.append(shared[name])
        specs.append(whole(shared[name].shape))
    for name in ("attend_weight", "output_weight", "router"):
        args.append(shared[name])
        specs.append(layer_of(shared[name].shape, depth))
    for name in ("bias", "mask", "perm", "perm_back"):
        args.append(shared[name][depth])
        specs.append(whole(shared[name][depth].shape))
    outs = [
        ((images, WROWS, 3 * D), BF16),
        ((images, WROWS, D), BF16),
        ((images, WROWS, D), BF16),
        ((images, HW, D), F32),
        ((images, HW, D), BF16),
        ((images, HW, LANES), F32),
        ((images, HW, LANES), F32),
    ]
    out_specs = [by_image(s) for s, _ in outs]
    outs.append(((SLOTS, D), BF16))
    out_specs.append(whole((SLOTS, D)))
    if depth:
        outs += [((images, HW, D), F32), ((images, HW, D), picked_type)]
        out_specs += [by_image((images, HW, D))] * 2
    if last:
        outs.append(((SLOTS, D), BF16))
        out_specs.append(whole((SLOTS, D)))
    scratch = [pltpu.VMEM((images, TPAD, D), BF16)] * (2 if last else 1)
    return pl.pallas_call(
        partial(forward_kernel, depth, images),
        grid=(images,),
        in_specs=specs,
        out_specs=out_specs,
        out_shape=[jax.ShapeDtypeStruct(s, t) for s, t in outs],
        scratch_shapes=scratch,
        compiler_params=pltpu.CompilerParams(vmem_limit_bytes=VMEM_BYTES),
        name="forward_%d" % depth,
    )(*args)


def expert_forward_kernel(n_ref, up_ref, down_ref, y_ref, hidden_ref, slope_ref):
    u = mm(n_ref[...], up_ref[...])
    value, slope = gelu_parts(u)
    hidden = value.astype(BF16)
    hidden_ref[...] = hidden
    slope_ref[...] = slope.astype(BF16)
    y_ref[...] = mm(hidden, down_ref[...]).astype(BF16)


def run_expert_forward(arrived, up, down):
    rows, width = arrived.shape[0], up.shape[1]
    block = CAP * 2
    row_spec = pl.BlockSpec((block, D), lambda i: (i, 0))
    wide_spec = pl.BlockSpec((block, width), lambda i: (i, 0))
    return pl.pallas_call(
        expert_forward_kernel,
        grid=(rows // block,),
        in_specs=[row_spec, whole(up.shape), whole(down.shape)],
        out_specs=[row_spec, wide_spec, wide_spec],
        out_shape=[
            jax.ShapeDtypeStruct((rows, D), BF16),
            jax.ShapeDtypeStruct((rows, width), BF16),
            jax.ShapeDtypeStruct((rows, width), BF16),
        ],
        compiler_params=pltpu.CompilerParams(vmem_limit_bytes=VMEM_BYTES),
        name="expert_forward",
    )(arrived, up, down)


def expert_inner_kernel(dy_ref, slope_ref, up_ref, down_ref, dn_ref, du_ref):
    dh = mm(dy_ref[...], down_ref[...], NT)
    du = (dh * slope_ref[...].astype(F32)).astype(BF16)
    du_ref[...] = du
    dn_ref[...] = mm(du, up_ref[...], NT).astype(BF16)


def run_expert_inner(dy, slope, up, down):
    rows, width = dy.shape[0], up.shape[1]
    block = CAP * 2
    row_spec = pl.BlockSpec((block, D), lambda i: (i, 0))
    wide_spec = pl.BlockSpec((block, width), lambda i: (i, 0))
    return pl.pallas_call(
        expert_inner_kernel,
        grid=(rows // block,),
        in_specs=[row_spec, wide_spec, whole(up.shape), whole(down.shape)],
        out_specs=[row_spec, wide_spec],
        out_shape=[
            jax.ShapeDtypeStruct((rows, D), BF16),
            jax.ShapeDtypeStruct((rows, width), BF16),
        ],
        compiler_params=pltpu.CompilerParams(vmem_limit_bytes=VMEM_BYTES),
        name="expert_inner",
    )(dy, slope, up, down)


def expert_weights_kernel(n_ref, dy_ref, hidden_ref, du_ref, out_ref):
    out_ref[0:D] = mm(n_ref[...], du_ref[...], TN).astype(BF16)
    out_ref[D : 2 * D] = mm(hidden_ref[...], dy_ref[...], TN).astype(BF16)


def run_expert_weights(arrived, dy, hidden, du):
    rows, width = hidden.shape
    wide_spec = pl.BlockSpec((rows, FCHUNK), lambda i: (0, i))
    return pl.pallas_call(
        expert_weights_kernel,
        grid=(width // FCHUNK,),
        in_specs=[whole(arrived.shape), whole(dy.shape), wide_spec, wide_spec],
        out_specs=pl.BlockSpec((2 * D, FCHUNK), lambda i: (0, i)),
        out_shape=jax.ShapeDtypeStruct((2 * D, width), BF16),
        compiler_params=pltpu.CompilerParams(vmem_limit_bytes=VMEM_BYTES),
        name="expert_weights",
    )(arrived, dy, hidden, du)


def backward_kernel(depth, images, *refs):
    last = depth == LAYERS - 1
    refs = list(refs)
    take = lambda: refs.pop(0)
    g_ref, dn_ref = take(), take()
    if last:
        y_ref, before_gate_ref, before_target_ref = take(), take(), take()
    else:
        picked_ref = take()
    (x_ref, qkv_ref, a_ref, mixed_ref, mid_ref, n_ref, probs_ref, gate_ref) = refs[:8]
    (route_ref, target_ref, g1_ref, g2_ref, attend_ref, out_w_ref) = refs[8:14]
    (router_ref, bias_ref, mask_ref, perm_ref, perm_back_ref) = refs[14:19]
    refs = refs[19:]
    g_out_ref, mats_ref, vecs_ref, table_ref = take(), take(), take(), take()
    if last:
        result_ref, dy_buf_ref = take(), take()
    attend_acc, out_acc, dqkv_ref = take(), take(), take()
    if last:
        dy_rows_ref = take()

    step = pl.program_id(0)

    @pl.when(step == 0)
    def _():
        attend_acc[...] = jnp.zeros_like(attend_acc)
        out_acc[...] = jnp.zeros_like(out_acc)
        vecs_ref[...] = jnp.zeros_like(vecs_ref)
        table_ref[...] = jnp.zeros_like(table_ref)
        if last:
            dy_rows_ref[...] = jnp.zeros_like(dy_rows_ref)

    grad = g_ref[0].astype(F32)
    mid = mid_ref[0]
    gate = gate_ref[0][:, 0:1]
    if last:
        picked = pick_rows(target_ref[0], y_ref)
        result_ref[0] = (mid + gate * picked).astype(BF16)
    else:
        picked = picked_ref[0].astype(F32)
    gate_grad = jnp.sum(grad * picked, axis=-1, keepdims=True)
    lane = lax.broadcasted_iota(jnp.int32, (HW, LANES), 1)
    chosen = jnp.where(lane == as_column(route_ref[0], HW), 1.0, 0.0)
    logit_grad = ((gate * gate_grad) * (chosen - probs_ref[0])).astype(BF16)
    router_grad = mm(logit_grad, n_ref[0], TN)
    grad_n = pick_rows(target_ref[0], dn_ref) + mm(logit_grad, router_ref[0], NT)
    unit, inverse = norm_parts(mid)
    vecs_ref[2:3] += jnp.sum(grad_n * unit, axis=0, keepdims=True)
    vecs_ref[3:4] += jnp.sum(grad_n, axis=0, keepdims=True)
    vecs_ref[8:16] += router_grad[0:8]
    grad_mid = grad + norm_back(grad_n, unit, inverse, g2_ref[depth : depth + 1])
    dz = mm(perm_ref[...], grad_mid.astype(BF16)).astype(BF16)
    out_acc[...] += mm(mixed_ref[0], dz, TN)
    dmixed_all = mm(dz, out_w_ref[0], NT).astype(BF16)
    masks = head_masks()
    for w in range(WINDOWS):
        rows = slice(w * LPAD, (w + 1) * LPAD)
        for g in range(GROUPS):
            cols = slice(g * LANES, (g + 1) * LANES)
            q_wide, k, v, probs = transposed_scores(
                qkv_ref.at[0], w, g, bias_ref, mask_ref, masks
            )
            dm_wide = spread_heads(dmixed_all[rows, cols], masks)
            dprobs = mm(v, dm_wide, NT)
            dv = mm(probs.astype(BF16), dm_wide)
            row_dot = jnp.sum(probs * dprobs, axis=0, keepdims=True)
            dscores = (probs * (dprobs - row_dot)).astype(BF16)
            table_ref[:, g * GW : (g + 1) * GW] += dscores.astype(F32)
            dk = mm(dscores, q_wide) * score_scale
            dq = fold_heads(mm(dscores, k, TN), masks) * score_scale
            dqkv_ref[rows, cols] = dq.astype(BF16)
            dqkv_ref[rows, D + g * LANES : D + (g + 1) * LANES] = dk.astype(BF16)
            dqkv_ref[rows, 2 * D + g * LANES : 2 * D + (g + 1) * LANES] = dv.astype(BF16)
    dqkv = dqkv_ref[...]
    attend_acc[...] += mm(a_ref[0], dqkv, TN)
    dqkv_tokens = mm(perm_back_ref[...], dqkv).astype(BF16)
    grad_normed = mm(dqkv_tokens, attend_ref[0], NT)
    unit, inverse = norm_parts(x_ref[0].astype(F32))
    vecs_ref[0:1] += jnp.sum(grad_normed * unit, axis=0, keepdims=True)
    vecs_ref[1:2] += jnp.sum(grad_normed, axis=0, keepdims=True)
    grad_x = grad_mid + norm_back(grad_normed, unit, inverse, g1_ref[depth : depth + 1])
    g_out_ref[0] = grad_x.astype(g_out_ref.dtype)
    if last:
        dy = (before_gate_ref[0][:, 0:1] * grad_x).astype(BF16)
        dy_rows_ref[pl.ds(step, 1), 0:HW, :] = dy[None]

    @pl.when(step == images - 1)
    def _():
        mats_ref[:, 0 : 3 * D] = attend_acc[...].astype(BF16)
        mats_ref[:, 3 * D : 4 * D] = out_acc[...].astype(BF16)
        if last:
            send_rows(
                dy_buf_ref, before_target_ref[...], dy_rows_ref[...].reshape(images * TPAD, D)
            )


def run_backward(depth, grad, dn_back, extra, saved, route_rows, target_rows, shared):
    images = grad.shape[0]
    last = depth == LAYERS - 1
    args, specs = [grad, dn_back], [by_image(grad.shape), whole(dn_back.shape)]
    if last:
        y_back, before_gate, before_target = extra
        args += [y_back, before_gate, before_target]
        specs += [whole(y_back.shape), by_image(before_gate.shape), whole(before_target.shape)]
    else:
        args.append(extra)
        specs.append(by_image(extra.shape))
    for array in saved + [route_rows, target_rows]:
        args.append(array)
        specs.append(by_image(array.shape))
    for name in ("first_gain", "second_gain"):
        args.append(shared[name])
        specs.append(whole(shared[name].shape))
    for name in ("attend_weight", "output_weight", "router"):
        args.append(shared[name])
        specs.append(layer_of(shared[name].shape, depth))
    for name in ("bias", "mask", "perm", "perm_back"):
        args.append(shared[name][depth])
        specs.append(whole(shared[name][depth].shape))
    token_shape = (images, HW, D)
    outs = [
        (token_shape, F32 if last else BF16, by_image(token_shape)),
        ((D, 4 * D), BF16, whole((D, 4 * D))),
        ((16, D), F32, whole((16, D))),
        ((LPAD, GROUPS * GW), F32, whole((LPAD, GROUPS * GW))),
    ]
    if last:
        outs.append((token_shape, BF16, by_image(token_shape)))
        outs.append(((SLOTS, D), BF16, whole((SLOTS, D))))
    scratch = [
        pltpu.VMEM((D, 3 * D), F32),
        pltpu.VMEM((D, D), F32),
        pltpu.VMEM((WROWS, 3 * D), BF16),
    ]
    if last:
        scratch.append(pltpu.VMEM((images, TPAD, D), BF16))
    return pl.pallas_call(
        partial(backward_kernel, depth, images),
        grid=(images,),
        in_specs=specs,
        out_specs=[o[2] for o in outs],
        out_shape=[jax.ShapeDtypeStruct(o[0], o[1]) for o in outs],
        scratch_shapes=scratch,
        compiler_params=pltpu.CompilerParams(vmem_limit_bytes=VMEM_BYTES),
        name="backward_%d" % depth,
    )(*args)


def bits_of(axis, low, high):
    steps = []
    bit = low
    while bit < high:
        steps.append((axis, bit))
        bit *= 2
    return steps


def swap(x, step):
    axis, bit = step
    size = lax.axis_size(axis)
    return lax.ppermute(x, axis, [(i, i ^ bit) for i in range(size)])


def bit_at(step):
    axis, bit = step
    return (lax.axis_index(axis) // bit) % 2


def halved(rows, steps, least):
    count = 0
    while count < len(steps) and rows % 2 == 0 and rows // 2 >= least:
        rows //= 2
        count += 1
    return count


def sum_over(x, steps, least=24):
    count = halved(x.shape[0], steps, least)
    x = sum_all(scatter_sum(x, steps[:count]), steps[count:])
    return gather_all(x, steps[:count])


def scatter_sum(x, steps):
    for step in steps:
        half = x.shape[0] // 2
        mine = bit_at(step)
        keep = lax.dynamic_slice_in_dim(x, mine * half, half, 0)
        away = lax.dynamic_slice_in_dim(x, (1 - mine) * half, half, 0)
        x = (keep.astype(F32) + swap(away, step).astype(F32)).astype(x.dtype)
    return x


def gather_all(x, steps, dim=0):
    for step in reversed(steps):
        other = swap(x, step)
        mine = bit_at(step)
        first = jnp.where(mine == 0, x, other)
        second = jnp.where(mine == 0, other, x)
        x = jnp.concatenate([first, second], axis=dim)
    return x


def sum_all(x, steps):
    for step in steps:
        x = (x.astype(F32) + swap(x, step).astype(F32)).astype(x.dtype)
    return x


def exchange(buffers, slices):
    groups = lax.axis_size("expert")
    out = lax.all_to_all(
        buffers.reshape(groups, CAP, D), "expert", split_axis=0, concat_axis=0, tiled=True
    )
    return out.reshape(groups * CAP, D)


def to_experts(buffers, slices):
    if slices > 1:
        buffers = jnp.repeat(buffers.reshape(EXPERTS, CAP, D), slices, axis=0)
    return exchange(buffers, slices)


def from_experts(rows, slices):
    back = exchange(rows, slices)
    return back.reshape(EXPERTS, slices, CAP, D).transpose(1, 0, 2, 3).reshape(slices, SLOTS, D)


def unpack_down(packed):
    width = packed.shape[1]
    return jnp.concatenate(
        [packed[:, j * D : (j + 1) * D] for j in range(width // D)], axis=0
    )


def body(
    block_input,
    routes,
    first_gain,
    first_shift,
    attend_weight,
    bias_table,
    output_weight,
    second_gain,
    second_shift,
    router_weight,
    core_up,
    core_down,
    residual_up,
    residual_down,
    cotangent,
):
    groups = lax.axis_size("expert")
    slices = groups // EXPERTS
    group_part = lax.axis_index("expert") % slices
    images = block_input.shape[0]
    width = residual_up.shape[2]

    routes_rows = jnp.pad(
        routes.reshape(LAYERS, images, HW), ((0, 0), (0, 0), (0, TPAD - HW)), constant_values=-1
    )
    targets = run_routing(routes_rows)

    table_index = jnp.asarray(offset_table(), jnp.int32)
    picker = (jnp.arange(OFFSETS, dtype=jnp.int32)[:, None] == table_index[None, :]).astype(F32)
    flat_table = bias_table.transpose(0, 2, 1).reshape(LAYERS * HEADS, OFFSETS)
    bias = jnp.dot(flat_table, picker, precision=lax.Precision.HIGHEST)
    bias = (
        bias.reshape(LAYERS, HEADS, LPAD, LPAD)
        .transpose(0, 2, 1, 3)
        .reshape(LAYERS, LPAD, HEADS * LPAD)
    )
    offsets = [SHIFT * (depth % 2) for depth in range(LAYERS)]
    shared = {
        "first_gain": first_gain,
        "first_shift": first_shift,
        "second_gain": second_gain,
        "second_shift": second_shift,
        "attend_weight": attend_weight,
        "output_weight": output_weight,
        "router": jnp.pad(router_weight, ((0, 0), (0, 0), (0, LANES - EXPERTS))),
        "bias": [bias[depth] for depth in range(LAYERS)],
        "mask": [jnp.asarray(score_mask(o)) for o in offsets],
        "perm": [jnp.asarray(permutation(o), BF16) for o in offsets],
        "perm_back": [jnp.asarray(permutation(o).T, BF16) for o in offsets],
    }
    route_rows = [routes_rows[d].reshape(images, 1, TPAD) for d in range(LAYERS)]
    target_rows = [targets[d].reshape(images, 1, TPAD) for d in range(LAYERS)]
    target_all = [targets[d].reshape(1, images * TPAD) for d in range(LAYERS)]
    ups, downs = [], []
    for d in range(LAYERS):
        up_core = lax.dynamic_slice_in_dim(core_up[d], group_part * width, width, 1)
        down_core = lax.dynamic_slice_in_dim(core_down[d], group_part * width, width, 0)
        ups.append((up_core.astype(F32) + residual_up[d].astype(F32)).astype(BF16))
        downs.append((down_core.astype(F32) + residual_down[d].astype(F32)).astype(BF16))

    picked_type = BF16 if slices == 1 else F32
    saved, inner, gates, xs, picks = [], [], [], [block_input], []
    x, earlier = block_input, None
    dy_arrived = None
    for d in range(LAYERS):
        outs = run_forward(
            d, x, earlier, cotangent, route_rows[d], target_rows[d], target_all[d], shared
        )
        qkv, a, mixed, mid, n, probs, gate, buffers = outs[:8]
        if d:
            xs.append(outs[8])
            picks.append(outs[9])
        arrived = to_experts(buffers, slices)
        if d == LAYERS - 1:
            dy_arrived = to_experts(outs[10], slices)
        y, hidden, slope = run_expert_forward(arrived, ups[d], downs[d])
        back = from_experts(y, slices)
        earlier = (back, gate, target_rows[d], picked_type)
        x = mid
        gates.append(gate)
        saved.append([xs[d], qkv, a, mixed, mid, n, probs, gate])
        inner.append((arrived, hidden, slope))

    grad = cotangent
    mats, vecs, tables, experts = [None] * 2, [None] * 2, [None] * 2, [None] * 2
    block_output = None
    for d in reversed(range(LAYERS)):
        arrived, hidden, slope = inner[d]
        dn, du = run_expert_inner(dy_arrived, slope, ups[d], downs[d])
        dn_back = from_experts(dn, slices)
        experts[d] = run_expert_weights(arrived, dy_arrived, hidden, du)
        if d == LAYERS - 1:
            extra = (earlier[0], gates[d - 1], target_all[d - 1])
        else:
            extra = picks[d]
        outs = run_backward(
            d, grad, dn_back, extra, saved[d], route_rows[d], target_rows[d], shared
        )
        grad, mats[d], vecs[d], tables[d] = outs[:4]
        if d == LAYERS - 1:
            block_output = outs[4]
            dy_arrived = to_experts(outs[5], slices)
    input_grad = grad

    dp_steps = bits_of("dp", 1, lax.axis_size("dp"))
    slice_steps = bits_of("expert", 1, slices)
    sum_steps = bits_of("expert", slices, groups)
    all_steps = dp_steps + slice_steps + sum_steps
    residual, core, full = [], [], []
    for d in reversed(range(LAYERS)):
        part = scatter_sum(experts[d], dp_steps)
        residual.insert(0, gather_all(part, dp_steps))
        total = sum_over(part, sum_steps)
        total = gather_all(total, dp_steps)
        core.insert(0, gather_all(total, slice_steps, dim=1))
        full.insert(0, sum_over(mats[d], all_steps))
    table_grad = jnp.stack(tables).reshape(LAYERS, LPAD, HEADS, LPAD).transpose(0, 2, 1, 3)
    table_grad = jnp.dot(
        table_grad.reshape(LAYERS * HEADS, LPAD * LPAD), picker.T, precision=lax.Precision.HIGHEST
    )
    small = jnp.concatenate(
        [
            jnp.stack(vecs).reshape(LAYERS * 16, D),
            jnp.pad(table_grad, ((0, 0), (0, D - OFFSETS))),
        ],
        axis=0,
    )
    small = sum_all(small, all_steps)
    vec = small[: LAYERS * 16].reshape(LAYERS, 16, D)
    table = small[LAYERS * 16 :, :OFFSETS].reshape(LAYERS, HEADS, OFFSETS).transpose(0, 2, 1)
    full = jnp.stack(full).astype(F32)
    residual_up_grad = jnp.stack([r[:D] for r in residual]).astype(F32)
    residual_down_grad = jnp.stack([unpack_down(r[D:]) for r in residual]).astype(F32)
    core_up_grad = jnp.stack([c[:D] for c in core]).astype(F32)
    core_down_grad = jnp.stack([unpack_down(c[D:]) for c in core]).astype(F32)
    return (
        block_output,
        input_grad,
        vec[:, 0],
        vec[:, 1],
        full[:, :, : 3 * D],
        table,
        full[:, :, 3 * D :],
        vec[:, 2],
        vec[:, 3],
        vec[:, 8:16].transpose(0, 2, 1),
        core_up_grad,
        core_down_grad,
        residual_up_grad,
        residual_down_grad,
    )


def solution(mesh):
    placed = (
        P(("dp", "expert"), None, None),
        P(None, ("dp", "expert"), None, None),
        P(),
        P(),
        P(),
        P(),
        P(),
        P(),
        P(),
        P(),
        P(),
        P(),
        P(None, None, "expert"),
        P(None, "expert", None),
        P(("dp", "expert"), None, None),
    )
    return jax.shard_map(
        body,
        mesh=mesh,
        in_specs=placed,
        out_specs=(
            P(("dp", "expert"), None, None),
            P(("dp", "expert"), None, None),
            P(),
            P(),
            P(),
            P(),
            P(),
            P(),
            P(),
            P(),
            P(),
            P(),
            P(None, None, "expert"),
            P(None, "expert", None),
        ),
        check_vma=False,
    )
```

time: 1050 us -> 634 us (0.60)
  local copies, waits for them, and re-layouts: 249 us -> 36.5 us
  Pallas kernels: 0 us -> 209 us
  matrix products: 193 us -> 3.21 us
  waiting for transfers between devices: 354 us -> 198 us
  other arithmetic: 143 us -> 42.4 us
  starting transfers between devices: 44.1 us -> 101 us
  between operations: 16.4 us -> 2.12 us
  blocking collectives: 43.6 us -> 31.6 us
    psum x3 -> x0, waiting for transfers between devices: 228 us -> none  [the longest x1 141 us: body(): lax.psum((local_gain_one, local_shift_one, local_attend, local_table, loc...]
    pallas_call x0 -> x11, Pallas kernels: none -> 209 us  [the longest x2 83.4 us: run_backward(): pl.pallas_call(partial(backward_kernel, depth, images), grid=(images,), i...]
    dot_general x50 -> x2, matrix products: 193 us -> 3.21 us  [the longest x1 1.78 us: body(): bias = jnp.dot(flat_table, picker, precision=lax.Precision.HIGHEST)]
    convert_element_type x24 -> x0, local copies, waits for them, and re-layouts: 127 us -> none  [the longest x8 94.2 us: body(): grad_joined = jnp.stack([grad_queries, grad_keys, grad_values], axis=2).r...]
    ppermute x0 -> x47, waiting for transfers between devices: none -> 102 us  [swap(): return lax.ppermute(x, axis, [(i, i ^ bit) for i in range(size)])]
    ppermute x0 -> x47, starting transfers between devices: none -> 68.4 us  [swap(): return lax.ppermute(x, axis, [(i, i ^ bit) for i in range(size)])]
    convert_element_type x18 -> x27, other arithmetic: 74.5 us -> 22.3 us  [the longest x18 6.14 us: scatter_sum(): x = (keep.astype(F32) + swap(away, step).astype(F32)).astype(x.dtype)]
    psum x1 -> x0, blocking collectives: 43.6 us -> none  [body(): lax.psum((local_gain_one, local_shift_one, local_attend, local_table, loc...]
  transfers between devices with their start and end apart: 11 -> 54, of which waited for: 10 -> 30; matrix products, arithmetic and copies ran while one was open for 21% -> 9% of each run, Pallas kernels for 0% -> 18%
where the time goes in v1:
time: 634 us; the launch traced here: 625 us
  Pallas kernels  209 us (33%)
  waiting for transfers between devices  198 us (31%)
  starting transfers between devices  101 us (16%)
  other arithmetic  42.4 us (7%)
  local copies, waits for them, and re-layouts  36.5 us (6%)
  blocking collectives  31.6 us (5%)
    ppermute x47, waiting for transfers between devices, swap(): return lax.ppermute(x, axis, [(i, i ^ bit) for i in range(size)])  102 us
    all_to_all x7, waiting for transfers between devices, exchange(): lax.all_to_all(buffers.reshape(groups, CAP, D), 'expert', split_axis=0, c...  95.9 us
    pallas_call x2, Pallas kernels, run_backward(): pl.pallas_call(partial(backward_kernel, depth, images), grid=(images,), i...  83.4 us
    ppermute x47, starting transfers between devices, swap(): return lax.ppermute(x, axis, [(i, i ^ bit) for i in range(size)])  68.4 us
    pallas_call x2, Pallas kernels, run_forward(): pl.pallas_call(partial(forward_kernel, depth, images), grid=(images,), in...  61 us
    all_to_all x7, starting transfers between devices, exchange(): lax.all_to_all(buffers.reshape(groups, CAP, D), 'expert', split_axis=0, c...  33 us
    all_to_all x1, blocking collectives, exchange(): lax.all_to_all(buffers.reshape(groups, CAP, D), 'expert', split_axis=0, c...  31.6 us
    pallas_call x2, Pallas kernels, run_expert_forward(): pl.pallas_call(expert_forward_kernel, grid=(rows // block,), in_specs=[ro...  27.6 us
  transfers between devices with their start and end apart: 54, of which 30 were waited for; matrix products, arithmetic and copies ran while one was open for 9% of the time, Pallas kernels for 18%

profile of v1, /device:TPU:1, one launch (start us, length us, event | category | flops | bytes accessed | tf_op | source)
XLA Modules:
  0.0 624.8 jit_solution(6290206665139819881)
XLA Ops:
  2.6 1.9 routing.1
  7.5 1.8 convolution_bitcast_fusion
  12.5 27.0 %forward_0.1 = (bf16[6,256,1152]{2,1,0:T(8,128)(2,1)}, bf16[6,256,384]{2,1,0:T(8,128)(2,1)}, bf16[6,256,384]{2,1,0:T(8,128)(2,1)}, f32[6,196,384]{2,1,0:T(8,128)...) custom-call(bf16[6,196,384]{2,1,0:T(8,128)(2,1)} %refs_3_.3, ...), custom_call_target="tpu_custom_call" | custom-call | tf_op jit(solution)/shard_map/forward_0/pallas_call | solution.py:331
  39.5 6.4 %all-to-all-start = ((bf16[8,184,384]{2,1,0:T(8,128)(2,1)}), bf16[8,184,384]{2,1,0:T(8,128)(2,1)S(1)}, u32[]{:S(2)}, u32[]{:S(2)}) async-start(bf16[8,184,384]{2,1,0:T(8,128)(2,1)} %bitcast.99), calls=%async_computation | async-start | bytes 2260992 | tf_op jit(solution)/shard_map/all_to_all | solution.py:626
  45.9 3.8 fusion.6
  49.7 2.0 fusion.5
  51.7 20.8 %all-to-all-done = bf16[8,184,384]{2,1,0:T(8,128)(2,1)S(1)} async-done(((bf16[8,184,384]{2,1,0:T(8,128)(2,1)}), bf16[8,184,384]{2,1,0:T(8,128)(2,1)S(1)}, u32[]{:S(2)}, u32[]{:S(2)}) %all-to-all-start) | async-done | bytes 1130528 | tf_op jit(solution)/shard_map/all_to_all | solution.py:626
  73.6 13.8 %expert_forward.2 = (bf16[1472,384]{1,0:T(8,128)(2,1)}, bf16[1472,1536]{1,0:T(8,128)(2,1)}, bf16[1472,1536]{1,0:T(8,128)(2,1)}) custom-call(bf16[1472,384]{1,0:T(8,128)(2,1)} %bitcast.86, bf16[384,1536]{1,0:T(8,128)(2,1)} %get-tuple-element.109.up_ref, bf16[1536,384]{1,0:T(8,128)(2,1)} %get-tuple-element.107.down_ref), custom_call_target="tpu_custom_call" | custom-call | tf_op jit(solution)/shard_map/expert_forward/pallas_call | solution.py:357
  87.4 5.3 all-to-all-start.1
  94.7 24.8 %all-to-all-done.1 = bf16[8,184,384]{2,1,0:T(8,128)(2,1)S(1)} async-done(((bf16[8,184,384]{2,1,0:T(8,128)(2,1)}), bf16[8,184,384]{2,1,0:T(8,128)(2,1)S(1)}, u32[]{:S(2)}, u32[]{:S(2)}) %all-to-all-start.1) | async-done | bytes 1130528 | tf_op jit(solution)/shard_map/all_to_all | solution.py:626
  120.5 34.0 %forward_1.1 = (bf16[6,256,1152]{2,1,0:T(8,128)(2,1)}, bf16[6,256,384]{2,1,0:T(8,128)(2,1)}, bf16[6,256,384]{2,1,0:T(8,128)(2,1)}, f32[6,196,384]{2,1,0:T(8,128)...) custom-call(f32[6,196,384]{2,1,0:T(8,128)} %get-tuple-element.53.ref, ...), custom_call_target="tpu_custom_call" | custom-call | tf_op jit(solution)/shard_map/forward_1/pallas_call | solution.py:331
  154.5 31.6 %all_to_all.40 = bf16[8,184,384]{2,1,0:T(8,128)(2,1)} all-to-all(bf16[8,184,384]{2,1,0:T(8,128)(2,1)} %bitcast.101), channel_id=1, replica_groups=mesh['dp'=4,'expert'=8] {'expert'}, dimensions={0} | all-to-all | bytes 2260992 | tf_op jit(solution)/shard_map/all_to_all | solution.py:626
  186.1 3.7 all-to-all-start.2
  189.8 13.8 %expert_forward.3 = (bf16[1472,384]{1,0:T(8,128)(2,1)}, bf16[1472,1536]{1,0:T(8,128)(2,1)}, bf16[1472,1536]{1,0:T(8,128)(2,1)}) custom-call(bf16[1472,384]{1,0:T(8,128)(2,1)} %bitcast.90, bf16[384,1536]{1,0:T(8,128)(2,1)} %get-tuple-element.108.up_ref, bf16[1536,384]{1,0:T(8,128)(2,1)} %get-tuple-element.106.down_ref), custom_call_target="tpu_custom_call" | custom-call | tf_op jit(solution)/shard_map/expert_forward/pallas_call | solution.py:357
  203.6 12.1 %all-to-all-done.2 = bf16[8,184,384]{2,1,0:T(8,128)(2,1)S(1)} async-done(((bf16[8,184,384]{2,1,0:T(8,128)(2,1)}), bf16[8,184,384]{2,1,0:T(8,128)(2,1)S(1)}, u32[]{:S(2)}, u32[]{:S(2)}) %all-to-all-start.2) | async-done | bytes 1130528 | tf_op jit(solution)/shard_map/all_to_all | solution.py:626
  216.7 8.4 %expert_inner.2 = (bf16[1472,384]{1,0:T(8,128)(2,1)}, bf16[1472,1536]{1,0:T(8,128)(2,1)}) custom-call(bf16[1472,384]{1,0:T(8,128)(2,1)} %bitcast.92, bf16[1472,1536]{1,0:T(8,128)(2,1)} %get-tuple-element.59.slope_ref, bf16[384,1536]{1,0:T(8,128)(2,1)} %get-tuple-element.108.up_ref, bf16[1536,384]{1,0:T(8,128)(2,1)} %get-tuple-element.106.down_ref), custom_call_target="tpu_custom_call" | custom-call | tf_op jit(solution)/shard_map/expert_inner/pallas_call | solution.py:384
  225.1 9.3 %expert_weights.3 = bf16[768,1536]{1,0:T(8,128)(2,1)} custom-call(bf16[1472,384]{1,0:T(8,128)(2,1)} %bitcast.91, bf16[1472,384]{1,0:T(8,128)(2,1)} %bitcast.93, bf16[1472,1536]{1,0:T(8,128)(2,1)} %get-tuple-element.90.hidden_ref, bf16[1472,1536]{1,0:T(8,128)(2,1)} %get-tuple-element.91.du_ref), custom_call_target="tpu_custom_call" | custom-call | tf_op jit(solution)/shard_map/expert_weights/pallas_call | solution.py:406
  236.0 2.9 collective-permute-start.33
  238.8 4.4 all-to-all-start.4
  246.1 24.8 %all-to-all-done.4 = bf16[8,184,384]{2,1,0:T(8,128)(2,1)} async-done(((bf16[8,184,384]{2,1,0:T(8,128)(2,1)}), bf16[8,184,384]{2,1,0:T(8,128)(2,1)}, u32[]{:S(2)}, u32[]{:S(2)}) %all-to-all-start.4) | async-done | bytes 1130528 | tf_op jit(solution)/shard_map/all_to_all | solution.py:626
  270.9 3.7 all-to-all-start.5
  276.3 15.9 %collective-permute-done.35 = bf16[96,1536]{1,0:T(8,128)(2,1)S(1)} collective-permute-done((bf16[96,1536]{1,0:T(8,128)(2,1)S(1)}, bf16[96,1536]{1,0:T(8,128)(2,1)S(1)}, u32[]{:S(2)}, u32[]{:S(2)}) %collective-permute-start.35) | collective-permute-done | bytes 294944 | tf_op jit(solution)/shard_map/ppermute | solution.py:576
  294.2 7.4 %all-to-all-done.5 = bf16[8,184,384]{2,1,0:T(8,128)(2,1)S(1)} async-done(((bf16[8,184,384]{2,1,0:T(8,128)(2,1)}), bf16[8,184,384]{2,1,0:T(8,128)(2,1)S(1)}, u32[]{:S(2)}, u32[]{:S(2)}) %all-to-all-start.5) | async-done | bytes 1130528 | tf_op jit(solution)/shard_map/all_to_all | solution.py:626
  302.6 45.1 %backward_1.1 = (f32[6,196,384]{2,1,0:T(8,128)}, bf16[384,1536]{1,0:T(8,128)(2,1)}, f32[16,384]{1,0:T(8,128)}, f32[64,768]{1,0:T(8,128)}, bf16[6,196,384]{2,1,0:T(8,128)(2,1)}, /*index=5*/bf16[1472,384]{1,0:T(8,128)(2,1)}) custom-call(bf16[6,196,384]{2,1,0:T(8,128)(2,1)} %refs_0_.3, bf16[1,1472,384]{2,1,0:T(8,128)(2,1)} %bitcast.22.refs_1_, ...), custom_call_target="tpu_custom_call" | custom-call | tf_op jit(solution)/shard_map/backward_1/pallas_call | solution.py:552
  347.7 4.8 all-to-all-start.6
  353.6 2.4 collective-permute-start.37
  359.2 23.3 %collective-permute-done.37 = bf16[24,1536]{1,0:T(8,128)(2,1)S(1)} collective-permute-done((bf16[24,1536]{1,0:T(8,128)(2,1)S(1)}, bf16[24,1536]{1,0:T(8,128)(2,1)S(1)}, u32[]{:S(2)}, u32[]{:S(2)}) %collective-permute-start.37) | collective-permute-done | bytes 73760 | tf_op jit(solution)/shard_map/ppermute | solution.py:576
  383.8 1.7 collective-permute-start.46
  387.0 1.7 collective-permute-done.38
  388.7 5.7 collective-permute-done.15
  395.8 1.8 collective-permute-start.39
  397.6 1.6 collective-permute-done.16
  399.3 1.9 collective-permute-start.17
  401.2 1.7 collective-permute-done.17
  402.9 2.3 collective-permute-start.18
  408.7 2.3 collective-permute-done.40
  413.5 2.5 collective-permute-done.20
  417.4 4.4 collective-permute-done.41
  423.1 9.5 %collective-permute-start.42 = (bf16[384,1536]{1,0:T(8,128)(2,1)}, bf16[384,1536]{1,0:T(8,128)(2,1)}, u32[]{:S(2)}, u32[]{:S(2)}) collective-permute-start(bf16[384,1536]{1,0:T(8,128)(2,1)} %pad_maximum_fusion.1), channel_id=1, source_target_pairs={{0,8},{8,0},{16,24},{24,16},{1,9},{9,1},{17,25},{25,17},{2,10},{10... | collective-permute-start | bytes 3538952 | tf_op jit(solution)/shard_map/ppermute | solution.py:576
  436.6 8.4 %expert_inner.3 = (bf16[1472,384]{1,0:T(8,128)(2,1)}, bf16[1472,1536]{1,0:T(8,128)(2,1)}) custom-call(bf16[1472,384]{1,0:T(8,128)(2,1)} %bitcast.88, bf16[1472,1536]{1,0:T(8,128)(2,1)} %get-tuple-element.73.slope_ref, bf16[384,1536]{1,0:T(8,128)(2,1)} %get-tuple-element.109.up_ref, bf16[1536,384]{1,0:T(8,128)(2,1)} %get-tuple-element.107.down_ref), custom_call_target="tpu_custom_call" | custom-call | tf_op jit(solution)/shard_map/expert_inner/pallas_call | solution.py:384
  444.9 9.3 %expert_weights.2 = bf16[768,1536]{1,0:T(8,128)(2,1)} custom-call(bf16[1472,384]{1,0:T(8,128)(2,1)} %bitcast.87, bf16[1472,384]{1,0:T(8,128)(2,1)} %bitcast.89, bf16[1472,1536]{1,0:T(8,128)(2,1)} %get-tuple-element.88.hidden_ref, bf16[1472,1536]{1,0:T(8,128)(2,1)} %get-tuple-element.89.du_ref), custom_call_target="tpu_custom_call" | custom-call | tf_op jit(solution)/shard_map/expert_weights/pallas_call | solution.py:406
  454.3 2.4 constant_dynamic-slice_fusion.9
  458.1 4.6 all-to-all-start.7
  468.5 2.7 broadcast_select_fusion.2
  472.2 9.8 %collective-permute-done.24 = bf16[192,1536]{1,0:T(8,128)(2,1)S(1)} collective-permute-done((bf16[192,1536]{1,0:T(8,128)(2,1)S(1)}, bf16[192,1536]{1,0:T(8,128)(2,1)S(1)}, u32[]{:S(2)}, u32[]{:S(2)}) %collective-permute-start.24) | collective-permute-done | bytes 589856 | tf_op jit(solution)/shard_map/ppermute | solution.py:576
  484.0 6.0 all-to-all-done.7
  490.0 38.2 %backward_0.1 = (bf16[6,196,384]{2,1,0:T(8,128)(2,1)}, bf16[384,1536]{1,0:T(8,128)(2,1)}, f32[16,384]{1,0:T(8,128)}, f32[64,768]{1,0:T(8,128)}) custom-call(f32[6,196,384]{2,1,0:T(8,128)} %get-tuple-element.71.refs_0_, bf16[1,1472,384]{2,1,0:T(8,128)(2,1)} %bitcast.29.refs_1_, bf16[6,196,384]{2,1,0:T(8,128)(2,1)} %get-tuple-element.75.refs_2_, ...), custom_call_target="tpu_custom_call" | custom-call | tf_op jit(solution)/shard_map/backward_0/pallas_call | solution.py:552
  528.2 1.8 stack.66
  544.5 1.8 collective-permute-start.5
  551.7 2.9 collective-permute-done.43
  562.7 5.9 collective-permute-done.6
  570.4 2.4 collective-permute-done.7
  573.9 2.2 collective-permute-done.8
  577.5 3.4 collective-permute-done.9
  582.6 2.7 collective-permute-done.10
  586.6 3.0 collective-permute-done.11
  590.3 5.1 collective-permute-done.31
  595.8 9.7 %collective-permute-start.32 = (bf16[384,1536]{1,0:T(8,128)(2,1)S(1)}, bf16[384,1536]{1,0:T(8,128)(2,1)S(1)}, u32[]{:S(2)}, u32[]{:S(2)}) collective-permute-start(bf16[384,1536]{1,0:T(8,128)(2,1)S(1)} %pad_maximum_fusion), channel_id=1, source_target_pairs={{0,8},{8,0},{16,24},{24,16},{1,9},{9,1},{17,25},{25,17},{2,10},{10... | collective-permute-start | bytes 3538952 | tf_op jit(solution)/shard_map/ppermute | solution.py:576
  605.5 1.7 broadcast_select_fusion.1
  608.7 2.5 maximum_convert_fusion.4
  611.2 2.5 maximum_convert_fusion.3
  614.3 2.0 slice.167
  619.3 2.5 maximum_convert_fusion.2
  621.8 2.5 maximum_convert_fusion.1
  (251 shorter events, 94.0 us)
Async XLA Ops:
  12.5 33.4 %copy-start.15 = (bf16[2,1536,384]{2,1,0:T(8,128)(2,1)S(1)}, bf16[2,1536,384]{2,1,0:T(8,128)(2,1)}, u32[]{:S(2)}) copy-start(bf16[2,1536,384]{2,1,0:T(8,128)(2,1)} %param.35) | copy-start | bytes 7077892
  39.5 33.0 %all-to-all-start = ((bf16[8,184,384]{2,1,0:T(8,128)(2,1)}), bf16[8,184,384]{2,1,0:T(8,128)(2,1)S(1)}, u32[]{:S(2)}, u32[]{:S(2)}) async-start(bf16[8,184,384]{2,1,0:T(8,128)(2,1)} %bitcast.99), calls=%async_computation | async-start | bytes 2260992 | tf_op jit(solution)/shard_map/all_to_all | solution.py:626
  87.4 6.5 %copy-start.19 = (f32[1,64,12,64]{3,2,1,0:T(8,128)S(1)}, f32[1,64,12,64]{3,2,1,0:T(8,128)}, u32[]{:S(2)}) copy-start(f32[1,64,12,64]{3,2,1,0:T(8,128)} %get-tuple-element.146) | copy-start | bytes 589828
  87.4 32.1 %all-to-all-start.1 = ((bf16[8,184,384]{2,1,0:T(8,128)(2,1)}), bf16[8,184,384]{2,1,0:T(8,128)(2,1)S(1)}, u32[]{:S(2)}, u32[]{:S(2)}) async-start(bf16[8,184,384]{2,1,0:T(8,128)(2,1)} %bitcast.100), calls=%async_computation.1 | async-start | bytes 2260992 | tf_op jit(solution)/shard_map/all_to_all | solution.py:626
  186.1 29.6 %all-to-all-start.2 = ((bf16[8,184,384]{2,1,0:T(8,128)(2,1)}), bf16[8,184,384]{2,1,0:T(8,128)(2,1)S(1)}, u32[]{:S(2)}, u32[]{:S(2)}) async-start(bf16[8,184,384]{2,1,0:T(8,128)(2,1)} %bitcast.15), calls=%async_computation.2 | async-start | bytes 2260992 | tf_op jit(solution)/shard_map/all_to_all | solution.py:626
  234.5 8.8 %copy-start.3 = (bf16[768,1536]{1,0:T(8,128)(2,1)S(1)}, bf16[768,1536]{1,0:T(8,128)(2,1)}, u32[]{:S(2)}) copy-start(bf16[768,1536]{1,0:T(8,128)(2,1)} %expert_weights.3) | copy-start | bytes 7077892
  236.0 7.3 %collective-permute-start.33 = (bf16[384,1536]{1,0:T(8,128)(2,1)S(1)}, bf16[384,1536]{1,0:T(8,128)(2,1)}, u32[]{:S(2)}, u32[]{:S(2)}) collective-permute-start(bf16[384,1536]{1,0:T(8,128)(2,1)S(1)} %constant_dynamic-slice_fusion.4), channel_id=1, source_target_pairs={{0,8},{8,0},{16,24},{24,16},{1,9},{9,1},{17,25},{25,17},{2,10},{10... | collective-permute-start | bytes 3538952 | tf_op jit(solution)/shard_map/ppermute | solution.py:576
  238.8 32.1 %all-to-all-start.4 = ((bf16[8,184,384]{2,1,0:T(8,128)(2,1)}), bf16[8,184,384]{2,1,0:T(8,128)(2,1)}, u32[]{:S(2)}, u32[]{:S(2)}) async-start(bf16[8,184,384]{2,1,0:T(8,128)(2,1)} %bitcast.98), calls=%async_computation.4 | async-start | bytes 2260992 | tf_op jit(solution)/shard_map/all_to_all | solution.py:626
  244.9 29.7 %collective-permute-start.34 = (bf16[192,1536]{1,0:T(8,128)(2,1)S(1)}, bf16[192,1536]{1,0:T(8,128)(2,1)S(1)}, u32[]{:S(2)}, u32[]{:S(2)}) collective-permute-start(bf16[192,1536]{1,0:T(8,128)(2,1)S(1)} %constant_dynamic-slice_fusion.3), channel_id=1, source_target_pairs={{0,16},{8,24},{16,0},{24,8},{1,17},{9,25},{17,1},{25,9},{2,18},{10... | collective-permute-start | bytes 1769480 | tf_op jit(solution)/shard_map/ppermute | solution.py:576
  270.9 30.7 %all-to-all-start.5 = ((bf16[8,184,384]{2,1,0:T(8,128)(2,1)}), bf16[8,184,384]{2,1,0:T(8,128)(2,1)S(1)}, u32[]{:S(2)}, u32[]{:S(2)}) async-start(bf16[8,184,384]{2,1,0:T(8,128)(2,1)} %bitcast.23), calls=%async_computation.5 | async-start | bytes 2260992 | tf_op jit(solution)/shard_map/all_to_all | solution.py:626
  274.8 17.4 %collective-permute-start.35 = (bf16[96,1536]{1,0:T(8,128)(2,1)S(1)}, bf16[96,1536]{1,0:T(8,128)(2,1)S(1)}, u32[]{:S(2)}, u32[]{:S(2)}) collective-permute-start(bf16[96,1536]{1,0:T(8,128)(2,1)S(1)} %constant_dynamic-slice_fusion.2), channel_id=1, source_target_pairs={{0,1},{1,0},{2,3},{3,2},{4,5},{5,4},{6,7},{7,6},{8,9},{9,8},{10,11... | collective-permute-start | bytes 884744 | tf_op jit(solution)/shard_map/ppermute | solution.py:576
  292.3 60.3 %collective-permute-start.36 = (bf16[48,1536]{1,0:T(8,128)(2,1)S(1)}, bf16[48,1536]{1,0:T(8,128)(2,1)}, u32[]{:S(2)}, u32[]{:S(2)}) collective-permute-start(bf16[48,1536]{1,0:T(8,128)(2,1)S(1)} %constant_dynamic-slice_fusion.1), channel_id=1, source_target_pairs={{0,2},{1,3},{2,0},{3,1},{4,6},{5,7},{6,4},{7,5},{8,10},{9,11},{10,... | collective-permute-start | bytes 442376 | tf_op jit(solution)/shard_map/ppermute | solution.py:576
  293.0 89.6 %collective-permute-start.45 = (bf16[192,1536]{1,0:T(8,128)(2,1)S(1)}, bf16[192,1536]{1,0:T(8,128)(2,1)}, u32[]{:S(2)}, u32[]{:S(2)}) collective-permute-start(bf16[192,1536]{1,0:T(8,128)(2,1)S(1)} %add_convert_fusion.6), channel_id=1, source_target_pairs={{0,16},{8,24},{16,0},{24,8},{1,17},{9,25},{17,1},{25,9},{2,18},{10... | collective-permute-start | bytes 1769480 | tf_op jit(solution)/shard_map/ppermute | solution.py:576
  347.7 8.3 %copy-start.25 = (bf16[384,1536]{1,0:T(8,128)(2,1)S(1)}, bf16[384,1536]{1,0:T(8,128)(2,1)}, u32[]{:S(2)}) copy-start(bf16[384,1536]{1,0:T(8,128)(2,1)} %get-tuple-element.87) | copy-start | bytes 3538948
  347.7 87.8 %all-to-all-start.6 = ((bf16[8,184,384]{2,1,0:T(8,128)(2,1)}), bf16[8,184,384]{2,1,0:T(8,128)(2,1)S(1)}, u32[]{:S(2)}, u32[]{:S(2)}) async-start(bf16[8,184,384]{2,1,0:T(8,128)(2,1)} %bitcast.97), calls=%async_computation.6 | async-start | bytes 2260992 | tf_op jit(solution)/shard_map/all_to_all | solution.py:626
  353.6 28.9 %collective-permute-start.37 = (bf16[24,1536]{1,0:T(8,128)(2,1)S(1)}, bf16[24,1536]{1,0:T(8,128)(2,1)S(1)}, u32[]{:S(2)}, u32[]{:S(2)}) collective-permute-start(bf16[24,1536]{1,0:T(8,128)(2,1)S(1)} %constant_dynamic-slice_fusion), channel_id=1, source_target_pairs={{0,4},{1,5},{2,6},{3,7},{4,0},{5,1},{6,2},{7,3},{8,12},{9,13},{10,... | collective-permute-start | bytes 221192 | tf_op jit(solution)/shard_map/ppermute | solution.py:576
  357.8 27.8 %collective-permute-start.14 = (bf16[192,1536]{1,0:T(8,128)(2,1)}, bf16[192,1536]{1,0:T(8,128)(2,1)S(1)}, u32[]{:S(2)}, u32[]{:S(2)}) collective-permute-start(bf16[192,1536]{1,0:T(8,128)(2,1)} %constant_dynamic-slice_fusion.13), channel_id=1, source_target_pairs={{0,8},{8,0},{16,24},{24,16},{1,9},{9,1},{17,25},{25,17},{2,10},{10... | collective-permute-start | bytes 1769480 | tf_op jit(solution)/shard_map/ppermute | solution.py:576
  382.5 6.2 collective-permute-start.38
  383.8 48.7 %collective-permute-start.46 = (bf16[384,1536]{1,0:T(8,128)(2,1)S(1)}, bf16[384,1536]{1,0:T(8,128)(2,1)S(1)}, u32[]{:S(2)}, u32[]{:S(2)}) collective-permute-start(bf16[384,1536]{1,0:T(8,128)(2,1)S(1)} %pad_maximum_fusion.3), channel_id=1, source_target_pairs={{0,8},{8,0},{16,24},{24,16},{1,9},{9,1},{17,25},{25,17},{2,10},{10... | collective-permute-start | bytes 3538952 | tf_op jit(solution)/shard_map/ppermute | solution.py:576
  385.8 8.7 %collective-permute-start.15 = (bf16[96,1536]{1,0:T(8,128)(2,1)S(1)}, bf16[96,1536]{1,0:T(8,128)(2,1)S(1)}, u32[]{:S(2)}, u32[]{:S(2)}) collective-permute-start(bf16[96,1536]{1,0:T(8,128)(2,1)S(1)} %constant_dynamic-slice_fusion.12), channel_id=1, source_target_pairs={{0,16},{8,24},{16,0},{24,8},{1,17},{9,25},{17,1},{25,9},{2,18},{10... | collective-permute-start | bytes 884744 | tf_op jit(solution)/shard_map/ppermute | solution.py:576
  394.6 4.6 collective-permute-start.16
  395.8 5.4 collective-permute-start.39
  399.3 3.6 collective-permute-start.17
  402.9 4.2 collective-permute-start.18
  405.3 5.6 collective-permute-start.40
  407.1 3.9 collective-permute-start.19
  411.1 5.0 collective-permute-start.20
  412.3 9.5 %collective-permute-start.41 = (bf16[192,1536]{1,0:T(8,128)(2,1)S(1)}, bf16[192,1536]{1,0:T(8,128)(2,1)S(1)}, u32[]{:S(2)}, u32[]{:S(2)}) collective-permute-start(bf16[192,1536]{1,0:T(8,128)(2,1)S(1)} %pad_maximum_fusion.7), channel_id=1, source_target_pairs={{0,16},{8,24},{16,0},{24,8},{1,17},{9,25},{17,1},{25,9},{2,18},{10... | collective-permute-start | bytes 1769480 | tf_op jit(solution)/shard_map/ppermute | solution.py:576
  416.2 17.9 %collective-permute-start.21 = (bf16[96,1536]{1,0:T(8,128)(2,1)S(1)}, bf16[96,1536]{1,0:T(8,128)(2,1)S(1)}, u32[]{:S(2)}, u32[]{:S(2)}) collective-permute-start(bf16[96,1536]{1,0:T(8,128)(2,1)S(1)} %pad_maximum_fusion.9), channel_id=1, source_target_pairs={{0,16},{8,24},{16,0},{24,8},{1,17},{9,25},{17,1},{25,9},{2,18},{10... | collective-permute-start | bytes 884744 | tf_op jit(solution)/shard_map/ppermute | solution.py:576
  423.1 45.4 %collective-permute-start.42 = (bf16[384,1536]{1,0:T(8,128)(2,1)}, bf16[384,1536]{1,0:T(8,128)(2,1)}, u32[]{:S(2)}, u32[]{:S(2)}) collective-permute-start(bf16[384,1536]{1,0:T(8,128)(2,1)} %pad_maximum_fusion.1), channel_id=1, source_target_pairs={{0,8},{8,0},{16,24},{24,16},{1,9},{9,1},{17,25},{25,17},{2,10},{10... | collective-permute-start | bytes 3538952 | tf_op jit(solution)/shard_map/ppermute | solution.py:576
  435.2 27.5 %collective-permute-start.22 = (bf16[192,1536]{1,0:T(8,128)(2,1)}, bf16[192,1536]{1,0:T(8,128)(2,1)}, u32[]{:S(2)}, u32[]{:S(2)}) collective-permute-start(bf16[192,1536]{1,0:T(8,128)(2,1)} %pad_maximum_fusion.5), channel_id=1, source_target_pairs={{0,8},{8,0},{16,24},{24,16},{1,9},{9,1},{17,25},{25,17},{2,10},{10... | collective-permute-start | bytes 1769480 | tf_op jit(solution)/shard_map/ppermute | solution.py:576
  456.6 7.5 %collective-permute-start.23 = (bf16[384,1536]{1,0:T(8,128)(2,1)}, bf16[384,1536]{1,0:T(8,128)(2,1)}, u32[]{:S(2)}, u32[]{:S(2)}) collective-permute-start(bf16[384,1536]{1,0:T(8,128)(2,1)} %constant_dynamic-slice_fusion.9), channel_id=1, source_target_pairs={{0,8},{8,0},{16,24},{24,16},{1,9},{9,1},{17,25},{25,17},{2,10},{10... | collective-permute-start | bytes 3538952 | tf_op jit(solution)/shard_map/ppermute | solution.py:576
  458.1 31.9 %all-to-all-start.7 = ((bf16[8,184,384]{2,1,0:T(8,128)(2,1)}), bf16[8,184,384]{2,1,0:T(8,128)(2,1)}, u32[]{:S(2)}, u32[]{:S(2)}) async-start(bf16[8,184,384]{2,1,0:T(8,128)(2,1)} %bitcast.28), calls=%async_computation.7 | async-start | bytes 2260992 | tf_op jit(solution)/shard_map/all_to_all | solution.py:626
  467.3 14.7 %collective-permute-start.24 = (bf16[192,1536]{1,0:T(8,128)(2,1)S(1)}, bf16[192,1536]{1,0:T(8,128)(2,1)S(1)}, u32[]{:S(2)}, u32[]{:S(2)}) collective-permute-start(bf16[192,1536]{1,0:T(8,128)(2,1)S(1)} %constant_dynamic-slice_fusion.8), channel_id=1, source_target_pairs={{0,16},{8,24},{16,0},{24,8},{1,17},{9,25},{17,1},{25,9},{2,18},{10... | collective-permute-start | bytes 1769480 | tf_op jit(solution)/shard_map/ppermute | solution.py:576
  482.9 53.7 %collective-permute-start.25 = (bf16[96,1536]{1,0:T(8,128)(2,1)}, bf16[96,1536]{1,0:T(8,128)(2,1)}, u32[]{:S(2)}, u32[]{:S(2)}) collective-permute-start(bf16[96,1536]{1,0:T(8,128)(2,1)} %constant_dynamic-slice_fusion.7), channel_id=1, source_target_pairs={{0,1},{1,0},{2,3},{3,2},{4,5},{5,4},{6,7},{7,6},{8,9},{9,8},{10,11... | collective-permute-start | bytes 884744 | tf_op jit(solution)/shard_map/ppermute | solution.py:576
  490.0 40.1 %copy-start.18 = (f32[1,64,12,64]{3,2,1,0:T(8,128)S(1)}, f32[1,64,12,64]{3,2,1,0:T(8,128)}, u32[]{:S(2)}) copy-start(f32[1,64,12,64]{3,2,1,0:T(8,128)} %stack.67) | copy-start | bytes 589828
  533.8 5.2 copy-start.20
  533.8 5.2 copy-start.21
  533.8 5.2 copy-start.22
  533.8 5.2 copy-start.23
  535.3 2.5 collective-permute-start
  537.7 5.5 collective-permute-start.26
  537.8 4.1 collective-permute-start.1
  539.0 5.4 copy-start.24
  540.2 14.5 %collective-permute-start.43 = (bf16[192,1536]{1,0:T(8,128)(2,1)S(1)}, bf16[192,1536]{1,0:T(8,128)(2,1)S(1)}, u32[]{:S(2)}, u32[]{:S(2)}) collective-permute-start(bf16[192,1536]{1,0:T(8,128)(2,1)S(1)} %add_convert_fusion.7), channel_id=1, source_target_pairs={{0,16},{8,24},{16,0},{24,8},{1,17},{9,25},{17,1},{25,9},{2,18},{10... | collective-permute-start | bytes 1769480 | tf_op jit(solution)/shard_map/ppermute | solution.py:576
  541.9 4.4 collective-permute-start.2
  543.3 4.2 collective-permute-start.27
  544.5 14.8 %collective-permute-start.5 = (bf16[192,1536]{1,0:T(8,128)(2,1)S(1)}, bf16[192,1536]{1,0:T(8,128)(2,1)S(1)}, u32[]{:S(2)}, u32[]{:S(2)}) collective-permute-start(bf16[192,1536]{1,0:T(8,128)(2,1)S(1)} %constant_dynamic-slice_fusion.17), channel_id=1, source_target_pairs={{0,8},{8,0},{16,24},{24,16},{1,9},{9,1},{17,25},{25,17},{2,10},{10... | collective-permute-start | bytes 1769480 | tf_op jit(solution)/shard_map/ppermute | solution.py:576
  546.3 4.0 collective-permute-start.3
  547.5 9.6 %collective-permute-start.28 = (bf16[24,1536]{1,0:T(8,128)(2,1)S(1)}, bf16[24,1536]{1,0:T(8,128)(2,1)S(1)}, u32[]{:S(2)}, u32[]{:S(2)}) collective-permute-start(bf16[24,1536]{1,0:T(8,128)(2,1)S(1)} %add_convert_fusion.19), channel_id=1, source_target_pairs={{0,4},{1,5},{2,6},{3,7},{4,0},{5,1},{6,2},{7,3},{8,12},{9,13},{10,... | collective-permute-start | bytes 221192 | tf_op jit(solution)/shard_map/ppermute | solution.py:576
  550.3 8.9 %collective-permute-start.4 = (f32[56,384]{1,0:T(8,128)S(1)}, f32[56,384]{1,0:T(8,128)S(1)}, u32[]{:S(2)}, u32[]{:S(2)}) collective-permute-start(f32[56,384]{1,0:T(8,128)S(1)} %add.237), channel_id=1, source_target_pairs={{0,4},{1,5},{2,6},{3,7},{4,0},{5,1},{6,2},{7,3},{8,12},{9,13},{10,... | collective-permute-start | bytes 258056 | tf_op jit(solution)/shard_map/ppermute | solution.py:576
  555.8 49.7 %collective-permute-start.44 = (bf16[384,1536]{1,0:T(8,128)(2,1)}, bf16[384,1536]{1,0:T(8,128)(2,1)}, u32[]{:S(2)}, u32[]{:S(2)}) collective-permute-start(bf16[384,1536]{1,0:T(8,128)(2,1)} %pad_maximum_fusion.2), channel_id=1, source_target_pairs={{0,8},{8,0},{16,24},{24,16},{1,9},{9,1},{17,25},{25,17},{2,10},{10... | collective-permute-start | bytes 3538952 | tf_op jit(solution)/shard_map/ppermute | solution.py:576
  557.8 15.2 %collective-permute-start.29 = (bf16[48,1536]{1,0:T(8,128)(2,1)}, bf16[48,1536]{1,0:T(8,128)(2,1)}, u32[]{:S(2)}, u32[]{:S(2)}) collective-permute-start(bf16[48,1536]{1,0:T(8,128)(2,1)} %pad_maximum_fusion.14), channel_id=1, source_target_pairs={{0,2},{1,3},{2,0},{3,1},{4,6},{5,7},{6,4},{7,5},{8,10},{9,11},{10,... | collective-permute-start | bytes 442376 | tf_op jit(solution)/shard_map/ppermute | solution.py:576
  560.2 8.4 %collective-permute-start.6 = (bf16[96,1536]{1,0:T(8,128)(2,1)}, bf16[96,1536]{1,0:T(8,128)(2,1)S(1)}, u32[]{:S(2)}, u32[]{:S(2)}) collective-permute-start(bf16[96,1536]{1,0:T(8,128)(2,1)} %constant_dynamic-slice_fusion.16), channel_id=1, source_target_pairs={{0,16},{8,24},{16,0},{24,8},{1,17},{9,25},{17,1},{25,9},{2,18},{10... | collective-permute-start | bytes 884744 | tf_op jit(solution)/shard_map/ppermute | solution.py:576
  568.7 4.1 collective-permute-start.7
  572.8 3.3 collective-permute-start.8
  576.1 4.8 collective-permute-start.9
  576.9 5.6 collective-permute-start.30
  581.0 4.4 collective-permute-start.10
  585.3 4.2 collective-permute-start.11
  586.1 9.3 %collective-permute-start.31 = (bf16[192,1536]{1,0:T(8,128)(2,1)S(1)}, bf16[192,1536]{1,0:T(8,128)(2,1)S(1)}, u32[]{:S(2)}, u32[]{:S(2)}) collective-permute-start(bf16[192,1536]{1,0:T(8,128)(2,1)S(1)} %pad_maximum_fusion.6), channel_id=1, source_target_pairs={{0,16},{8,24},{16,0},{24,8},{1,17},{9,25},{17,1},{25,9},{2,18},{10... | collective-permute-start | bytes 1769480 | tf_op jit(solution)/shard_map/ppermute | solution.py:576
  589.7 17.8 %collective-permute-start.12 = (bf16[96,1536]{1,0:T(8,128)(2,1)S(1)}, bf16[96,1536]{1,0:T(8,128)(2,1)S(1)}, u32[]{:S(2)}, u32[]{:S(2)}) collective-permute-start(bf16[96,1536]{1,0:T(8,128)(2,1)S(1)} %pad_maximum_fusion.8), channel_id=1, source_target_pairs={{0,16},{8,24},{16,0},{24,8},{1,17},{9,25},{17,1},{25,9},{2,18},{10... | collective-permute-start | bytes 884744 | tf_op jit(solution)/shard_map/ppermute | solution.py:576
  595.8 21.7 %collective-permute-start.32 = (bf16[384,1536]{1,0:T(8,128)(2,1)S(1)}, bf16[384,1536]{1,0:T(8,128)(2,1)S(1)}, u32[]{:S(2)}, u32[]{:S(2)}) collective-permute-start(bf16[384,1536]{1,0:T(8,128)(2,1)S(1)} %pad_maximum_fusion), channel_id=1, source_target_pairs={{0,8},{8,0},{16,24},{24,16},{1,9},{9,1},{17,25},{25,17},{2,10},{10... | collective-permute-start | bytes 3538952 | tf_op jit(solution)/shard_map/ppermute | solution.py:576
  607.6 6.1 collective-permute-start.13
  (20 other events, 46.3 us)

commit v2 on v1

v2 whole, which is shorter than its diff:
```python
from functools import partial

import jax
import jax.numpy as jnp
import numpy as np
from jax import lax
from jax.experimental import pallas as pl
from jax.experimental.pallas import tpu as pltpu
from jax.sharding import PartitionSpec as P

D = 384
HEADS = 12
HD = 32
FF = 1536
EXPERTS = 8
WIN = 7
SIDE = 14
SHIFT = 3
LAYERS = 2
HW = 196
CAP = 184
OFFSETS = 169
ROWS = 192
SLOTS = EXPERTS * ROWS

WINDOWS = (SIDE // WIN) * (SIDE // WIN)
LENGTH = WIN * WIN
LPAD = 64
WROWS = WINDOWS * LPAD
TPAD = 256
LANES = 128
GROUP = LANES // HD
GROUPS = HEADS // GROUP
GW = GROUP * LPAD
FCHUNK = 384
JOIN = 2
FTILE = 512
EXPERT_VMEM = 32 * 1024 * 1024
BLOCK = 48
PAIRS_AT_ONCE = 2
SEND_ORDER = (4, 5, 6, 7, 2, 3, 1)
PART = 4
STEP_IMAGES = 3

F32 = jnp.float32
BF16 = jnp.bfloat16
eps_norm = 1e-05
mask_fill = -100.0
pad_fill = -1e30
score_scale = HD ** (-0.5)
VMEM_BYTES = 56 * 1024 * 1024

NN = (((1,), (0,)), ((), ()))
NT = (((1,), (1,)), ((), ()))
TN = (((0,), (0,)), ((), ()))


def mm(a, b, dims=NN):
    return lax.dot_general(a, b, dims, preferred_element_type=F32)


def window_tokens(offset):
    rows = np.full((WINDOWS, LPAD), -1, np.int64)
    per_side = SIDE // WIN
    for w in range(WINDOWS):
        for i in range(LENGTH):
            r = (w // per_side) * WIN + i // WIN
            c = (w % per_side) * WIN + i % WIN
            rows[w, i] = ((r + offset) % SIDE) * SIDE + (c + offset) % SIDE
    return rows.reshape(-1)


def permutation(offset):
    rows = window_tokens(offset)
    return (rows[:, None] == np.arange(HW)[None, :]).astype(np.float32)


def score_mask(offset):
    coords = np.arange(SIDE)
    bands = (coords >= SIDE - WIN).astype(int) + (coords >= SIDE - offset).astype(int)
    labels = bands[:, None] * 3 + bands[None, :]
    per_side = SIDE // WIN
    out = np.zeros((WINDOWS, LPAD, LPAD), np.float32)
    for w in range(WINDOWS):
        r0, c0 = (w // per_side) * WIN, (w % per_side) * WIN
        flat = labels[r0 : r0 + WIN, c0 : c0 + WIN].reshape(-1)
        out[w, :LENGTH, :LENGTH] = np.where(flat[:, None] == flat[None, :], 0.0, mask_fill)
        out[w, LENGTH:, :] = pad_fill
    return np.tile(out, (1, 1, GROUP))


def offset_table():
    i = np.arange(LENGTH)
    r, c = i // WIN, i % WIN
    index = np.full((LPAD, LPAD), -1, np.int64)
    index[:LENGTH, :LENGTH] = (
        (r[None, :] - r[:, None] + WIN - 1) * (2 * WIN - 1) + c[None, :] - c[:, None] + WIN - 1
    )
    return index.reshape(-1)


def norm_parts(x):
    centred = x - jnp.mean(x, axis=-1, keepdims=True)
    inverse = lax.rsqrt(jnp.mean(centred * centred, axis=-1, keepdims=True) + eps_norm)
    return centred * inverse, inverse


def norm_back(grad, unit, inverse, gain):
    scaled = grad * gain
    return inverse * (
        scaled
        - jnp.mean(scaled, axis=-1, keepdims=True)
        - unit * jnp.mean(scaled * unit, axis=-1, keepdims=True)
    )


def one_hot(cond):
    return jnp.where(cond, 1.0, 0.0).astype(BF16)


def head_masks():
    lane = lax.broadcasted_iota(jnp.int32, (1, LANES), 1) // HD
    return [jnp.where(lane == h, 1.0, 0.0) for h in range(GROUP)]


def spread_heads(block, masks):
    return jnp.concatenate([block * m.astype(BF16) for m in masks], axis=0)


def fold_heads(tall, masks):
    total = tall[0:LPAD] * masks[0]
    for h in range(1, GROUP):
        total = total + tall[h * LPAD : (h + 1) * LPAD] * masks[h]
    return total


def as_column(row, count):
    wide = jnp.broadcast_to(row.astype(F32), (8, TPAD))
    return wide.T[:count, 0:1].astype(jnp.int32)


def pick_rows(target_row, rows_ref):
    column = as_column(target_row, HW)
    place = one_hot(lax.broadcasted_iota(jnp.int32, (HW, SLOTS), 1) == column)
    total = mm(place, rows_ref[0])
    for k in range(1, rows_ref.shape[0]):
        total = total + mm(place, rows_ref[k])
    return total


def join_chunks(rows_ref, chunks):
    parts = rows_ref.shape[0]
    for i, chunk in enumerate(chunks):
        rows_ref[i % parts, (i // parts) * ROWS : (i // parts + 1) * ROWS] = chunk[...]


def send_rows(out_refs, target_all, rows):
    step = SLOTS // 4
    for c in range(4):
        slot = lax.broadcasted_iota(jnp.int32, (step, rows.shape[0]), 0) + c * step
        block = mm(one_hot(slot == target_all), rows).astype(BF16)
        for group, refs in enumerate(out_refs):
            for k in range(step // ROWS):
                refs[c * (step // ROWS) + k][...] = block[
                    k * ROWS : (k + 1) * ROWS, group * D : (group + 1) * D
                ]


def gelu_parts(u):
    cdf = 0.5 + 0.5 * lax.erf(u * (0.5**0.5))
    bell = jnp.exp(-0.5 * u * u)
    return u * cdf, cdf + u * (bell * 0.3989422804014327)


def cost(microseconds):
    return pl.CostEstimate(
        flops=int(microseconds * 9e8), bytes_accessed=1000, transcendentals=0
    )


def routing_kernel(flip_ref, routes_ref, target_ref):
    before = one_hot(
        lax.broadcasted_iota(jnp.int32, (TPAD, TPAD), 0)
        <= lax.broadcasted_iota(jnp.int32, (TPAD, TPAD), 1)
    )
    expert = lax.broadcasted_iota(jnp.int32, (16, TPAD), 0)
    for depth in range(LAYERS):
        carry = jnp.zeros((16, 1), F32)
        for i in range(routes_ref.shape[1]):
            row = routes_ref[depth, i : i + 1, :]
            chosen = jnp.where(expert == row, 1.0, 0.0)
            counts = mm(chosen.astype(BF16), before) + carry
            carry = counts[:, TPAD - 1 : TPAD]
            slot = jnp.sum(chosen * counts, axis=0, keepdims=True).astype(jnp.int32) - 1
            kept = (slot >= 0) & (slot < CAP)
            target_ref[depth, i : i + 1, :] = jnp.where(
                kept, jnp.bitwise_xor(row, flip_ref[0]) * ROWS + slot, -1
            )


def run_routing(routes, flip):
    return pl.pallas_call(
        routing_kernel,
        in_specs=[
            pl.BlockSpec(memory_space=pltpu.SMEM),
            pl.BlockSpec(memory_space=pltpu.VMEM),
        ],
        out_shape=jax.ShapeDtypeStruct(routes.shape, jnp.int32),
        name="routing",
    )(flip, routes)


def group_cols(part, g):
    return slice(part * D + g * LANES, part * D + (g + 1) * LANES)


def softmax_down(scores):
    raised = jnp.exp(scores - jnp.max(scores, axis=0, keepdims=True))
    return raised * (1.0 / jnp.sum(raised, axis=0, keepdims=True))


def window_items(some):
    pairs = [(w, g) for w in range(WINDOWS) for g in range(GROUPS)]
    runs = []
    for first in range(0, len(pairs), PAIRS_AT_ONCE):
        runs.append([(w, g, b) for w, g in pairs[first : first + PAIRS_AT_ONCE] for b in some])
    return runs


def raw_scores(qkv_ref, items, masks):
    wide, scores = [], []
    for w, g, b in items:
        rows = slice(w * LPAD, (w + 1) * LPAD)
        wide.append(spread_heads(qkv_ref[b, rows, group_cols(0, g)], masks))
    for (w, g, b), q_wide in zip(items, wide):
        rows = slice(w * LPAD, (w + 1) * LPAD)
        scores.append(mm(qkv_ref[b, rows, group_cols(1, g)], q_wide, NT))
    return wide, scores


def to_probs(items, scores, bias_ref, mask_ref):
    probs = []
    for (w, g, b), score in zip(items, scores):
        probs.append(
            softmax_down(
                score * score_scale + bias_ref[:, g * GW : (g + 1) * GW] + mask_ref[w]
            )
        )
    return probs


def forward_kernel(depth, images, chunks, *refs):
    last = depth == LAYERS - 1
    refs = list(refs)
    take = lambda: refs.pop(0)
    x_ref = take()
    if depth:
        back = [take() for _ in range(chunks)]
        gate_in_ref, target_in_ref = take(), take()
    if last:
        cot_ref = take()
    (route_ref, target_ref, g1_ref, s1_ref, g2_ref, s2_ref, attend_ref, out_w_ref) = refs[:8]
    (router_ref, bias_ref, mask_ref, perm_ref, perm_back_ref) = refs[8:13]
    refs = refs[13:]
    (qkv_ref, a_ref, mixed_ref, mid_ref, n_ref, probs_ref, gate_ref) = refs[:7]
    refs = refs[7:]
    if depth:
        x_out_ref, picked_ref = take(), take()
    outgoing = [[take() for _ in range(EXPERTS)] for _ in range(2 if last else 1)]
    rows_ref = take()
    if depth:
        back_ref = take()

    step = pl.program_id(0)

    @pl.when(step == 0)
    def _():
        rows_ref[...] = jnp.zeros_like(rows_ref)
        if depth:
            join_chunks(back_ref, back)

    some = range(x_ref.shape[0])
    xs = []
    for b in some:
        x = x_ref[b].astype(F32)
        if depth:
            picked = pick_rows(target_in_ref[b], back_ref)
            picked_ref[b] = picked.astype(picked_ref.dtype)
            x = x + gate_in_ref[b][:, 0:1] * picked
            x_out_ref[b] = x
        xs.append(x)
    for b in some:
        unit, _ = norm_parts(xs[b])
        normed = (unit * g1_ref[depth : depth + 1] + s1_ref[depth : depth + 1]).astype(BF16)
        a_ref[b] = mm(perm_ref[...], normed).astype(BF16)
    qkv = mm(a_ref[...].reshape(len(some) * WROWS, D), attend_ref[0]).astype(BF16)
    qkv_ref[...] = qkv.reshape(len(some), WROWS, 3 * D)
    masks = head_masks()
    runs = window_items(some)
    ready = raw_scores(qkv_ref, runs[0], masks)
    for at, items in enumerate(runs):
        _, scores = ready
        if at + 1 < len(runs):
            ready = raw_scores(qkv_ref, runs[at + 1], masks)
        probs = to_probs(items, scores, bias_ref, mask_ref)
        tall = []
        for (w, g, b), p in zip(items, probs):
            rows = slice(w * LPAD, (w + 1) * LPAD)
            tall.append(mm(p.astype(BF16), qkv_ref[b, rows, group_cols(2, g)], TN))
        for (w, g, b), t in zip(items, tall):
            rows = slice(w * LPAD, (w + 1) * LPAD)
            mixed_ref[b, rows, group_cols(0, g)] = fold_heads(t, masks).astype(BF16)
    lane = lax.broadcasted_iota(jnp.int32, (HW, LANES), 1)
    for b in some:
        mixed = mm(perm_back_ref[...], mixed_ref[b]).astype(BF16)
        mid = xs[b] + mm(mixed, out_w_ref[0])
        mid_ref[b] = mid
        unit, _ = norm_parts(mid)
        n = (unit * g2_ref[depth : depth + 1] + s2_ref[depth : depth + 1]).astype(BF16)
        n_ref[b] = n
        logits = jnp.where(lane < EXPERTS, mm(n, router_ref[0]), pad_fill)
        raised = jnp.exp(logits - jnp.max(logits, axis=-1, keepdims=True))
        router = raised / jnp.sum(raised, axis=-1, keepdims=True)
        probs_ref[b] = router
        chosen = lane == as_column(route_ref[b], HW)
        gate = jnp.sum(jnp.where(chosen, router, 0.0), axis=-1, keepdims=True)
        gate_ref[b] = jnp.broadcast_to(gate, (HW, LANES))
        at = step * len(some) + b
        rows_ref[pl.ds(at, 1), 0:HW, 0:D] = n[None]
        if last:
            dy = (gate * cot_ref[b].astype(F32)).astype(BF16)
            rows_ref[pl.ds(at, 1), 0:HW, D : 2 * D] = dy[None]

    @pl.when(step == pl.num_programs(0) - 1)
    def _():
        rows = rows_ref[...].reshape(images * TPAD, rows_ref.shape[2])
        send_rows(outgoing, target_ref[...], rows)


def whole(shape):
    return pl.BlockSpec(shape, lambda i: (0,) * len(shape))


def images_of(images):
    return STEP_IMAGES if images % STEP_IMAGES == 0 else 1


def by_image(shape):
    return pl.BlockSpec(
        (images_of(shape[0]),) + shape[1:], lambda i: (i,) + (0,) * (len(shape) - 1)
    )


def layer_of(shape, depth):
    return pl.BlockSpec((1,) + shape[1:], lambda i: (depth,) + (0,) * (len(shape) - 1))


def run_forward(depth, x, earlier, cotangent, route_rows, target_rows, target_all, shared):
    images = x.shape[0]
    last = depth == LAYERS - 1
    args, specs = [x], [by_image(x.shape)]
    if depth:
        back, gate_in, target_in, picked_type = earlier
        args += list(back) + [gate_in, target_in]
        specs += [whole(chunk.shape) for chunk in back]
        specs += [by_image(gate_in.shape), by_image(target_in.shape)]
    if last:
        args.append(cotangent)
        specs.append(by_image(cotangent.shape))
    args += [route_rows, target_all]
    specs += [by_image(route_rows.shape), whole(target_all.shape)]
    for name in ("first_gain", "first_shift", "second_gain", "second_shift"):
        args.append(shared[name])
        specs.append(whole(shared[name].shape))
    for name in ("attend_weight", "output_weight", "router"):
        args.append(shared[name])
        specs.append(layer_of(shared[name].shape, depth))
    for name in ("bias", "mask", "perm", "perm_back"):
        args.append(shared[name][depth])
        specs.append(whole(shared[name][depth].shape))
    outs = [
        ((images, WROWS, 3 * D), BF16),
        ((images, WROWS, D), BF16),
        ((images, WROWS, D), BF16),
        ((images, HW, D), F32),
        ((images, HW, D), BF16),
        ((images, HW, LANES), F32),
        ((images, HW, LANES), F32),
    ]
    out_specs = [by_image(s) for s, _ in outs]
    if depth:
        outs += [((images, HW, D), F32), ((images, HW, D), picked_type)]
        out_specs += [by_image((images, HW, D))] * 2
    count = EXPERTS * (2 if last else 1)
    outs += [((ROWS, D), BF16)] * count
    out_specs += [whole((ROWS, D))] * count
    scratch = [pltpu.VMEM((images, TPAD, 2 * D if last else D), BF16)]
    if depth:
        scratch.append(pltpu.VMEM((len(back) // EXPERTS, SLOTS, D), BF16))
    results = pl.pallas_call(
        partial(forward_kernel, depth, images, len(back) if depth else 0),
        grid=(images // images_of(images),),
        in_specs=specs,
        out_specs=out_specs,
        out_shape=[jax.ShapeDtypeStruct(s, t) for s, t in outs],
        scratch_shapes=scratch,
        compiler_params=pltpu.CompilerParams(vmem_limit_bytes=VMEM_BYTES),
        cost_estimate=cost(24 if last else 18),
        name="forward_%d" % depth,
    )(*args)
    return results[:-count], [results[-count:][i : i + EXPERTS] for i in range(0, count, EXPERTS)]


def expert_forward_kernel(chunks, *refs):
    sources, refs = refs[:chunks], refs[chunks:]
    up_ref, down_ref, refs = refs[0], refs[1], refs[2:]
    returns, refs = refs[:chunks], refs[chunks:]
    hidden_ref, slope_ref = refs
    width = up_ref.shape[1]
    tile = FTILE if width % FTILE == 0 else FCHUNK
    tiles = [(k, f) for k in range(0, chunks, JOIN) for f in range(0, width, tile)]
    joined = [
        jnp.concatenate([r[...] for r in sources[k : k + JOIN]], axis=0)
        for k in range(0, chunks, JOIN)
    ]
    first = lambda k, f: mm(joined[k // JOIN], up_ref[:, f : f + tile])
    ready = first(*tiles[0])
    for at, (k, f) in enumerate(tiles):
        u = ready
        if at + 1 < len(tiles):
            ready = first(*tiles[at + 1])
        rows = slice(k * ROWS, (k + JOIN) * ROWS)
        value, slope = gelu_parts(u)
        hidden_ref[rows, f : f + tile] = value.astype(BF16)
        slope_ref[rows, f : f + tile] = slope.astype(BF16)
        if f + tile >= width:
            y = mm(hidden_ref[rows], down_ref[...]).astype(BF16)
            for j in range(JOIN):
                returns[k + j][...] = y[j * ROWS : (j + 1) * ROWS]


def expert_inner_kernel(chunks, *refs):
    sources, refs = refs[:chunks], refs[chunks:]
    slope_ref, up_ref, down_ref, refs = refs[0], refs[1], refs[2], refs[3:]
    returns, refs = refs[:chunks], refs[chunks:]
    (du_ref,) = refs
    width = up_ref.shape[1]
    tile = FTILE if width % FTILE == 0 else FCHUNK
    tiles = [(k, f) for k in range(chunks) for f in range(0, width, tile)]
    first = lambda k, f: mm(sources[k][...], down_ref[f : f + tile], NT)
    ready = first(*tiles[0])
    for at, (k, f) in enumerate(tiles):
        dh = ready
        if at + 1 < len(tiles):
            ready = first(*tiles[at + 1])
        rows = slice(k * ROWS, (k + 1) * ROWS)
        du_ref[rows, f : f + tile] = (dh * slope_ref[rows, f : f + tile].astype(F32)).astype(
            BF16
        )
        if f + tile >= width:
            returns[k][...] = mm(du_ref[rows], up_ref[...], NT).astype(BF16)


def run_expert(kernel, name, sources, slopes, up, down, wides, time):
    rows, width = ROWS * len(sources), up.shape[1]
    results = pl.pallas_call(
        partial(kernel, len(sources)),
        out_shape=[jax.ShapeDtypeStruct((ROWS, D), BF16)] * len(sources)
        + [jax.ShapeDtypeStruct((rows, width), BF16)] * wides,
        compiler_params=pltpu.CompilerParams(vmem_limit_bytes=EXPERT_VMEM),
        cost_estimate=cost(time),
        name=name,
    )(*sources, *slopes, up, down)
    return results[: len(sources)], results[len(sources) :]


def run_expert_forward(sources, up, down):
    return run_expert(expert_forward_kernel, "expert_forward", sources, [], up, down, 2, 5.5)


def run_expert_inner(sources, slope, up, down):
    return run_expert(expert_inner_kernel, "expert_inner", sources, [slope], up, down, 1, 4)


def expert_weights_kernel(chunks, parts, order, *refs):
    if order:
        order_ref, refs = refs[0], refs[1:]
    ns, refs = refs[:chunks], refs[chunks:]
    dys, refs = refs[:chunks], refs[chunks:]
    hiddens, refs = refs[:parts], refs[parts:]
    dus, refs = refs[:parts], refs[parts:]
    if order:
        keep_ref, send_ref, n_rows, dy_rows, sum_ref = refs
    else:
        out_ref, n_rows, dy_rows = refs
    for k in range(chunks):
        n_rows[k * ROWS : (k + 1) * ROWS] = ns[k][...]
        dy_rows[k * ROWS : (k + 1) * ROWS] = dys[k][...]
    for f in range(0, hiddens[0].shape[1], FCHUNK):
        columns = slice(f, f + FCHUNK)
        up, down, at = 0.0, 0.0, 0
        for hidden, du in zip(hiddens, dus):
            rows = slice(at, at + du.shape[0])
            at += du.shape[0]
            up = up + mm(n_rows[rows], du[:, columns], TN)
            down = down + mm(hidden[:, columns], dy_rows[rows], TN)
        if order:
            sum_ref[0:D] = up
            sum_ref[D : 2 * D] = down
            spread_blocks(order_ref, sum_ref, keep_ref, send_ref, columns)
        else:
            out_ref[0:D, columns] = up.astype(BF16)
            out_ref[D : 2 * D, columns] = down.astype(BF16)


def spread_blocks(order_ref, sum_ref, keep_ref, send_ref, columns):
    count = sum_ref.shape[0] // BLOCK
    for j in range(count):
        start = pl.multiple_of(jnp.bitwise_xor(order_ref[0], j) * BLOCK, BLOCK)
        block = sum_ref[pl.ds(start, BLOCK)].astype(BF16)
        ref = keep_ref if j < count // 2 else send_ref
        at = (j % (count // 2)) * BLOCK
        ref[at : at + BLOCK, columns] = block


def run_expert_weights(ns, dys, hiddens, dus, order=None):
    width = hiddens[0].shape[1]
    rows = ROWS * len(ns)
    scratch = [pltpu.VMEM((rows, D), BF16)] * 2
    shape, leading, specs = jax.ShapeDtypeStruct((2 * D, width), BF16), [], None
    if order is not None:
        shape = [jax.ShapeDtypeStruct((D, width), BF16)] * 2
        leading = [order]
        scratch.append(pltpu.VMEM((2 * D, FCHUNK), F32))
    vmem = pl.BlockSpec(memory_space=pltpu.VMEM)
    return pl.pallas_call(
        partial(expert_weights_kernel, len(ns), len(hiddens), order is not None),
        in_specs=[pl.BlockSpec(memory_space=pltpu.SMEM)] * len(leading)
        + [vmem] * (2 * len(ns) + 2 * len(hiddens)),
        out_shape=shape,
        scratch_shapes=scratch,
        compiler_params=pltpu.CompilerParams(vmem_limit_bytes=EXPERT_VMEM),
        cost_estimate=cost(6.5),
        name="expert_weights",
    )(*leading, *ns, *dys, *hiddens, *dus)


def backward_kernel(depth, images, chunks, order, *refs):
    last = depth == LAYERS - 1
    refs = list(refs)
    take = lambda: refs.pop(0)
    if order:
        order_ref = take()
    g_ref = take()
    dn_back = [take() for _ in range(chunks)]
    if last:
        y_back = [take() for _ in range(chunks)]
        before_gate_ref, before_target_ref = take(), take()
    else:
        picked_ref = take()
    (x_ref, qkv_ref, a_ref, mixed_ref, mid_ref, n_ref, probs_ref, gate_ref) = refs[:8]
    (route_ref, target_ref, g1_ref, g2_ref, attend_ref, out_w_ref) = refs[8:14]
    (router_ref, bias_ref, mask_ref, perm_ref, perm_back_ref) = refs[14:19]
    refs = refs[19:]
    g_out_ref = take()
    mats_refs = [take() for _ in range(2 if order else 1)]
    vecs_ref, table_ref = take(), take()
    if last:
        result_ref = take()
        outgoing = [take() for _ in range(EXPERTS)]
    attend_acc, out_acc, dqkv_ref, dz_ref, dn_ref = (take() for _ in range(5))
    if last:
        y_ref, dy_rows_ref = take(), take()

    step = pl.program_id(0)

    @pl.when(step == 0)
    def _():
        attend_acc[...] = jnp.zeros_like(attend_acc)
        out_acc[...] = jnp.zeros_like(out_acc)
        vecs_ref[...] = jnp.zeros_like(vecs_ref)
        table_ref[...] = jnp.zeros_like(table_ref)
        join_chunks(dn_ref, dn_back)
        if last:
            join_chunks(y_ref, y_back)
            dy_rows_ref[...] = jnp.zeros_like(dy_rows_ref)

    some = range(g_ref.shape[0])
    lane = lax.broadcasted_iota(jnp.int32, (HW, LANES), 1)
    grad_mids, dmixed_all = [], []
    for b in some:
        grad = g_ref[b].astype(F32)
        mid = mid_ref[b]
        gate = gate_ref[b][:, 0:1]
        if last:
            picked = pick_rows(target_ref[b], y_ref)
            result_ref[b] = (mid + gate * picked).astype(BF16)
        else:
            picked = picked_ref[b].astype(F32)
        gate_grad = jnp.sum(grad * picked, axis=-1, keepdims=True)
        chosen = jnp.where(lane == as_column(route_ref[b], HW), 1.0, 0.0)
        logit_grad = ((gate * gate_grad) * (chosen - probs_ref[b])).astype(BF16)
        router_grad = mm(logit_grad, n_ref[b], TN)
        grad_n = pick_rows(target_ref[b], dn_ref) + mm(logit_grad, router_ref[0], NT)
        unit, inverse = norm_parts(mid)
        vecs_ref[2:3] += jnp.sum(grad_n * unit, axis=0, keepdims=True)
        vecs_ref[3:4] += jnp.sum(grad_n, axis=0, keepdims=True)
        vecs_ref[8:16] += router_grad[0:8]
        grad_mid = grad + norm_back(grad_n, unit, inverse, g2_ref[depth : depth + 1])
        grad_mids.append(grad_mid)
        dz = mm(perm_ref[...], grad_mid.astype(BF16)).astype(BF16)
        dz_ref[b] = dz
    dz = dz_ref[...].reshape(len(some) * WROWS, D)
    out_acc[...] += mm(mixed_ref[...].reshape(len(some) * WROWS, D), dz, TN)
    dmixed_all = mm(dz, out_w_ref[0], NT).astype(BF16)
    masks = head_masks()
    def first_part(items):
        dm_wide, dprobs = [], []
        for w, g, b in items:
            start = b * WROWS + w * LPAD
            dm_wide.append(
                spread_heads(dmixed_all[start : start + LPAD, group_cols(0, g)], masks)
            )
        for (w, g, b), dm in zip(items, dm_wide):
            rows = slice(w * LPAD, (w + 1) * LPAD)
            dprobs.append(mm(qkv_ref[b, rows, group_cols(2, g)], dm, NT))
        return raw_scores(qkv_ref, items, masks) + (dm_wide, dprobs)

    runs = window_items(some)
    ready = first_part(runs[0])
    for at, items in enumerate(runs):
        places = [(b, slice(w * LPAD, (w + 1) * LPAD), g) for w, g, b in items]
        q_wide, scores, dm_wide, dprobs = ready
        if at + 1 < len(runs):
            ready = first_part(runs[at + 1])
        probs = to_probs(items, scores, bias_ref, mask_ref)
        dscores, tables = [], {}
        for (b, rows, g), p, dp in zip(places, probs, dprobs):
            row_dot = jnp.sum(p * dp, axis=0, keepdims=True)
            dscores.append((p * (dp - row_dot)).astype(BF16))
            wide = dscores[-1].astype(F32)
            tables[g] = tables[g] + wide if g in tables else wide
        for g, total in tables.items():
            table_ref[:, g * GW : (g + 1) * GW] += total
        dv, dk, tall = [], [], []
        for p, dm in zip(probs, dm_wide):
            dv.append(mm(p.astype(BF16), dm))
        for ds, q in zip(dscores, q_wide):
            dk.append(mm(ds, q))
        for (b, rows, g), ds in zip(places, dscores):
            tall.append(mm(ds, qkv_ref[b, rows, group_cols(1, g)], TN))
        for i, (b, rows, g) in enumerate(places):
            dq = fold_heads(tall[i], masks) * score_scale
            dqkv_ref[b, rows, group_cols(0, g)] = dq.astype(BF16)
            dqkv_ref[b, rows, group_cols(1, g)] = (dk[i] * score_scale).astype(BF16)
            dqkv_ref[b, rows, group_cols(2, g)] = dv[i].astype(BF16)
    dqkv = dqkv_ref[...].reshape(len(some) * WROWS, 3 * D)
    attend_acc[...] += mm(a_ref[...].reshape(len(some) * WROWS, D), dqkv, TN)
    for b in some:
        dqkv_tokens = mm(perm_back_ref[...], dqkv_ref[b]).astype(BF16)
        grad_normed = mm(dqkv_tokens, attend_ref[0], NT)
        unit, inverse = norm_parts(x_ref[b].astype(F32))
        vecs_ref[0:1] += jnp.sum(grad_normed * unit, axis=0, keepdims=True)
        vecs_ref[1:2] += jnp.sum(grad_normed, axis=0, keepdims=True)
        grad_x = grad_mids[b] + norm_back(grad_normed, unit, inverse, g1_ref[depth : depth + 1])
        g_out_ref[b] = grad_x.astype(g_out_ref.dtype)
        if last:
            dy = (before_gate_ref[b][:, 0:1] * grad_x).astype(BF16)
            dy_rows_ref[pl.ds(step * len(some) + b, 1), 0:HW, :] = dy[None]

    @pl.when(step == pl.num_programs(0) - 1)
    def _():
        for acc, columns in ((attend_acc, slice(0, 3 * D)), (out_acc, slice(3 * D, 4 * D))):
            if order:
                spread_blocks(order_ref, acc, *mats_refs, columns)
            else:
                mats_refs[0][:, columns] = acc[...].astype(BF16)
        if last:
            rows = dy_rows_ref[...].reshape(images * TPAD, D)
            send_rows([outgoing], before_target_ref[...], rows)


def run_backward(
    depth, grad, dn_back, extra, saved, route_rows, target_rows, shared, order=None
):
    images = grad.shape[0]
    last = depth == LAYERS - 1
    args, specs = [], []
    if order is not None:
        args.append(order)
        specs.append(pl.BlockSpec(memory_space=pltpu.SMEM))
    args += [grad] + list(dn_back)
    specs += [by_image(grad.shape)] + [whole(chunk.shape) for chunk in dn_back]
    if last:
        y_back, before_gate, before_target = extra
        args += list(y_back) + [before_gate, before_target]
        specs += [whole(chunk.shape) for chunk in y_back]
        specs += [by_image(before_gate.shape), whole(before_target.shape)]
    else:
        args.append(extra)
        specs.append(by_image(extra.shape))
    for array in saved + [route_rows, target_rows]:
        args.append(array)
        specs.append(by_image(array.shape))
    for name in ("first_gain", "second_gain"):
        args.append(shared[name])
        specs.append(whole(shared[name].shape))
    for name in ("attend_weight", "output_weight", "router"):
        args.append(shared[name])
        specs.append(layer_of(shared[name].shape, depth))
    for name in ("bias", "mask", "perm", "perm_back"):
        args.append(shared[name][depth])
        specs.append(whole(shared[name][depth].shape))
    token_shape = (images, HW, D)
    outs = [
        (token_shape, F32 if last else BF16, by_image(token_shape)),
    ]
    if order is None:
        outs.append(((D, 4 * D), BF16, whole((D, 4 * D))))
    else:
        outs += [((D // 2, 4 * D), BF16, whole((D // 2, 4 * D)))] * 2
    outs += [
        ((16, D), F32, whole((16, D))),
        ((LPAD, GROUPS * GW), F32, whole((LPAD, GROUPS * GW))),
    ]
    if last:
        outs.append((token_shape, BF16, by_image(token_shape)))
        outs += [((ROWS, D), BF16, whole((ROWS, D)))] * EXPERTS
    some = images_of(images)
    scratch = [
        pltpu.VMEM((D, 3 * D), F32),
        pltpu.VMEM((D, D), F32),
        pltpu.VMEM((some, WROWS, 3 * D), BF16),
        pltpu.VMEM((some, WROWS, D), BF16),
        pltpu.VMEM((len(dn_back) // EXPERTS, SLOTS, D), BF16),
    ]
    if last:
        scratch.append(pltpu.VMEM((len(y_back) // EXPERTS, SLOTS, D), BF16))
        scratch.append(pltpu.VMEM((images, TPAD, D), BF16))
    return pl.pallas_call(
        partial(backward_kernel, depth, images, len(dn_back), order is not None),
        grid=(images // images_of(images),),
        in_specs=specs,
        out_specs=[o[2] for o in outs],
        out_shape=[jax.ShapeDtypeStruct(o[0], o[1]) for o in outs],
        scratch_shapes=scratch,
        compiler_params=pltpu.CompilerParams(vmem_limit_bytes=VMEM_BYTES),
        cost_estimate=cost(33 if last else 24),
        name="backward_%d" % depth,
    )(*args)


def bits_of(axis, low, high):
    steps = []
    bit = low
    while bit < high:
        steps.append((axis, bit))
        bit *= 2
    return steps


def swap(x, step):
    axis, bit = step
    size = lax.axis_size(axis)
    return lax.ppermute(x, axis, [(i, i ^ bit) for i in range(size)])


def bit_at(step):
    axis, bit = step
    return (lax.axis_index(axis) // bit) % 2


def halved(rows, steps, least):
    count = 0
    while count < len(steps) and rows % 2 == 0 and rows // 2 >= least:
        rows //= 2
        count += 1
    return count


def sum_over(x, steps, least=24):
    count = halved(x.shape[0], steps, least)
    x = sum_all(scatter_sum(x, steps[:count]), steps[count:])
    return gather_all(x, steps[:count])


def scatter_sum(x, steps):
    for step in steps:
        half = x.shape[0] // 2
        mine = bit_at(step)
        keep = lax.dynamic_slice_in_dim(x, mine * half, half, 0)
        away = lax.dynamic_slice_in_dim(x, (1 - mine) * half, half, 0)
        x = (keep.astype(F32) + swap(away, step).astype(F32)).astype(x.dtype)
    return x


def gather_all(x, steps, dim=0):
    for step in reversed(steps):
        other = swap(x, step)
        mine = bit_at(step)
        first = jnp.where(mine == 0, x, other)
        second = jnp.where(mine == 0, other, x)
        x = jnp.concatenate([first, second], axis=dim)
    return x


def sum_all(x, steps):
    for step in steps:
        x = (x.astype(F32) + swap(x, step).astype(F32)).astype(x.dtype)
    return x


def exchange(chunks):
    groups = lax.axis_size("expert")
    if groups > EXPERTS:
        rows = jnp.stack(chunks)
        rows = lax.all_to_all(rows, "expert", split_axis=0, concat_axis=0, tiled=True)
        return [rows[k] for k in range(groups)]
    out = list(chunks)
    for k in SEND_ORDER:
        out[k] = lax.ppermute(chunks[k], "expert", [(i, i ^ k) for i in range(groups)])
    return out


def to_experts(chunks, slices):
    return exchange([chunk for chunk in chunks for _ in range(slices)])


def unpack_down(packed):
    width = packed.shape[1]
    return jnp.concatenate(
        [packed[:, j * D : (j + 1) * D] for j in range(width // D)], axis=0
    )


def add_kernel(cuts, keep_ref, got_ref, *outs):
    total = keep_ref[...].astype(F32) + got_ref[...].astype(F32)
    for (start, stop), out in zip(cuts, outs):
        out[...] = total[start:stop].astype(out.dtype)


def add_rows(keep, got, cuts):
    rows, width = got.shape
    return pl.pallas_call(
        partial(add_kernel, cuts),
        grid=(1,),
        in_specs=[pl.BlockSpec((rows, width), lambda i: (0, 0))] * 2,
        out_specs=[pl.BlockSpec((b - a, width), lambda i: (0, 0)) for a, b in cuts],
        out_shape=[jax.ShapeDtypeStruct((b - a, width), keep.dtype) for a, b in cuts],
        compiler_params=pltpu.CompilerParams(vmem_limit_bytes=12 * 1024 * 1024),
        cost_estimate=cost(1),
        name="add_rows",
    )(keep, got)


def join_kernel(first_ref, second_ref, out_ref):
    rows = first_ref.shape[0]
    out_ref[0:rows] = first_ref[...]
    out_ref[rows:] = second_ref[...]


def join_rows(first, second):
    rows, width = first.shape
    return pl.pallas_call(
        join_kernel,
        out_shape=jax.ShapeDtypeStruct((2 * rows, width), first.dtype),
        compiler_params=pltpu.CompilerParams(vmem_limit_bytes=8 * 1024 * 1024),
        cost_estimate=cost(1),
        name="join_rows",
    )(first, second)


def expert_outputs_kernel(earlier, order_ref, *refs):
    pieces, refs = refs[:8], refs[8:]
    refs = refs[4 if earlier else 0 :]
    outs, (rows_ref,) = refs[:4], refs[4:]
    step = pl.program_id(0)
    quarter = pieces[0].shape[0]

    @pl.when(step == 0)
    def _():
        for kind in range(2):
            for r in range(4):
                rows_ref[kind, r * quarter : (r + 1) * quarter] = pieces[kind * 4 + r][...]

    half = pl.num_programs(0)
    for kind in range(2):
        for part in range(2):
            place = jnp.bitwise_xor(order_ref[0], step + part * half)
            start = pl.multiple_of(place * BLOCK, BLOCK)
            block = rows_ref[kind, pl.ds(start, BLOCK)].astype(F32)
            out = outs[kind * 2 + part]
            if part == 0:
                out[0] = block
            else:
                for c in range(out.shape[1]):
                    out[0, c] = block[:, c * D : (c + 1) * D]


def expert_outputs(depth, order, residual, core, earlier):
    width = residual[0].shape[1]
    half = D // BLOCK
    count = width // D
    up = jax.ShapeDtypeStruct((LAYERS, D, width), F32)
    down = jax.ShapeDtypeStruct((LAYERS, count, D, D), F32)
    up_spec = pl.BlockSpec((1, BLOCK, width), lambda i: (depth, i, 0))
    down_spec = pl.BlockSpec((1, count, BLOCK, D), lambda i: (depth, 0, i, 0))
    pieces = residual + core
    earlier = list(earlier or [])
    return pl.pallas_call(
        partial(expert_outputs_kernel, bool(earlier)),
        grid=(half,),
        in_specs=[pl.BlockSpec(memory_space=pltpu.SMEM)]
        + [whole(p.shape) for p in pieces]
        + [pl.BlockSpec(memory_space=pl.ANY)] * len(earlier),
        out_specs=[up_spec, down_spec] * 2,
        out_shape=[up, down] * 2,
        scratch_shapes=[pltpu.VMEM((2, 2 * D, width), BF16)],
        input_output_aliases={9 + i: i for i in range(len(earlier))},
        compiler_params=pltpu.CompilerParams(vmem_limit_bytes=32 * 1024 * 1024),
        cost_estimate=cost(4),
        name="expert_outputs",
    )(order, *pieces, *earlier)


def attend_outputs_kernel(earlier, order_ref, *refs):
    pieces, refs = refs[:2], refs[2:]
    refs = refs[2 if earlier else 0 :]
    attend_ref, out_ref, rows_ref = refs
    half = pieces[0].shape[0]
    for r in range(2):
        rows_ref[r * half : (r + 1) * half] = pieces[r][...].astype(F32)
    for j in range(D // BLOCK):
        start = pl.multiple_of(jnp.bitwise_xor(order_ref[0], j) * BLOCK, BLOCK)
        block = rows_ref[pl.ds(start, BLOCK)]
        attend_ref[0, j * BLOCK : (j + 1) * BLOCK] = block[:, : 3 * D]
        out_ref[0, j * BLOCK : (j + 1) * BLOCK] = block[:, 3 * D :]


def attend_outputs(depth, order, pieces, earlier):
    earlier = list(earlier or [])
    shapes = [(LAYERS, D, 3 * D), (LAYERS, D, D)]
    return pl.pallas_call(
        partial(attend_outputs_kernel, bool(earlier)),
        grid=(1,),
        in_specs=[pl.BlockSpec(memory_space=pltpu.SMEM)]
        + [whole(p.shape) for p in pieces]
        + [pl.BlockSpec(memory_space=pl.ANY)] * len(earlier),
        out_specs=[layer_of(shape, depth) for shape in shapes],
        out_shape=[jax.ShapeDtypeStruct(shape, F32) for shape in shapes],
        scratch_shapes=[pltpu.VMEM((D, 4 * D), F32)],
        input_output_aliases={3 + i: i for i in range(len(earlier))},
        compiler_params=pltpu.CompilerParams(vmem_limit_bytes=24 * 1024 * 1024),
        cost_estimate=cost(2),
        name="attend_outputs",
    )(order, *pieces, *earlier)


CORE, ROW = ("dp", 1), ("dp", 2)
NEAR_X, NEAR_Z, FAR_Z = ("expert", 1), ("expert", 2), ("expert", 4)


def place_order(steps):
    order = 0
    for step in steps:
        order = order * 2 + bit_at(step)
    return jnp.full((1,), order, jnp.int32)


class ExpertSum:
    def __init__(self, keep, send):
        self.keep, self.send = keep, send
        self.steps = iter(
            (self.core, self.row, self.near_x, self.near_z, self.far_z, self.back_z, self.back_x)
        )

    def run(self, count):
        for _ in range(count):
            next(self.steps)()
        return self.done

    def core(self):
        quarter = self.keep.shape[0] // 2
        cuts = ((0, quarter), (quarter, 2 * quarter))
        self.keep, self.send = add_rows(self.keep, swap(self.send, CORE), cuts)
        self.done = [self.keep, self.send]

    def row(self):
        quarter = self.keep.shape[0]
        cuts = ((0, quarter), (quarter // 2, quarter))
        self.mine, self.send = add_rows(self.keep, swap(self.send, ROW), cuts)
        self.done = [self.mine, self.send]

    def near_x(self):
        rows = self.send.shape[0]
        cuts = ((0, rows // 2), (rows // 2, rows))
        self.keep, self.send = add_rows(self.mine, swap(self.send, NEAR_X), cuts)
        self.done = [self.keep, self.send]

    def near_z(self):
        rows = self.send.shape[0]
        (self.total,) = add_rows(self.keep, swap(self.send, NEAR_Z), ((0, rows),))
        self.done = [self.total]

    def far_z(self):
        rows = self.total.shape[0]
        (self.total,) = add_rows(self.total, swap(self.total, FAR_Z), ((0, rows),))
        self.done = [self.total]

    def back_z(self):
        self.total = join_rows(self.total, swap(self.total, NEAR_Z))
        self.done = [self.total]

    def back_x(self):
        self.total = join_rows(self.total, swap(self.total, NEAR_X))
        self.done = [self.total]

    def residual_row(self):
        self.mine_row = swap(self.mine, ROW)
        return [self.mine_row]

    def residual_core(self):
        self.residual = [self.mine, self.mine_row, swap(self.mine, CORE), swap(self.mine_row, CORE)]
        return self.residual[2:]

    def core_row(self):
        self.total_row = swap(self.total, ROW)
        return [self.total_row]

    def core_core(self):
        self.whole = [self.total, self.total_row, swap(self.total, CORE), swap(self.total_row, CORE)]
        return self.whole[2:]


class AttendSum:
    def __init__(self, keep, send):
        self.keep, self.send = keep, send
        self.steps = iter(
            [lambda step=step: self.halve(step) for step in (CORE, ROW, NEAR_X)]
            + [lambda step=step: self.add(step) for step in (NEAR_Z, FAR_Z)]
            + [lambda step=step: self.join(step) for step in (NEAR_X, ROW)]
            + [self.last]
        )

    def run(self, count):
        for _ in range(count):
            next(self.steps)()
        return self.done

    def halve(self, step):
        rows = self.send.shape[0]
        got = swap(self.send, step)
        if step == NEAR_X:
            (self.keep,) = add_rows(self.keep, got, ((0, rows),))
            self.done = [self.keep]
        else:
            cuts = ((0, rows // 2), (rows // 2, rows))
            self.keep, self.send = add_rows(self.keep, got, cuts)
            self.done = [self.keep, self.send]

    def add(self, step):
        (self.keep,) = add_rows(self.keep, swap(self.keep, step), ((0, self.keep.shape[0]),))
        self.done = [self.keep]

    def join(self, step):
        self.keep = join_rows(self.keep, swap(self.keep, step))
        self.done = [self.keep]

    def last(self):
        self.pieces = [self.keep, swap(self.keep, CORE)]
        self.done = self.pieces


def after(value, *done):
    return lax.optimization_barrier((value,) + done)[0]


def body(
    block_input,
    routes,
    first_gain,
    first_shift,
    attend_weight,
    bias_table,
    output_weight,
    second_gain,
    second_shift,
    router_weight,
    core_up,
    core_down,
    residual_up,
    residual_down,
    cotangent,
):
    groups = lax.axis_size("expert")
    slices = groups // EXPERTS
    group_part = lax.axis_index("expert") % slices
    images = block_input.shape[0]
    width = residual_up.shape[2]

    routes_rows = jnp.pad(
        routes.reshape(LAYERS, images, HW), ((0, 0), (0, 0), (0, TPAD - HW)), constant_values=-1
    )
    flip = lax.axis_index("expert") if slices == 1 else 0
    targets = run_routing(routes_rows, jnp.full((1,), flip, jnp.int32))

    table_index = jnp.asarray(offset_table(), jnp.int32)
    picker = (jnp.arange(OFFSETS, dtype=jnp.int32)[:, None] == table_index[None, :]).astype(F32)
    flat_table = bias_table.transpose(0, 2, 1).reshape(LAYERS * HEADS, OFFSETS)
    bias = jnp.dot(flat_table, picker, precision=lax.Precision.HIGHEST)
    bias = (
        bias.reshape(LAYERS, HEADS, LPAD, LPAD)
        .transpose(0, 2, 1, 3)
        .reshape(LAYERS, LPAD, HEADS * LPAD)
    )
    offsets = [SHIFT * (depth % 2) for depth in range(LAYERS)]
    shared = {
        "first_gain": first_gain,
        "first_shift": first_shift,
        "second_gain": second_gain,
        "second_shift": second_shift,
        "attend_weight": attend_weight,
        "output_weight": output_weight,
        "router": jnp.pad(router_weight, ((0, 0), (0, 0), (0, LANES - EXPERTS))),
        "bias": [bias[depth] for depth in range(LAYERS)],
        "mask": [jnp.asarray(score_mask(o)) for o in offsets],
        "perm": [jnp.asarray(permutation(o), BF16) for o in offsets],
        "perm_back": [jnp.asarray(permutation(o).T, BF16) for o in offsets],
    }
    route_rows = [routes_rows[d].reshape(images, 1, TPAD) for d in range(LAYERS)]
    target_rows = [targets[d].reshape(images, 1, TPAD) for d in range(LAYERS)]
    target_all = [targets[d].reshape(1, images * TPAD) for d in range(LAYERS)]
    ups, downs = [], []
    for d in range(LAYERS):
        up_core = lax.dynamic_slice_in_dim(core_up[d], group_part * width, width, 1)
        down_core = lax.dynamic_slice_in_dim(core_down[d], group_part * width, width, 0)
        ups.append((up_core.astype(F32) + residual_up[d].astype(F32)).astype(BF16))
        downs.append((down_core.astype(F32) + residual_down[d].astype(F32)).astype(BF16))

    picked_type = BF16 if slices == 1 else F32
    saved, inner, gates, xs, picks = [], [], [], [block_input], []
    x, earlier = block_input, None
    dy_arrived = None
    def in_parts(chunks):
        return [chunks[i : i + PART] for i in range(0, len(chunks), PART)]

    for d in range(LAYERS):
        outs, outgoing = run_forward(
            d, x, earlier, cotangent, route_rows[d], target_rows[d], target_all[d], shared
        )
        qkv, a, mixed, mid, n, probs, gate = outs[:7]
        if d:
            xs.append(outs[7])
            picks.append(outs[8])
        arrived = to_experts(outgoing[0], slices)
        if d == LAYERS - 1:
            dy_arrived = to_experts(outgoing[1], slices)
        ys, hiddens, slopes = [], [], []
        for part in in_parts(arrived):
            y, (hidden, slope) = run_expert_forward(part, ups[d], downs[d])
            ys += y
            hiddens.append(hidden)
            slopes.append(slope)
        back = exchange(ys)
        earlier = (back, gate, target_rows[d], picked_type)
        x = mid
        gates.append(gate)
        saved.append([xs[d], qkv, a, mixed, mid, n, probs, gate])
        inner.append((arrived, hiddens, slopes))

    grad = cotangent
    vecs, tables = [None] * 2, [None] * 2
    block_output = None
    alone = slices == 1
    expert_order = place_order((CORE, ROW, NEAR_X, NEAR_Z)) if alone else None
    attend_order = place_order((CORE, ROW, NEAR_X)) if alone else None
    expert_sums, attend_sums = [None] * 2, [None] * 2
    for d in reversed(range(LAYERS)):
        arrived, hiddens, slopes = inner[d]
        dns, dus = [], []
        for at, (part, slope) in enumerate(zip(in_parts(dy_arrived), slopes)):
            if alone and d == 0:
                if at == 0:
                    slope = after(slope, *expert_sums[1].run(1))
                    expert_sums[1].residual_row()
                else:
                    slope = after(slope, *expert_sums[1].run(1), *attend_sums[1].run(1))
            dn, (du,) = run_expert_inner(part, slope, ups[d], downs[d])
            dns += dn
            dus.append(du)
        dn_back = exchange(dns)
        grads = run_expert_weights(arrived, dy_arrived, hiddens, dus, expert_order)
        expert_sums[d] = ExpertSum(*grads) if alone else grads
        if d == LAYERS - 1:
            extra = (earlier[0], gates[d - 1], target_all[d - 1])
        else:
            extra = picks[d]
        if alone:
            done = expert_sums[d].run(1 if d else 2)
            if d == 0:
                done = done + expert_sums[1].run(4) + [expert_sums[1].mine_row]
                done = done + attend_sums[1].run(4)
            grad = after(grad, *done)
        outs = run_backward(
            d,
            grad,
            dn_back,
            extra,
            saved[d],
            route_rows[d],
            target_rows[d],
            shared,
            attend_order,
        )
        if alone:
            grad, keep, send, vecs[d], tables[d] = outs[:5]
            attend_sums[d] = AttendSum(keep, send)
            outs = outs[5:]
        else:
            grad, attend_sums[d], vecs[d], tables[d] = outs[:4]
            outs = outs[4:]
        if d == LAYERS - 1:
            block_output = outs[0]
            dy_arrived = to_experts(outs[1:], slices)
    input_grad = grad

    dp_steps = bits_of("dp", 1, lax.axis_size("dp"))
    slice_steps = bits_of("expert", 1, slices)
    sum_steps = bits_of("expert", slices, groups)
    all_steps = dp_steps + slice_steps + sum_steps
    if alone:
        experts, full = None, None
        for d in reversed(range(LAYERS)):
            sums, attend = expert_sums[d], attend_sums[d]
            if d:
                sums.residual_core()
                sums.core_row()
                sums.core_core()
                attend.run(3)
            else:
                sums.residual_row()
                sums.run(5)
                sums.residual_core()
                sums.core_row()
                sums.core_core()
                attend.run(8)
            experts = expert_outputs(d, expert_order, sums.residual, sums.whole, experts)
            full = attend_outputs(d, attend_order, attend.pieces, full)
        residual_up_grad, residual_down_grad, core_up_grad, core_down_grad = experts
        residual_down_grad = residual_down_grad.reshape(LAYERS, width, D)
        core_down_grad = core_down_grad.reshape(LAYERS, width, D)
        attend_weight_grad, output_weight_grad = full
    else:
        residual, core, full = [], [], []
        for d in range(LAYERS):
            part = scatter_sum(expert_sums[d], dp_steps)
            residual.append(gather_all(part, dp_steps))
            total = gather_all(sum_over(part, sum_steps), dp_steps)
            core.append(gather_all(total, slice_steps, dim=1))
            full.append(sum_over(attend_sums[d], all_steps))
        full = jnp.stack(full).astype(F32)
        attend_weight_grad, output_weight_grad = full[:, :, : 3 * D], full[:, :, 3 * D :]
        residual_up_grad = jnp.stack([r[:D] for r in residual]).astype(F32)
        residual_down_grad = jnp.stack([unpack_down(r[D:]) for r in residual]).astype(F32)
        core_up_grad = jnp.stack([c[:D] for c in core]).astype(F32)
        core_down_grad = jnp.stack([unpack_down(c[D:]) for c in core]).astype(F32)
    table_grad = jnp.stack(tables).reshape(LAYERS, LPAD, HEADS, LPAD).transpose(0, 2, 1, 3)
    table_grad = jnp.dot(
        table_grad.reshape(LAYERS * HEADS, LPAD * LPAD), picker.T, precision=lax.Precision.HIGHEST
    )
    small = jnp.concatenate(
        [
            jnp.stack(vecs).reshape(LAYERS * 16, D),
            jnp.pad(table_grad, ((0, 0), (0, D - OFFSETS))),
        ],
        axis=0,
    )
    small = sum_all(small, all_steps)
    vec = small[: LAYERS * 16].reshape(LAYERS, 16, D)
    table = small[LAYERS * 16 :, :OFFSETS].reshape(LAYERS, HEADS, OFFSETS).transpose(0, 2, 1)
    return (
        block_output,
        input_grad,
        vec[:, 0],
        vec[:, 1],
        attend_weight_grad,
        table,
        output_weight_grad,
        vec[:, 2],
        vec[:, 3],
        vec[:, 8:16].transpose(0, 2, 1),
        core_up_grad,
        core_down_grad,
        residual_up_grad,
        residual_down_grad,
    )


def solution(mesh):
    placed = (
        P(("dp", "expert"), None, None),
        P(None, ("dp", "expert"), None, None),
        P(),
        P(),
        P(),
        P(),
        P(),
        P(),
        P(),
        P(),
        P(),
        P(),
        P(None, None, "expert"),
        P(None, "expert", None),
        P(("dp", "expert"), None, None),
    )
    return jax.shard_map(
        body,
        mesh=mesh,
        in_specs=placed,
        out_specs=(
            P(("dp", "expert"), None, None),
            P(("dp", "expert"), None, None),
            P(),
            P(),
            P(),
            P(),
            P(),
            P(),
            P(),
            P(),
            P(),
            P(),
            P(None, None, "expert"),
            P(None, "expert", None),
        ),
        check_vma=False,
    )
```

time: 634 us -> 544 us (0.86)
  starting transfers between devices: 101 us -> 177 us
  waiting for transfers between devices: 198 us -> 150 us
  Pallas kernels: 209 us -> 165 us
  other arithmetic: 42.4 us -> 3.57 us
  blocking collectives: 31.6 us -> 0 us
    ppermute x0 -> x56, starting transfers between devices: none -> 106 us  [exchange(): lax.ppermute(chunks[k], 'expert', [(i, i ^ k) for i in range(groups)])]
    ppermute x0 -> x56, waiting for transfers between devices: none -> 102 us  [exchange(): lax.ppermute(chunks[k], 'expert', [(i, i ^ k) for i in range(groups)])]
    all_to_all x7 -> x0, waiting for transfers between devices: 95.9 us -> none  [exchange(): lax.all_to_all(buffers.reshape(groups, CAP, D), 'expert', split_axis=0, c...]
    ppermute x47, waiting for transfers between devices: 102 us -> 47.6 us  [swap(): return lax.ppermute(x, axis, [(i, i ^ bit) for i in range(size)])]
    pallas_call x11 -> x47, Pallas kernels: 209 us -> 165 us  [the longest x2 57.9 us: run_backward(): pl.pallas_call(partial(backward_kernel, depth, images, len(dn_back), orde...]
    all_to_all x7 -> x0, starting transfers between devices: 33 us -> none  [exchange(): lax.all_to_all(buffers.reshape(groups, CAP, D), 'expert', split_axis=0, c...]
    all_to_all x1 -> x0, blocking collectives: 31.6 us -> none  [exchange(): lax.all_to_all(buffers.reshape(groups, CAP, D), 'expert', split_axis=0, c...]
    convert_element_type x25 -> x0, other arithmetic: 16.5 us -> none  [the longest x18 6.14 us: scatter_sum(): x = (keep.astype(F32) + swap(away, step).astype(F32)).astype(x.dtype)]
  transfers between devices with their start and end apart: 54 -> 103, of which waited for: 30 -> 33; matrix products, arithmetic and copies ran while one was open for 9% -> 4% of each run, Pallas kernels for 18% -> 19%
where the time goes in v2:
time: 544 us; the launch traced here: 537 us
  starting transfers between devices  177 us (33%)
  Pallas kernels  165 us (30%)
  waiting for transfers between devices  150 us (28%)
  local copies, waits for them, and re-layouts  34.9 us (6%)
    ppermute x56, starting transfers between devices, exchange(): lax.ppermute(chunks[k], 'expert', [(i, i ^ k) for i in range(groups)])  106 us
    ppermute x56, waiting for transfers between devices, exchange(): lax.ppermute(chunks[k], 'expert', [(i, i ^ k) for i in range(groups)])  102 us
    ppermute x47, starting transfers between devices, swap(): return lax.ppermute(x, axis, [(i, i ^ bit) for i in range(size)])  71.2 us
    pallas_call x2, Pallas kernels, run_backward(): pl.pallas_call(partial(backward_kernel, depth, images, len(dn_back), orde...  57.9 us
    ppermute x47, waiting for transfers between devices, swap(): return lax.ppermute(x, axis, [(i, i ^ bit) for i in range(size)])  47.6 us
    pallas_call x2, Pallas kernels, run_forward(): pl.pallas_call(partial(forward_kernel, depth, images, len(back) if depth...  42 us
    pallas_call x8, Pallas kernels, run_expert(): pl.pallas_call(partial(kernel, len(sources)), out_shape=[jax.ShapeDtypeSt...  29.3 us
    unnamed x168, local copies, waits for them, and re-layouts  17.8 us
  transfers between devices with their start and end apart: 103, of which 33 were waited for; matrix products, arithmetic and copies ran while one was open for 4% of the time, Pallas kernels for 19%

profile of v2, /device:TPU:1, one launch (start us, length us, event | category | flops | bytes accessed | tf_op | source)
XLA Modules:
  0.0 536.7 jit_solution(9914355314368370648)
XLA Ops:
  12.5 18.1 %forward_0.1 = (bf16[6,256,1152]{2,1,0:T(8,128)(2,1)}, bf16[6,256,384]{2,1,0:T(8,128)(2,1)}, bf16[6,256,384]{2,1,0:T(8,128)(2,1)}, f32[6,196,384]{2,1,0:T(8,128)...) custom-call(bf16[6,196,384]{2,1,0:T(8,128)(2,1)} %refs_11_.4, ...), custom_call_target="tpu_custom_call" | custom-call | flops 16199999488 | bytes 1000 | tf_op jit(solution)/shard_map/forward_0/pallas_call | solution.py:400
  32.7 2.3 collective-permute-start.6
  35.0 3.3 collective-permute-start.8
  42.3 8.8 %collective-permute-done.6.refs_0_.refs_5_ = bf16[192,384]{1,0:T(8,128)(2,1)S(1)} collective-permute-done((bf16[192,384]{1,0:T(8,128)(2,1)}, bf16[192,384]{1,0:T(8,128)(2,1)S(1)}, u32[]{:S(2)}, u32[]{:S(2)}) %collective-permute-start.6) | collective-permute-done | bytes 147488 | tf_op jit(solution)/shard_map/ppermute | solution.py:821
  55.9 4.1 expert_forward.5
  62.8 10.7 %collective-permute-start.10 = (bf16[192,384]{1,0:T(8,128)(2,1)S(1)}, bf16[192,384]{1,0:T(8,128)(2,1)S(1)}, u32[]{:S(2)}, u32[]{:S(2)}) collective-permute-start(bf16[192,384]{1,0:T(8,128)(2,1)S(1)} %get-tuple-element.170), channel_id=1, source_target_pairs={{0,4},{1,5},{2,6},{3,7},{4,0},{5,1},{6,2},{7,3},{8,12},{9,13},{10,... | collective-permute-start | bytes 442376 | tf_op jit(solution)/shard_map/ppermute | solution.py:821
  73.9 3.8 collective-permute-start.13
  77.8 4.1 expert_forward.4
  86.0 4.2 collective-permute-done.10.refs_5_
  90.2 3.0 collective-permute-done.11.refs_6_
  96.4 2.8 collective-permute-done.5.refs_4_
  99.2 23.9 %forward_1.1 = (bf16[6,256,1152]{2,1,0:T(8,128)(2,1)}, bf16[6,256,384]{2,1,0:T(8,128)(2,1)}, bf16[6,256,384]{2,1,0:T(8,128)(2,1)}, f32[6,196,384]{2,1,0:T(8,128)...) custom-call(f32[6,196,384]{2,1,0:T(8,128)} %get-tuple-element.157.re, ...), custom_call_target="tpu_custom_call" | custom-call | flops 21600000000 | bytes 1000 | tf_op jit(solution)/shard_map/forward_1/pallas_call | solution.py:400
  126.6 2.9 collective-permute-start.19
  131.0 11.9 %collective-permute-start.15 = (bf16[192,384]{1,0:T(8,128)(2,1)}, bf16[192,384]{1,0:T(8,128)(2,1)S(1)}, u32[]{:S(2)}, u32[]{:S(2)}) collective-permute-start(bf16[192,384]{1,0:T(8,128)(2,1)} %get-tuple-element.177), channel_id=1, source_target_pairs={{0,2},{1,3},{2,0},{3,1},{4,6},{5,7},{6,4},{7,5},{8,10},{9,11},{10,... | collective-permute-start | bytes 442376 | tf_op jit(solution)/shard_map/ppermute | solution.py:821
  142.9 2.6 collective-permute-done.18.refs_1_.refs_6_
  147.3 8.9 %collective-permute-start.24 = (bf16[192,384]{1,0:T(8,128)(2,1)}, bf16[192,384]{1,0:T(8,128)(2,1)S(1)}, u32[]{:S(2)}, u32[]{:S(2)}) collective-permute-start(bf16[192,384]{1,0:T(8,128)(2,1)} %get-tuple-element.187), channel_id=1, source_target_pairs={{0,4},{1,5},{2,6},{3,7},{4,0},{5,1},{6,2},{7,3},{8,12},{9,13},{10,... | collective-permute-start | bytes 442376 | tf_op jit(solution)/shard_map/ppermute | solution.py:821
  157.4 4.7 expert_forward.7
  163.8 3.3 collective-permute-start.27
  167.1 3.5 expert_forward.6
  171.3 6.3 %collective-permute-done.25.refs_1_.refs_14_ = bf16[192,384]{1,0:T(8,128)(2,1)S(1)} collective-permute-done((bf16[192,384]{1,0:T(8,128)(2,1)S(1)}, bf16[192,384]{1,0:T(8,128)(2,1)S(1)}, u32[]{:S(2)}, u32[]{:S(2)}) %collective-permute-start.25) | collective-permute-done | bytes 147488 | tf_op jit(solution)/shard_map/ppermute | solution.py:821
  177.6 3.2 expert_inner.5
  182.9 3.2 expert_inner.4
  186.7 6.4 %expert_weights.2 = (bf16[384,1536]{1,0:T(8,128)(2,1)S(1)}, bf16[384,1536]{1,0:T(8,128)(2,1)S(1)}) custom-call(s32[1]{0:T(128)} %bitcast.1.refs_0_.order_ref, bf16[192,384]{1,0:T(8,128)(2,1)S(1)} %copy-done.34, bf16[192,384]{1,0:T(8,128)(2,1)S(1)} %collective-permute-done.14.refs_1_.refs_2_, bf16[192,384]{1,0:T(8,128)(2,1)S(1)} %collective-permute-done.15.refs_2_.refs_3_, ...), custom_call_target="tpu_custom_call" | custom-call | flops 5849999872 | bytes 1000 | tf_op jit(solution)/shard_map/expert_weights/pallas_call | solution.py:536
  195.0 5.4 %collective-permute-start.39 = (bf16[192,384]{1,0:T(8,128)(2,1)S(1)}, bf16[192,384]{1,0:T(8,128)(2,1)S(1)}, u32[]{:S(2)}, u32[]{:S(2)}) collective-permute-start(bf16[192,384]{1,0:T(8,128)(2,1)S(1)} %get-tuple-element.214), channel_id=1, source_target_pairs={{0,4},{1,5},{2,6},{3,7},{4,0},{5,1},{6,2},{7,3},{8,12},{9,13},{10,... | collective-permute-start | bytes 442376 | tf_op jit(solution)/shard_map/ppermute | solution.py:821
  204.6 12.6 %collective-permute-done.39.refs_14_ = bf16[192,384]{1,0:T(8,128)(2,1)S(1)} collective-permute-done((bf16[192,384]{1,0:T(8,128)(2,1)S(1)}, bf16[192,384]{1,0:T(8,128)(2,1)S(1)}, u32[]{:S(2)}, u32[]{:S(2)}) %collective-permute-start.39) | collective-permute-done | bytes 147488 | tf_op jit(solution)/shard_map/ppermute | solution.py:821
  217.2 3.9 collective-permute-done.40.refs_15_
  221.1 7.0 %collective-permute-start.34 = (bf16[192,384]{1,0:T(8,128)(2,1)S(1)}, bf16[192,384]{1,0:T(8,128)(2,1)S(1)}, u32[]{:S(2)}, u32[]{:S(2)}) collective-permute-start(bf16[192,384]{1,0:T(8,128)(2,1)S(1)} %get-tuple-element.208), channel_id=1, source_target_pairs={{0,6},{1,7},{2,4},{3,5},{4,2},{5,3},{6,0},{7,1},{8,14},{9,15},{10,... | collective-permute-start | bytes 442376 | tf_op jit(solution)/shard_map/ppermute | solution.py:821
  228.1 14.4 %collective-permute-done.32.refs_6_ = bf16[192,384]{1,0:T(8,128)(2,1)S(1)} collective-permute-done((bf16[192,384]{1,0:T(8,128)(2,1)S(1)}, bf16[192,384]{1,0:T(8,128)(2,1)S(1)}, u32[]{:S(2)}, u32[]{:S(2)}) %collective-permute-start.32) | collective-permute-done | bytes 147488 | tf_op jit(solution)/shard_map/ppermute | solution.py:821
  243.4 2.9 collective-permute-done.33.refs_7_
  246.3 3.4 collective-permute-start.38
  250.3 3.2 collective-permute-start.30
  257.9 2.6 collective-permute-done.31.refs_5_
  261.1 33.3 %backward_1.1 = (f32[6,196,384]{2,1,0:T(8,128)}, bf16[192,1536]{1,0:T(8,128)(2,1)}, bf16[192,1536]{1,0:T(8,128)(2,1)}, f32[16,384]{1,0:T(8,128)}, f32[64,768]{1,...) custom-call(s32[1]{0:T(128)} %bitcast.refs_0_.order_ref, ...), custom_call_target="tpu_custom_call" | custom-call | flops 29699999744 | bytes 1000 | tf_op jit(solution)/shard_map/backward_1/pallas_call | solution.py:740
  299.0 2.5 collective-permute-start.46
  302.0 2.3 collective-permute-start.47
  305.5 5.8 %collective-permute-done.45.refs_3_.refs_12_ = bf16[192,384]{1,0:T(8,128)(2,1)S(1)} collective-permute-done((bf16[192,384]{1,0:T(8,128)(2,1)}, bf16[192,384]{1,0:T(8,128)(2,1)S(1)}, u32[]{:S(2)}, u32[]{:S(2)}) %collective-permute-start.45) | collective-permute-done | bytes 147488 | tf_op jit(solution)/shard_map/ppermute | solution.py:821
  311.9 3.2 expert_inner.6
  318.9 3.1 collective-permute-done.49.refs_3_.refs_16_
  322.0 3.2 expert_inner.7
  325.4 5.2 expert_weights.3
  330.6 3.2 collective-permute-start.53
  335.0 7.4 %collective-permute-done.60.got_ref = bf16[96,1536]{1,0:T(8,128)(2,1)S(1)} collective-permute-done((bf16[96,1536]{1,0:T(8,128)(2,1)S(1)}, bf16[96,1536]{1,0:T(8,128)(2,1)S(1)}, u32[]{:S(2)}, u32[]{:S(2)}) %collective-permute-start.60) | collective-permute-done | bytes 294944 | tf_op jit(solution)/shard_map/ppermute | solution.py:765
  343.5 4.2 collective-permute-start.55
  347.7 3.8 collective-permute-start.62
  354.1 2.5 collective-permute-start.63
  362.4 5.2 collective-permute-done.63.got_ref
  368.9 2.7 collective-permute-start.58
  372.0 9.8 %collective-permute-done.64.refs_3_ = bf16[192,384]{1,0:T(8,128)(2,1)S(1)} collective-permute-done((bf16[192,384]{1,0:T(8,128)(2,1)S(1)}, bf16[192,384]{1,0:T(8,128)(2,1)S(1)}, u32[]{:S(2)}, u32[]{:S(2)}) %collective-permute-start.64) | collective-permute-done | bytes 147488 | tf_op jit(solution)/shard_map/ppermute | solution.py:821
  391.2 13.3 %collective-permute-done.68.refs_7_ = bf16[192,384]{1,0:T(8,128)(2,1)S(1)} collective-permute-done((bf16[192,384]{1,0:T(8,128)(2,1)S(1)}, bf16[192,384]{1,0:T(8,128)(2,1)S(1)}, u32[]{:S(2)}, u32[]{:S(2)}) %collective-permute-start.68) | collective-permute-done | bytes 147488 | tf_op jit(solution)/shard_map/ppermute | solution.py:821
  405.3 24.7 %backward_0.1 = (bf16[6,196,384]{2,1,0:T(8,128)(2,1)}, bf16[192,1536]{1,0:T(8,128)(2,1)}, bf16[192,1536]{1,0:T(8,128)(2,1)}, f32[16,384]{1,0:T(8,128)}, f32[64,768]{1,0:T(8,128)}) custom-call(s32[1]{0:T(128)} %bitcast.refs_0_.order_ref, f32[6,196,384]{2,1,0:T(8,128)} %get-tuple-element.260.refs_1_, bf16[192,384]{1,0:T(8,128)(2,1)} %copy-done.29, ...), custom_call_target="tpu_custom_call" | custom-call | flops 21600000000 | bytes 1000 | tf_op jit(solution)/shard_map/backward_0/pallas_call | solution.py:740
  429.9 2.9 collective-permute-start.76
  441.5 2.5 fusion
  445.0 5.4 collective-permute-start.91
  455.6 2.8 collective-permute-done.77.got_ref
  460.6 2.5 collective-permute-done.92.got_ref
  469.5 3.6 collective-permute-start.98
  478.7 2.6 collective-permute-done.80.got_ref
  481.3 4.8 collective-permute-start.88
  488.7 6.1 %expert_outputs.2 = (f32[2,384,1536]{2,1,0:T(8,128)}, f32[2,4,384,384]{3,2,1,0:T(8,128)}, f32[2,384,1536]{2,1,0:T(8,128)}, f32[2,4,384,384]{3,2,1,0:T(8,128)}) custom-call(s32[1]{0:T(128)} %bitcast.1.refs_0_.order_ref, bf16[192,1536]{1,0:T(8,128)(2,1)S(1)} %get-tuple-element.239.keep_ref.refs_0_, bf16[192,1536]{1,0:T(8,128)(2,1)S(1)} %copy-done.3, ...), custom_call_target="tpu_custom_call" | custom-call | flops 3600000000 | bytes 1000 | tf_op jit(solution)/shard_map/expert_outputs/pallas_call | solution.py:910
  495.9 5.3 collective-permute-done.87.refs_1_
  502.4 11.5 %collective-permute-done.95.refs_5_ = bf16[192,1536]{1,0:T(8,128)(2,1)S(1)} collective-permute-done((bf16[192,1536]{1,0:T(8,128)(2,1)S(1)}, bf16[192,1536]{1,0:T(8,128)(2,1)S(1)}, u32[]{:S(2)}, u32[]{:S(2)}) %collective-permute-start.95) | collective-permute-done | bytes 589856 | tf_op jit(solution)/shard_map/ppermute | solution.py:765
  515.6 4.6 collective-permute-done.82.second_ref
  527.1 6.1 %expert_outputs.3 = (f32[2,384,1536]{2,1,0:T(8,128)}, f32[2,4,384,384]{3,2,1,0:T(8,128)}, f32[2,384,1536]{2,1,0:T(8,128)}, f32[2,4,384,384]{3,2,1,0:T(8,128)}) custom-call(s32[1]{0:T(128)} %bitcast.1.refs_0_.order_ref, ...), custom_call_target="tpu_custom_call", output_to_operand_aliasing={{0}: (9, {}), {1}: (10, {}), {2}: (11, {}), {3}: (12, {})} | custom-call | flops 3600000000 | bytes 1000 | tf_op jit(solution)/shard_map/expert_outputs/pallas_call | solution.py:910
  533.3 2.9 attend_outputs.3
  (389 shorter events, 134.1 us)
Async XLA Ops:
  30.6 43.3 %collective-permute-start = (bf16[192,384]{1,0:T(8,128)(2,1)}, bf16[192,384]{1,0:T(8,128)(2,1)S(1)}, u32[]{:S(2)}, u32[]{:S(2)}) collective-permute-start(bf16[192,384]{1,0:T(8,128)(2,1)} %get-tuple-element.159), channel_id=1, source_target_pairs={{0,1},{1,0},{2,3},{3,2},{4,5},{5,4},{6,7},{7,6},{8,9},{9,8},{10,11... | collective-permute-start | bytes 442376 | tf_op jit(solution)/shard_map/ppermute | solution.py:821
  32.7 18.4 %collective-permute-start.6 = (bf16[192,384]{1,0:T(8,128)(2,1)}, bf16[192,384]{1,0:T(8,128)(2,1)S(1)}, u32[]{:S(2)}, u32[]{:S(2)}) collective-permute-start(bf16[192,384]{1,0:T(8,128)(2,1)} %get-tuple-element.166), channel_id=1, source_target_pairs={{0,4},{1,5},{2,6},{3,7},{4,0},{5,1},{6,2},{7,3},{8,12},{9,13},{10,... | collective-permute-start | bytes 442376 | tf_op jit(solution)/shard_map/ppermute | solution.py:821
  35.0 19.2 %collective-permute-start.7 = (bf16[192,384]{1,0:T(8,128)(2,1)}, bf16[192,384]{1,0:T(8,128)(2,1)S(1)}, u32[]{:S(2)}, u32[]{:S(2)}) collective-permute-start(bf16[192,384]{1,0:T(8,128)(2,1)} %get-tuple-element.167), channel_id=1, source_target_pairs={{0,5},{1,4},{2,7},{3,6},{4,1},{5,0},{6,3},{7,2},{8,13},{9,12},{10,... | collective-permute-start | bytes 442376 | tf_op jit(solution)/shard_map/ppermute | solution.py:821
  35.0 20.8 %collective-permute-start.8 = (bf16[192,384]{1,0:T(8,128)(2,1)}, bf16[192,384]{1,0:T(8,128)(2,1)S(1)}, u32[]{:S(2)}, u32[]{:S(2)}) collective-permute-start(bf16[192,384]{1,0:T(8,128)(2,1)} %get-tuple-element.168), channel_id=1, source_target_pairs={{0,6},{1,7},{2,4},{3,5},{4,2},{5,3},{6,0},{7,1},{8,14},{9,15},{10,... | collective-permute-start | bytes 442376 | tf_op jit(solution)/shard_map/ppermute | solution.py:821
  38.3 17.5 %collective-permute-start.9 = (bf16[192,384]{1,0:T(8,128)(2,1)}, bf16[192,384]{1,0:T(8,128)(2,1)S(1)}, u32[]{:S(2)}, u32[]{:S(2)}) collective-permute-start(bf16[192,384]{1,0:T(8,128)(2,1)} %get-tuple-element.169), channel_id=1, source_target_pairs={{0,7},{1,6},{2,5},{3,4},{4,3},{5,2},{6,1},{7,0},{8,15},{9,14},{10,... | collective-permute-start | bytes 442376 | tf_op jit(solution)/shard_map/ppermute | solution.py:821
  51.1 22.8 %collective-permute-start.1 = (bf16[192,384]{1,0:T(8,128)(2,1)S(1)}, bf16[192,384]{1,0:T(8,128)(2,1)S(1)}, u32[]{:S(2)}, u32[]{:S(2)}) collective-permute-start(bf16[192,384]{1,0:T(8,128)(2,1)S(1)} %copy-done.73), channel_id=1, source_target_pairs={{0,2},{1,3},{2,0},{3,1},{4,6},{5,7},{6,4},{7,5},{8,10},{9,11},{10,... | collective-permute-start | bytes 442376 | tf_op jit(solution)/shard_map/ppermute | solution.py:821
  54.2 23.5 %collective-permute-start.2 = (bf16[192,384]{1,0:T(8,128)(2,1)S(1)}, bf16[192,384]{1,0:T(8,128)(2,1)S(1)}, u32[]{:S(2)}, u32[]{:S(2)}) collective-permute-start(bf16[192,384]{1,0:T(8,128)(2,1)S(1)} %copy-done.70), channel_id=1, source_target_pairs={{0,3},{1,2},{2,1},{3,0},{4,7},{5,6},{6,5},{7,4},{8,11},{9,10},{10,... | collective-permute-start | bytes 442376 | tf_op jit(solution)/shard_map/ppermute | solution.py:821
  62.8 27.4 %collective-permute-start.10 = (bf16[192,384]{1,0:T(8,128)(2,1)S(1)}, bf16[192,384]{1,0:T(8,128)(2,1)S(1)}, u32[]{:S(2)}, u32[]{:S(2)}) collective-permute-start(bf16[192,384]{1,0:T(8,128)(2,1)S(1)} %get-tuple-element.170), channel_id=1, source_target_pairs={{0,4},{1,5},{2,6},{3,7},{4,0},{5,1},{6,2},{7,3},{8,12},{9,13},{10,... | collective-permute-start | bytes 442376 | tf_op jit(solution)/shard_map/ppermute | solution.py:821
  73.6 19.7 %collective-permute-start.11 = (bf16[192,384]{1,0:T(8,128)(2,1)S(1)}, bf16[192,384]{1,0:T(8,128)(2,1)S(1)}, u32[]{:S(2)}, u32[]{:S(2)}) collective-permute-start(bf16[192,384]{1,0:T(8,128)(2,1)S(1)} %get-tuple-element.171), channel_id=1, source_target_pairs={{0,5},{1,4},{2,7},{3,6},{4,1},{5,0},{6,3},{7,2},{8,13},{9,12},{10,... | collective-permute-start | bytes 442376 | tf_op jit(solution)/shard_map/ppermute | solution.py:821
  73.9 22.5 %collective-permute-start.12 = (bf16[192,384]{1,0:T(8,128)(2,1)}, bf16[192,384]{1,0:T(8,128)(2,1)}, u32[]{:S(2)}, u32[]{:S(2)}) collective-permute-start(bf16[192,384]{1,0:T(8,128)(2,1)} %get-tuple-element.172), channel_id=1, source_target_pairs={{0,6},{1,7},{2,4},{3,5},{4,2},{5,3},{6,0},{7,1},{8,14},{9,15},{10,... | collective-permute-start | bytes 442376 | tf_op jit(solution)/shard_map/ppermute | solution.py:821
  73.9 22.4 %collective-permute-start.13 = (bf16[192,384]{1,0:T(8,128)(2,1)}, bf16[192,384]{1,0:T(8,128)(2,1)}, u32[]{:S(2)}, u32[]{:S(2)}) collective-permute-start(bf16[192,384]{1,0:T(8,128)(2,1)} %get-tuple-element.173), channel_id=1, source_target_pairs={{0,7},{1,6},{2,5},{3,4},{4,3},{5,2},{6,1},{7,0},{8,15},{9,14},{10,... | collective-permute-start | bytes 442376 | tf_op jit(solution)/shard_map/ppermute | solution.py:821
  85.4 11.0 %collective-permute-start.3 = (bf16[192,384]{1,0:T(8,128)(2,1)}, bf16[192,384]{1,0:T(8,128)(2,1)}, u32[]{:S(2)}, u32[]{:S(2)}) collective-permute-start(bf16[192,384]{1,0:T(8,128)(2,1)} %get-tuple-element.163), channel_id=1, source_target_pairs={{0,1},{1,0},{2,3},{3,2},{4,5},{5,4},{6,7},{7,6},{8,9},{9,8},{10,11... | collective-permute-start | bytes 442376 | tf_op jit(solution)/shard_map/ppermute | solution.py:821
  125.2 20.3 %collective-permute-start.18 = (bf16[192,384]{1,0:T(8,128)(2,1)}, bf16[192,384]{1,0:T(8,128)(2,1)}, u32[]{:S(2)}, u32[]{:S(2)}) collective-permute-start(bf16[192,384]{1,0:T(8,128)(2,1)} %get-tuple-element.180), channel_id=1, source_target_pairs={{0,5},{1,4},{2,7},{3,6},{4,1},{5,0},{6,3},{7,2},{8,13},{9,12},{10,... | collective-permute-start | bytes 442376 | tf_op jit(solution)/shard_map/ppermute | solution.py:821
  126.6 19.2 %collective-permute-start.19 = (bf16[192,384]{1,0:T(8,128)(2,1)}, bf16[192,384]{1,0:T(8,128)(2,1)}, u32[]{:S(2)}, u32[]{:S(2)}) collective-permute-start(bf16[192,384]{1,0:T(8,128)(2,1)} %get-tuple-element.181), channel_id=1, source_target_pairs={{0,6},{1,7},{2,4},{3,5},{4,2},{5,3},{6,0},{7,1},{8,14},{9,15},{10,... | collective-permute-start | bytes 442376 | tf_op jit(solution)/shard_map/ppermute | solution.py:821
  129.5 17.8 %collective-permute-start.20 = (bf16[192,384]{1,0:T(8,128)(2,1)}, bf16[192,384]{1,0:T(8,128)(2,1)}, u32[]{:S(2)}, u32[]{:S(2)}) collective-permute-start(bf16[192,384]{1,0:T(8,128)(2,1)} %get-tuple-element.182), channel_id=1, source_target_pairs={{0,7},{1,6},{2,5},{3,4},{4,3},{5,2},{6,1},{7,0},{8,15},{9,14},{10,... | collective-permute-start | bytes 442376 | tf_op jit(solution)/shard_map/ppermute | solution.py:821
  129.7 32.4 %collective-permute-start.14 = (bf16[192,384]{1,0:T(8,128)(2,1)}, bf16[192,384]{1,0:T(8,128)(2,1)S(1)}, u32[]{:S(2)}, u32[]{:S(2)}) collective-permute-start(bf16[192,384]{1,0:T(8,128)(2,1)} %get-tuple-element.176), channel_id=1, source_target_pairs={{0,1},{1,0},{2,3},{3,2},{4,5},{5,4},{6,7},{7,6},{8,9},{9,8},{10,11... | collective-permute-start | bytes 442376 | tf_op jit(solution)/shard_map/ppermute | solution.py:821
  131.0 32.7 %collective-permute-start.15 = (bf16[192,384]{1,0:T(8,128)(2,1)}, bf16[192,384]{1,0:T(8,128)(2,1)S(1)}, u32[]{:S(2)}, u32[]{:S(2)}) collective-permute-start(bf16[192,384]{1,0:T(8,128)(2,1)} %get-tuple-element.177), channel_id=1, source_target_pairs={{0,2},{1,3},{2,0},{3,1},{4,6},{5,7},{6,4},{7,5},{8,10},{9,11},{10,... | collective-permute-start | bytes 442376 | tf_op jit(solution)/shard_map/ppermute | solution.py:821
  145.5 18.2 %collective-permute-start.16 = (bf16[192,384]{1,0:T(8,128)(2,1)}, bf16[192,384]{1,0:T(8,128)(2,1)S(1)}, u32[]{:S(2)}, u32[]{:S(2)}) collective-permute-start(bf16[192,384]{1,0:T(8,128)(2,1)} %get-tuple-element.178), channel_id=1, source_target_pairs={{0,3},{1,2},{2,1},{3,0},{4,7},{5,6},{6,5},{7,4},{8,11},{9,10},{10,... | collective-permute-start | bytes 442376 | tf_op jit(solution)/shard_map/ppermute | solution.py:821
  145.8 35.1 %collective-permute-start.21 = (bf16[192,384]{1,0:T(8,128)(2,1)}, bf16[192,384]{1,0:T(8,128)(2,1)S(1)}, u32[]{:S(2)}, u32[]{:S(2)}) collective-permute-start(bf16[192,384]{1,0:T(8,128)(2,1)} %get-tuple-element.184), channel_id=1, source_target_pairs={{0,1},{1,0},{2,3},{3,2},{4,5},{5,4},{6,7},{7,6},{8,9},{9,8},{10,11... | collective-permute-start | bytes 442376 | tf_op jit(solution)/shard_map/ppermute | solution.py:821
  147.3 24.0 %collective-permute-start.24 = (bf16[192,384]{1,0:T(8,128)(2,1)}, bf16[192,384]{1,0:T(8,128)(2,1)S(1)}, u32[]{:S(2)}, u32[]{:S(2)}) collective-permute-start(bf16[192,384]{1,0:T(8,128)(2,1)} %get-tuple-element.187), channel_id=1, source_target_pairs={{0,4},{1,5},{2,6},{3,7},{4,0},{5,1},{6,2},{7,3},{8,12},{9,13},{10,... | collective-permute-start | bytes 442376 | tf_op jit(solution)/shard_map/ppermute | solution.py:821
  162.2 15.4 %collective-permute-start.25 = (bf16[192,384]{1,0:T(8,128)(2,1)S(1)}, bf16[192,384]{1,0:T(8,128)(2,1)S(1)}, u32[]{:S(2)}, u32[]{:S(2)}) collective-permute-start(bf16[192,384]{1,0:T(8,128)(2,1)S(1)} %copy-done.49), channel_id=1, source_target_pairs={{0,5},{1,4},{2,7},{3,6},{4,1},{5,0},{6,3},{7,2},{8,13},{9,12},{10,... | collective-permute-start | bytes 442376 | tf_op jit(solution)/shard_map/ppermute | solution.py:821
  163.7 13.8 %collective-permute-start.26 = (bf16[192,384]{1,0:T(8,128)(2,1)S(1)}, bf16[192,384]{1,0:T(8,128)(2,1)S(1)}, u32[]{:S(2)}, u32[]{:S(2)}) collective-permute-start(bf16[192,384]{1,0:T(8,128)(2,1)S(1)} %copy-done.48), channel_id=1, source_target_pairs={{0,6},{1,7},{2,4},{3,5},{4,2},{5,3},{6,0},{7,1},{8,14},{9,15},{10,... | collective-permute-start | bytes 442376 | tf_op jit(solution)/shard_map/ppermute | solution.py:821
  163.8 13.8 %collective-permute-start.27 = (bf16[192,384]{1,0:T(8,128)(2,1)S(1)}, bf16[192,384]{1,0:T(8,128)(2,1)S(1)}, u32[]{:S(2)}, u32[]{:S(2)}) collective-permute-start(bf16[192,384]{1,0:T(8,128)(2,1)S(1)} %copy-done.47), channel_id=1, source_target_pairs={{0,7},{1,6},{2,5},{3,4},{4,3},{5,2},{6,1},{7,0},{8,15},{9,14},{10,... | collective-permute-start | bytes 442376 | tf_op jit(solution)/shard_map/ppermute | solution.py:821
  193.1 60.3 %collective-permute-start.28 = (bf16[384,1536]{1,0:T(8,128)(2,1)S(1)}, bf16[384,1536]{1,0:T(8,128)(2,1)S(1)}, u32[]{:S(2)}, u32[]{:S(2)}) collective-permute-start(bf16[384,1536]{1,0:T(8,128)(2,1)S(1)} %get-tuple-element.198), channel_id=1, source_target_pairs={{0,8},{8,0},{16,24},{24,16},{1,9},{9,1},{17,25},{25,17},{2,10},{10... | collective-permute-start | bytes 3538952 | tf_op jit(solution)/shard_map/ppermute | solution.py:765
  195.0 22.2 %collective-permute-start.39 = (bf16[192,384]{1,0:T(8,128)(2,1)S(1)}, bf16[192,384]{1,0:T(8,128)(2,1)S(1)}, u32[]{:S(2)}, u32[]{:S(2)}) collective-permute-start(bf16[192,384]{1,0:T(8,128)(2,1)S(1)} %get-tuple-element.214), channel_id=1, source_target_pairs={{0,4},{1,5},{2,6},{3,7},{4,0},{5,1},{6,2},{7,3},{8,12},{9,13},{10,... | collective-permute-start | bytes 442376 | tf_op jit(solution)/shard_map/ppermute | solution.py:821
  200.4 20.6 %collective-permute-start.40 = (bf16[192,384]{1,0:T(8,128)(2,1)S(1)}, bf16[192,384]{1,0:T(8,128)(2,1)S(1)}, u32[]{:S(2)}, u32[]{:S(2)}) collective-permute-start(bf16[192,384]{1,0:T(8,128)(2,1)S(1)} %get-tuple-element.215), channel_id=1, source_target_pairs={{0,5},{1,4},{2,7},{3,6},{4,1},{5,0},{6,3},{7,2},{8,13},{9,12},{10,... | collective-permute-start | bytes 442376 | tf_op jit(solution)/shard_map/ppermute | solution.py:821
  201.1 19.9 %collective-permute-start.41 = (bf16[192,384]{1,0:T(8,128)(2,1)S(1)}, bf16[192,384]{1,0:T(8,128)(2,1)S(1)}, u32[]{:S(2)}, u32[]{:S(2)}) collective-permute-start(bf16[192,384]{1,0:T(8,128)(2,1)S(1)} %get-tuple-element.216), channel_id=1, source_target_pairs={{0,6},{1,7},{2,4},{3,5},{4,2},{5,3},{6,0},{7,1},{8,14},{9,15},{10,... | collective-permute-start | bytes 442376 | tf_op jit(solution)/shard_map/ppermute | solution.py:821
  203.3 24.8 %collective-permute-start.42 = (bf16[192,384]{1,0:T(8,128)(2,1)S(1)}, bf16[192,384]{1,0:T(8,128)(2,1)S(1)}, u32[]{:S(2)}, u32[]{:S(2)}) collective-permute-start(bf16[192,384]{1,0:T(8,128)(2,1)S(1)} %get-tuple-element.217), channel_id=1, source_target_pairs={{0,7},{1,6},{2,5},{3,4},{4,3},{5,2},{6,1},{7,0},{8,15},{9,14},{10,... | collective-permute-start | bytes 442376 | tf_op jit(solution)/shard_map/ppermute | solution.py:821
  217.2 25.3 %collective-permute-start.32 = (bf16[192,384]{1,0:T(8,128)(2,1)S(1)}, bf16[192,384]{1,0:T(8,128)(2,1)S(1)}, u32[]{:S(2)}, u32[]{:S(2)}) collective-permute-start(bf16[192,384]{1,0:T(8,128)(2,1)S(1)} %get-tuple-element.206), channel_id=1, source_target_pairs={{0,4},{1,5},{2,6},{3,7},{4,0},{5,1},{6,2},{7,3},{8,12},{9,13},{10,... | collective-permute-start | bytes 442376 | tf_op jit(solution)/shard_map/ppermute | solution.py:821
  221.0 25.3 %collective-permute-start.33 = (bf16[192,384]{1,0:T(8,128)(2,1)S(1)}, bf16[192,384]{1,0:T(8,128)(2,1)S(1)}, u32[]{:S(2)}, u32[]{:S(2)}) collective-permute-start(bf16[192,384]{1,0:T(8,128)(2,1)S(1)} %get-tuple-element.207), channel_id=1, source_target_pairs={{0,5},{1,4},{2,7},{3,6},{4,1},{5,0},{6,3},{7,2},{8,13},{9,12},{10,... | collective-permute-start | bytes 442376 | tf_op jit(solution)/shard_map/ppermute | solution.py:821
  221.1 25.3 %collective-permute-start.34 = (bf16[192,384]{1,0:T(8,128)(2,1)S(1)}, bf16[192,384]{1,0:T(8,128)(2,1)S(1)}, u32[]{:S(2)}, u32[]{:S(2)}) collective-permute-start(bf16[192,384]{1,0:T(8,128)(2,1)S(1)} %get-tuple-element.208), channel_id=1, source_target_pairs={{0,6},{1,7},{2,4},{3,5},{4,2},{5,3},{6,0},{7,1},{8,14},{9,15},{10,... | collective-permute-start | bytes 442376 | tf_op jit(solution)/shard_map/ppermute | solution.py:821
  228.0 21.7 %collective-permute-start.35 = (bf16[192,384]{1,0:T(8,128)(2,1)S(1)}, bf16[192,384]{1,0:T(8,128)(2,1)S(1)}, u32[]{:S(2)}, u32[]{:S(2)}) collective-permute-start(bf16[192,384]{1,0:T(8,128)(2,1)S(1)} %get-tuple-element.209), channel_id=1, source_target_pairs={{0,7},{1,6},{2,5},{3,4},{4,3},{5,2},{6,1},{7,0},{8,15},{9,14},{10,... | collective-permute-start | bytes 442376 | tf_op jit(solution)/shard_map/ppermute | solution.py:821
  255.1 43.9 %collective-permute-start.50 = (bf16[192,1536]{1,0:T(8,128)(2,1)S(1)}, bf16[192,1536]{1,0:T(8,128)(2,1)S(1)}, u32[]{:S(2)}, u32[]{:S(2)}) collective-permute-start(bf16[192,1536]{1,0:T(8,128)(2,1)S(1)} %get-tuple-element.200), channel_id=1, source_target_pairs={{0,16},{8,24},{16,0},{24,8},{1,17},{9,25},{17,1},{25,9},{2,18},{10... | collective-permute-start | bytes 1769480 | tf_op jit(solution)/shard_map/ppermute | solution.py:765
  294.4 20.7 %collective-permute-start.52 = (bf16[192,1536]{1,0:T(8,128)(2,1)}, bf16[192,1536]{1,0:T(8,128)(2,1)S(1)}, u32[]{:S(2)}, u32[]{:S(2)}) collective-permute-start(bf16[192,1536]{1,0:T(8,128)(2,1)} %get-tuple-element.247), channel_id=1, source_target_pairs={{0,8},{8,0},{16,24},{24,16},{1,9},{9,1},{17,25},{25,17},{2,10},{10... | collective-permute-start | bytes 1769480 | tf_op jit(solution)/shard_map/ppermute | solution.py:765
  298.1 13.2 %collective-permute-start.45 = (bf16[192,384]{1,0:T(8,128)(2,1)}, bf16[192,384]{1,0:T(8,128)(2,1)S(1)}, u32[]{:S(2)}, u32[]{:S(2)}) collective-permute-start(bf16[192,384]{1,0:T(8,128)(2,1)} %get-tuple-element.231), channel_id=1, source_target_pairs={{0,3},{1,2},{2,1},{3,0},{4,7},{5,6},{6,5},{7,4},{8,11},{9,10},{10,... | collective-permute-start | bytes 442376 | tf_op jit(solution)/shard_map/ppermute | solution.py:821
  299.0 19.9 %collective-permute-start.46 = (bf16[192,384]{1,0:T(8,128)(2,1)}, bf16[192,384]{1,0:T(8,128)(2,1)S(1)}, u32[]{:S(2)}, u32[]{:S(2)}) collective-permute-start(bf16[192,384]{1,0:T(8,128)(2,1)} %get-tuple-element.232), channel_id=1, source_target_pairs={{0,4},{1,5},{2,6},{3,7},{4,0},{5,1},{6,2},{7,3},{8,12},{9,13},{10,... | collective-permute-start | bytes 442376 | tf_op jit(solution)/shard_map/ppermute | solution.py:821
  302.0 16.9 %collective-permute-start.47 = (bf16[192,384]{1,0:T(8,128)(2,1)S(1)}, bf16[192,384]{1,0:T(8,128)(2,1)S(1)}, u32[]{:S(2)}, u32[]{:S(2)}) collective-permute-start(bf16[192,384]{1,0:T(8,128)(2,1)S(1)} %copy-done.59), channel_id=1, source_target_pairs={{0,5},{1,4},{2,7},{3,6},{4,1},{5,0},{6,3},{7,2},{8,13},{9,12},{10,... | collective-permute-start | bytes 442376 | tf_op jit(solution)/shard_map/ppermute | solution.py:821
  304.3 14.6 %collective-permute-start.48 = (bf16[192,384]{1,0:T(8,128)(2,1)S(1)}, bf16[192,384]{1,0:T(8,128)(2,1)S(1)}, u32[]{:S(2)}, u32[]{:S(2)}) collective-permute-start(bf16[192,384]{1,0:T(8,128)(2,1)S(1)} %copy-done.57), channel_id=1, source_target_pairs={{0,6},{1,7},{2,4},{3,5},{4,2},{5,3},{6,0},{7,1},{8,14},{9,15},{10,... | collective-permute-start | bytes 442376 | tf_op jit(solution)/shard_map/ppermute | solution.py:821
  330.6 26.0 %collective-permute-start.53 = (bf16[384,1536]{1,0:T(8,128)(2,1)S(1)}, bf16[384,1536]{1,0:T(8,128)(2,1)S(1)}, u32[]{:S(2)}, u32[]{:S(2)}) collective-permute-start(bf16[384,1536]{1,0:T(8,128)(2,1)S(1)} %get-tuple-element.253), channel_id=1, source_target_pairs={{0,8},{8,0},{16,24},{24,16},{1,9},{9,1},{17,25},{25,17},{2,10},{10... | collective-permute-start | bytes 3538952 | tf_op jit(solution)/shard_map/ppermute | solution.py:765
  351.5 33.2 %collective-permute-start.59 = (bf16[192,1536]{1,0:T(8,128)(2,1)S(1)}, bf16[192,1536]{1,0:T(8,128)(2,1)S(1)}, u32[]{:S(2)}, u32[]{:S(2)}) collective-permute-start(bf16[192,1536]{1,0:T(8,128)(2,1)S(1)} %get-tuple-element.239.keep_ref.refs_0_), channel_id=1, source_target_pairs={{0,16},{8,24},{16,0},{24,8},{1,17},{9,25},{17,1},{25,9},{2,18},{10... | collective-permute-start | bytes 1769480 | tf_op jit(solution)/shard_map/ppermute | solution.py:765
  354.1 13.5 %collective-permute-start.63 = (bf16[48,1536]{1,0:T(8,128)(2,1)S(1)}, bf16[48,1536]{1,0:T(8,128)(2,1)S(1)}, u32[]{:S(2)}, u32[]{:S(2)}) collective-permute-start(bf16[48,1536]{1,0:T(8,128)(2,1)S(1)} %add_rows.30.keep_ref), channel_id=1, source_target_pairs={{0,4},{1,5},{2,6},{3,7},{4,0},{5,1},{6,2},{7,3},{8,12},{9,13},{10,... | collective-permute-start | bytes 442376 | tf_op jit(solution)/shard_map/ppermute | solution.py:765
  356.9 30.2 %collective-permute-start.54 = (bf16[192,1536]{1,0:T(8,128)(2,1)S(1)}, bf16[192,1536]{1,0:T(8,128)(2,1)S(1)}, u32[]{:S(2)}, u32[]{:S(2)}) collective-permute-start(bf16[192,1536]{1,0:T(8,128)(2,1)S(1)} %get-tuple-element.255), channel_id=1, source_target_pairs={{0,16},{8,24},{16,0},{24,8},{1,17},{9,25},{17,1},{25,9},{2,18},{10... | collective-permute-start | bytes 1769480 | tf_op jit(solution)/shard_map/ppermute | solution.py:765
  368.9 16.7 %collective-permute-start.58 = (bf16[96,1536]{1,0:T(8,128)(2,1)S(1)}, bf16[96,1536]{1,0:T(8,128)(2,1)S(1)}, u32[]{:S(2)}, u32[]{:S(2)}) collective-permute-start(bf16[96,1536]{1,0:T(8,128)(2,1)S(1)} %join_rows.8.first_ref), channel_id=1, source_target_pairs={{0,1},{1,0},{2,3},{3,2},{4,5},{5,4},{6,7},{7,6},{8,9},{9,8},{10,11... | collective-permute-start | bytes 884744 | tf_op jit(solution)/shard_map/ppermute | solution.py:765
  372.0 10.7 %collective-permute-start.65 = (bf16[192,384]{1,0:T(8,128)(2,1)S(1)}, bf16[192,384]{1,0:T(8,128)(2,1)S(1)}, u32[]{:S(2)}, u32[]{:S(2)}) collective-permute-start(bf16[192,384]{1,0:T(8,128)(2,1)S(1)} %get-tuple-element.263), channel_id=1, source_target_pairs={{0,2},{1,3},{2,0},{3,1},{4,6},{5,7},{6,4},{7,5},{8,10},{9,11},{10,... | collective-permute-start | bytes 442376 | tf_op jit(solution)/shard_map/ppermute | solution.py:821
  384.8 19.7 %collective-permute-start.68 = (bf16[192,384]{1,0:T(8,128)(2,1)S(1)}, bf16[192,384]{1,0:T(8,128)(2,1)S(1)}, u32[]{:S(2)}, u32[]{:S(2)}) collective-permute-start(bf16[192,384]{1,0:T(8,128)(2,1)S(1)} %get-tuple-element.266), channel_id=1, source_target_pairs={{0,5},{1,4},{2,7},{3,6},{4,1},{5,0},{6,3},{7,2},{8,13},{9,12},{10,... | collective-permute-start | bytes 442376 | tf_op jit(solution)/shard_map/ppermute | solution.py:821
  385.6 18.9 %collective-permute-start.69 = (bf16[192,384]{1,0:T(8,128)(2,1)S(1)}, bf16[192,384]{1,0:T(8,128)(2,1)S(1)}, u32[]{:S(2)}, u32[]{:S(2)}) collective-permute-start(bf16[192,384]{1,0:T(8,128)(2,1)S(1)} %get-tuple-element.267), channel_id=1, source_target_pairs={{0,6},{1,7},{2,4},{3,5},{4,2},{5,3},{6,0},{7,1},{8,14},{9,15},{10,... | collective-permute-start | bytes 442376 | tf_op jit(solution)/shard_map/ppermute | solution.py:821
  387.1 17.3 %collective-permute-start.70 = (bf16[192,384]{1,0:T(8,128)(2,1)S(1)}, bf16[192,384]{1,0:T(8,128)(2,1)S(1)}, u32[]{:S(2)}, u32[]{:S(2)}) collective-permute-start(bf16[192,384]{1,0:T(8,128)(2,1)S(1)} %get-tuple-element.268), channel_id=1, source_target_pairs={{0,7},{1,6},{2,5},{3,4},{4,3},{5,2},{6,1},{7,0},{8,15},{9,14},{10,... | collective-permute-start | bytes 442376 | tf_op jit(solution)/shard_map/ppermute | solution.py:821
  390.9 42.9 %collective-permute-start.85 = (bf16[96,1536]{1,0:T(8,128)(2,1)S(1)}, bf16[96,1536]{1,0:T(8,128)(2,1)S(1)}, u32[]{:S(2)}, u32[]{:S(2)}) collective-permute-start(bf16[96,1536]{1,0:T(8,128)(2,1)S(1)} %join_rows.12.first_ref), channel_id=1, source_target_pairs={{0,16},{8,24},{16,0},{24,8},{1,17},{9,25},{17,1},{25,9},{2,18},{10... | collective-permute-start | bytes 884744 | tf_op jit(solution)/shard_map/ppermute | solution.py:765
  429.9 20.5 %collective-permute-start.76 = (bf16[192,1536]{1,0:T(8,128)(2,1)}, bf16[192,1536]{1,0:T(8,128)(2,1)S(1)}, u32[]{:S(2)}, u32[]{:S(2)}) collective-permute-start(bf16[192,1536]{1,0:T(8,128)(2,1)} %get-tuple-element.281), channel_id=1, source_target_pairs={{0,8},{8,0},{16,24},{24,16},{1,9},{9,1},{17,25},{25,17},{2,10},{10... | collective-permute-start | bytes 1769480 | tf_op jit(solution)/shard_map/ppermute | solution.py:765
  433.8 35.7 %collective-permute-start.100 = (bf16[192,1536]{1,0:T(8,128)(2,1)}, bf16[192,1536]{1,0:T(8,128)(2,1)}, u32[]{:S(2)}, u32[]{:S(2)}) collective-permute-start(bf16[192,1536]{1,0:T(8,128)(2,1)} %join_rows.9.refs_4_), channel_id=1, source_target_pairs={{0,16},{8,24},{16,0},{24,8},{1,17},{9,25},{17,1},{25,9},{2,18},{10... | collective-permute-start | bytes 1769480 | tf_op jit(solution)/shard_map/ppermute | solution.py:765
  433.8 39.2 %collective-permute-start.86 = (bf16[192,1536]{1,0:T(8,128)(2,1)S(1)}, bf16[192,1536]{1,0:T(8,128)(2,1)S(1)}, u32[]{:S(2)}, u32[]{:S(2)}) collective-permute-start(bf16[192,1536]{1,0:T(8,128)(2,1)S(1)} %join_rows.13.refs_0_), channel_id=1, source_target_pairs={{0,8},{8,0},{16,24},{24,16},{1,9},{9,1},{17,25},{25,17},{2,10},{10... | collective-permute-start | bytes 1769480 | tf_op jit(solution)/shard_map/ppermute | solution.py:765
  463.8 10.9 %collective-permute-start.79 = (bf16[48,1536]{1,0:T(8,128)(2,1)S(1)}, bf16[48,1536]{1,0:T(8,128)(2,1)S(1)}, u32[]{:S(2)}, u32[]{:S(2)}) collective-permute-start(bf16[48,1536]{1,0:T(8,128)(2,1)S(1)} %add_rows.34.keep_ref), channel_id=1, source_target_pairs={{0,2},{1,3},{2,0},{3,1},{4,6},{5,7},{6,4},{7,5},{8,10},{9,11},{10,... | collective-permute-start | bytes 442376 | tf_op jit(solution)/shard_map/ppermute | solution.py:765
  469.5 16.7 %collective-permute-start.98 = (bf16[192,1536]{1,0:T(8,128)(2,1)S(1)}, bf16[192,1536]{1,0:T(8,128)(2,1)S(1)}, u32[]{:S(2)}, u32[]{:S(2)}) collective-permute-start(bf16[192,1536]{1,0:T(8,128)(2,1)S(1)} %get-tuple-element.239.keep_ref.refs_0_), channel_id=1, source_target_pairs={{0,8},{8,0},{16,24},{24,16},{1,9},{9,1},{17,25},{25,17},{2,10},{10... | collective-permute-start | bytes 1769480 | tf_op jit(solution)/shard_map/ppermute | solution.py:765
  473.1 14.3 %collective-permute-start.99 = (bf16[192,1536]{1,0:T(8,128)(2,1)S(1)}, bf16[192,1536]{1,0:T(8,128)(2,1)S(1)}, u32[]{:S(2)}, u32[]{:S(2)}) collective-permute-start(bf16[192,1536]{1,0:T(8,128)(2,1)S(1)} %collective-permute-done.59.refs_1_), channel_id=1, source_target_pairs={{0,8},{8,0},{16,24},{24,16},{1,9},{9,1},{17,25},{25,17},{2,10},{10... | collective-permute-start | bytes 1769480 | tf_op jit(solution)/shard_map/ppermute | solution.py:765
  473.1 14.3 %collective-permute-start.101 = (bf16[192,1536]{1,0:T(8,128)(2,1)}, bf16[192,1536]{1,0:T(8,128)(2,1)S(1)}, u32[]{:S(2)}, u32[]{:S(2)}) collective-permute-start(bf16[192,1536]{1,0:T(8,128)(2,1)} %join_rows.9.refs_4_), channel_id=1, source_target_pairs={{0,8},{8,0},{16,24},{24,16},{1,9},{9,1},{17,25},{25,17},{2,10},{10... | collective-permute-start | bytes 1769480 | tf_op jit(solution)/shard_map/ppermute | solution.py:765
  474.7 13.1 %collective-permute-start.102 = (bf16[192,1536]{1,0:T(8,128)(2,1)}, bf16[192,1536]{1,0:T(8,128)(2,1)S(1)}, u32[]{:S(2)}, u32[]{:S(2)}) collective-permute-start(bf16[192,1536]{1,0:T(8,128)(2,1)} %collective-permute-done.100.refs_5_), channel_id=1, source_target_pairs={{0,8},{8,0},{16,24},{24,16},{1,9},{9,1},{17,25},{25,17},{2,10},{10... | collective-permute-start | bytes 1769480 | tf_op jit(solution)/shard_map/ppermute | solution.py:765
  481.3 45.8 %collective-permute-start.88 = (bf16[192,1536]{1,0:T(8,128)(2,1)S(1)}, bf16[192,1536]{1,0:T(8,128)(2,1)S(1)}, u32[]{:S(2)}, u32[]{:S(2)}) collective-permute-start(bf16[192,1536]{1,0:T(8,128)(2,1)S(1)} %get-tuple-element.256.keep_ref.refs_0_), channel_id=1, source_target_pairs={{0,8},{8,0},{16,24},{24,16},{1,9},{9,1},{17,25},{25,17},{2,10},{10... | collective-permute-start | bytes 1769480 | tf_op jit(solution)/shard_map/ppermute | solution.py:765
  486.2 15.0 %collective-permute-start.87 = (bf16[192,1536]{1,0:T(8,128)(2,1)S(1)}, bf16[192,1536]{1,0:T(8,128)(2,1)S(1)}, u32[]{:S(2)}, u32[]{:S(2)}) collective-permute-start(bf16[192,1536]{1,0:T(8,128)(2,1)S(1)} %get-tuple-element.256.keep_ref.refs_0_), channel_id=1, source_target_pairs={{0,16},{8,24},{16,0},{24,8},{1,17},{9,25},{17,1},{25,9},{2,18},{10... | collective-permute-start | bytes 1769480 | tf_op jit(solution)/shard_map/ppermute | solution.py:765
  487.4 26.4 %collective-permute-start.95 = (bf16[192,1536]{1,0:T(8,128)(2,1)S(1)}, bf16[192,1536]{1,0:T(8,128)(2,1)S(1)}, u32[]{:S(2)}, u32[]{:S(2)}) collective-permute-start(bf16[192,1536]{1,0:T(8,128)(2,1)S(1)} %join_rows.15.refs_4_), channel_id=1, source_target_pairs={{0,16},{8,24},{16,0},{24,8},{1,17},{9,25},{17,1},{25,9},{2,18},{10... | collective-permute-start | bytes 1769480 | tf_op jit(solution)/shard_map/ppermute | solution.py:765
  494.9 25.3 %collective-permute-start.82 = (bf16[96,1536]{1,0:T(8,128)(2,1)S(1)}, bf16[96,1536]{1,0:T(8,128)(2,1)S(1)}, u32[]{:S(2)}, u32[]{:S(2)}) collective-permute-start(bf16[96,1536]{1,0:T(8,128)(2,1)S(1)} %join_rows.10.first_ref), channel_id=1, source_target_pairs={{0,16},{8,24},{16,0},{24,8},{1,17},{9,25},{17,1},{25,9},{2,18},{10... | collective-permute-start | bytes 884744 | tf_op jit(solution)/shard_map/ppermute | solution.py:765
  501.2 25.9 %collective-permute-start.89 = (bf16[192,1536]{1,0:T(8,128)(2,1)S(1)}, bf16[192,1536]{1,0:T(8,128)(2,1)S(1)}, u32[]{:S(2)}, u32[]{:S(2)}) collective-permute-start(bf16[192,1536]{1,0:T(8,128)(2,1)S(1)} %collective-permute-done.87.refs_1_), channel_id=1, source_target_pairs={{0,8},{8,0},{16,24},{24,16},{1,9},{9,1},{17,25},{25,17},{2,10},{10... | collective-permute-start | bytes 1769480 | tf_op jit(solution)/shard_map/ppermute | solution.py:765
  502.4 24.7 %collective-permute-start.96 = (bf16[192,1536]{1,0:T(8,128)(2,1)S(1)}, bf16[192,1536]{1,0:T(8,128)(2,1)}, u32[]{:S(2)}, u32[]{:S(2)}) collective-permute-start(bf16[192,1536]{1,0:T(8,128)(2,1)S(1)} %join_rows.15.refs_4_), channel_id=1, source_target_pairs={{0,8},{8,0},{16,24},{24,16},{1,9},{9,1},{17,25},{25,17},{2,10},{10... | collective-permute-start | bytes 1769480 | tf_op jit(solution)/shard_map/ppermute | solution.py:765
  513.8 13.3 %collective-permute-start.97 = (bf16[192,1536]{1,0:T(8,128)(2,1)S(1)}, bf16[192,1536]{1,0:T(8,128)(2,1)}, u32[]{:S(2)}, u32[]{:S(2)}) collective-permute-start(bf16[192,1536]{1,0:T(8,128)(2,1)S(1)} %collective-permute-done.95.refs_5_), channel_id=1, source_target_pairs={{0,8},{8,0},{16,24},{24,16},{1,9},{9,1},{17,25},{25,17},{2,10},{10... | collective-permute-start | bytes 1769480 | tf_op jit(solution)/shard_map/ppermute | solution.py:765
  521.0 12.2 %collective-permute-start.83 = (bf16[192,1536]{1,0:T(8,128)(2,1)}, bf16[192,1536]{1,0:T(8,128)(2,1)}, u32[]{:S(2)}, u32[]{:S(2)}) collective-permute-start(bf16[192,1536]{1,0:T(8,128)(2,1)} %join_rows.11.refs_0_), channel_id=1, source_target_pairs={{0,8},{8,0},{16,24},{24,16},{1,9},{9,1},{17,25},{25,17},{2,10},{10... | collective-permute-start | bytes 1769480 | tf_op jit(solution)/shard_map/ppermute | solution.py:765
  (118 other events, 1096.1 us)

commit v3 on v2

--- a/solution.py
+++ b/solution.py
@@ -33,13 +33,12 @@
 GROUPS = HEADS // GROUP
 GW = GROUP * LPAD
 FCHUNK = 384
-JOIN = 2
+SOURCES = 2
 FTILE = 512
 EXPERT_VMEM = 32 * 1024 * 1024
 BLOCK = 48
 PAIRS_AT_ONCE = 2
-SEND_ORDER = (4, 5, 6, 7, 2, 3, 1)
-PART = 4
+TEAM = 4
 STEP_IMAGES = 3
 
 F32 = jnp.float32
@@ -148,22 +147,11 @@
     return total
 
 
-def join_chunks(rows_ref, chunks):
-    parts = rows_ref.shape[0]
-    for i, chunk in enumerate(chunks):
-        rows_ref[i % parts, (i // parts) * ROWS : (i // parts + 1) * ROWS] = chunk[...]
-
-
-def send_rows(out_refs, target_all, rows):
+def send_rows(out_ref, target_all, rows):
     step = SLOTS // 4
     for c in range(4):
         slot = lax.broadcasted_iota(jnp.int32, (step, rows.shape[0]), 0) + c * step
-        block = mm(one_hot(slot == target_all), rows).astype(BF16)
-        for group, refs in enumerate(out_refs):
-            for k in range(step // ROWS):
-                refs[c * (step // ROWS) + k][...] = block[
-                    k * ROWS : (k + 1) * ROWS, group * D : (group + 1) * D
-                ]
+        out_ref[c * step : (c + 1) * step] = mm(one_hot(slot == target_all), rows).astype(BF16)
 
 
 def gelu_parts(u):
@@ -178,7 +166,7 @@
     )
 
 
-def routing_kernel(flip_ref, routes_ref, target_ref):
+def routing_kernel(paired, half_ref, routes_ref, target_ref):
     before = one_hot(
         lax.broadcasted_iota(jnp.int32, (TPAD, TPAD), 0)
         <= lax.broadcasted_iota(jnp.int32, (TPAD, TPAD), 1)
@@ -193,21 +181,22 @@
             carry = counts[:, TPAD - 1 : TPAD]
             slot = jnp.sum(chosen * counts, axis=0, keepdims=True).astype(jnp.int32) - 1
             kept = (slot >= 0) & (slot < CAP)
-            target_ref[depth, i : i + 1, :] = jnp.where(
-                kept, jnp.bitwise_xor(row, flip_ref[0]) * ROWS + slot, -1
-            )
-
-
-def run_routing(routes, flip):
+            place = row
+            if paired:
+                place = (row % TEAM) * 2 + jnp.bitwise_xor(row // TEAM, half_ref[0])
+            target_ref[depth, i : i + 1, :] = jnp.where(kept, place * ROWS + slot, -1)
+
+
+def run_routing(routes, half, paired):
     return pl.pallas_call(
-        routing_kernel,
+        partial(routing_kernel, paired),
         in_specs=[
             pl.BlockSpec(memory_space=pltpu.SMEM),
             pl.BlockSpec(memory_space=pltpu.VMEM),
         ],
         out_shape=jax.ShapeDtypeStruct(routes.shape, jnp.int32),
         name="routing",
-    )(flip, routes)
+    )(half, routes)
 
 
 def group_cols(part, g):
@@ -249,14 +238,13 @@
     return probs
 
 
-def forward_kernel(depth, images, chunks, *refs):
+def forward_kernel(depth, images, *refs):
     last = depth == LAYERS - 1
     refs = list(refs)
     take = lambda: refs.pop(0)
     x_ref = take()
     if depth:
-        back = [take() for _ in range(chunks)]
-        gate_in_ref, target_in_ref = take(), take()
+        back_ref, gate_in_ref, target_in_ref = take(), take(), take()
     if last:
         cot_ref = take()
     (route_ref, target_ref, g1_ref, s1_ref, g2_ref, s2_ref, attend_ref, out_w_ref) = refs[:8]
@@ -266,18 +254,13 @@
     refs = refs[7:]
     if depth:
         x_out_ref, picked_ref = take(), take()
-    outgoing = [[take() for _ in range(EXPERTS)] for _ in range(2 if last else 1)]
-    rows_ref = take()
-    if depth:
-        back_ref = take()
+    out_ref, rows_ref = take(), take()
 
     step = pl.program_id(0)
 
     @pl.when(step == 0)
     def _():
         rows_ref[...] = jnp.zeros_like(rows_ref)
-        if depth:
-            join_chunks(back_ref, back)
 
     some = range(x_ref.shape[0])
     xs = []
@@ -334,7 +317,7 @@
     @pl.when(step == pl.num_programs(0) - 1)
     def _():
         rows = rows_ref[...].reshape(images * TPAD, rows_ref.shape[2])
-        send_rows(outgoing, target_ref[...], rows)
+        send_rows(out_ref, target_ref[...], rows)
 
 
 def whole(shape):
@@ -361,9 +344,8 @@
     args, specs = [x], [by_image(x.shape)]
     if depth:
         back, gate_in, target_in, picked_type = earlier
-        args += list(back) + [gate_in, target_in]
-        specs += [whole(chunk.shape) for chunk in back]
-        specs += [by_image(gate_in.shape), by_image(target_in.shape)]
+        args += [back, gate_in, target_in]
+        specs += [whole(back.shape), by_image(gate_in.shape), by_image(target_in.shape)]
     if last:
         args.append(cotangent)
         specs.append(by_image(cotangent.shape))
@@ -391,14 +373,12 @@
     if depth:
         outs += [((images, HW, D), F32), ((images, HW, D), picked_type)]
         out_specs += [by_image((images, HW, D))] * 2
-    count = EXPERTS * (2 if last else 1)
-    outs += [((ROWS, D), BF16)] * count
-    out_specs += [whole((ROWS, D))] * count
-    scratch = [pltpu.VMEM((images, TPAD, 2 * D if last else D), BF16)]
-    if depth:
-        scratch.append(pltpu.VMEM((len(back) // EXPERTS, SLOTS, D), BF16))
+    sent = 2 * D if last else D
+    outs.append(((SLOTS, sent), BF16))
+    out_specs.append(whole((SLOTS, sent)))
+    scratch = [pltpu.VMEM((images, TPAD, sent), BF16)]
     results = pl.pallas_call(
-        partial(forward_kernel, depth, images, len(back) if depth else 0),
+        partial(forward_kernel, depth, images),
         grid=(images // images_of(images),),
         in_specs=specs,
         out_specs=out_specs,
@@ -408,109 +388,142 @@
         cost_estimate=cost(24 if last else 18),
         name="forward_%d" % depth,
     )(*args)
-    return results[:-count], [results[-count:][i : i + EXPERTS] for i in range(0, count, EXPERTS)]
-
-
-def expert_forward_kernel(chunks, *refs):
-    sources, refs = refs[:chunks], refs[chunks:]
-    up_ref, down_ref, refs = refs[0], refs[1], refs[2:]
-    returns, refs = refs[:chunks], refs[chunks:]
-    hidden_ref, slope_ref = refs
-    width = up_ref.shape[1]
+    return results[:-1], results[-1]
+
+
+def joined(ref, columns=slice(None)):
+    return jnp.concatenate([ref[s, 0, :, columns] for s in range(ref.shape[0])], axis=0)
+
+
+def spread(ref, value, columns=slice(None)):
+    for s in range(ref.shape[0]):
+        ref[s, 0, :, columns] = value[s * ROWS : (s + 1) * ROWS]
+
+
+def hidden_tiles(width):
     tile = FTILE if width % FTILE == 0 else FCHUNK
-    tiles = [(k, f) for k in range(0, chunks, JOIN) for f in range(0, width, tile)]
-    joined = [
-        jnp.concatenate([r[...] for r in sources[k : k + JOIN]], axis=0)
-        for k in range(0, chunks, JOIN)
-    ]
-    first = lambda k, f: mm(joined[k // JOIN], up_ref[:, f : f + tile])
-    ready = first(*tiles[0])
-    for at, (k, f) in enumerate(tiles):
+    return [slice(f, f + tile) for f in range(0, width, tile)]
+
+
+def expert_forward_kernel(n_ref, up_ref, down_ref, y_ref, hidden_ref):
+    n = joined(n_ref)
+    tiles = hidden_tiles(up_ref.shape[2])
+    ready = mm(n, up_ref[0, :, tiles[0]])
+    for at, tile in enumerate(tiles):
         u = ready
         if at + 1 < len(tiles):
-            ready = first(*tiles[at + 1])
-        rows = slice(k * ROWS, (k + JOIN) * ROWS)
+            ready = mm(n, up_ref[0, :, tiles[at + 1]])
+        hidden_ref[:, tile] = gelu_parts(u)[0].astype(BF16)
+    spread(y_ref, mm(hidden_ref[...], down_ref[0]).astype(BF16))
+
+
+def by_expert(shape):
+    return pl.BlockSpec((1,) + shape[1:], lambda k, i: (k,) + (0,) * (len(shape) - 1))
+
+
+def by_sources(array):
+    return pl.BlockSpec((SOURCES, 1) + array.shape[2:], lambda k, i: (i, k, 0, 0))
+
+
+def run_expert_forward(arrived, up, down):
+    total, width = up.shape[0], up.shape[2]
+    return pl.pallas_call(
+        expert_forward_kernel,
+        grid=(total, arrived.shape[0] // SOURCES),
+        in_specs=[by_sources(arrived), by_expert(up.shape), by_expert(down.shape)],
+        out_specs=by_sources(arrived),
+        out_shape=jax.ShapeDtypeStruct(arrived.shape, BF16),
+        scratch_shapes=[pltpu.VMEM((SOURCES * ROWS, width), BF16)],
+        compiler_params=pltpu.CompilerParams(vmem_limit_bytes=VMEM_BYTES),
+        cost_estimate=cost(4 * total),
+        name="expert_forward",
+    )(arrived, up, down)
+
+
+def expert_both_kernel(joint, *refs):
+    n_ref, refs = refs[0], refs[1:]
+    if joint:
+        dy = joined(n_ref, slice(D, 2 * D))
+    else:
+        dy, refs = joined(refs[0]), refs[1:]
+    up_ref, down_ref, out_ref, hidden_ref, du_ref = refs
+    n = joined(n_ref, slice(0, D))
+    tiles = hidden_tiles(up_ref.shape[2])
+
+    def first(tile):
+        return mm(n, up_ref[0, :, tile]), mm(dy, down_ref[0, tile], NT)
+
+    ready = first(tiles[0])
+    for at, tile in enumerate(tiles):
+        u, dh = ready
+        if at + 1 < len(tiles):
+            ready = first(tiles[at + 1])
         value, slope = gelu_parts(u)
-        hidden_ref[rows, f : f + tile] = value.astype(BF16)
-        slope_ref[rows, f : f + tile] = slope.astype(BF16)
-        if f + tile >= width:
-            y = mm(hidden_ref[rows], down_ref[...]).astype(BF16)
-            for j in range(JOIN):
-                returns[k + j][...] = y[j * ROWS : (j + 1) * ROWS]
-
-
-def expert_inner_kernel(chunks, *refs):
-    sources, refs = refs[:chunks], refs[chunks:]
-    slope_ref, up_ref, down_ref, refs = refs[0], refs[1], refs[2], refs[3:]
-    returns, refs = refs[:chunks], refs[chunks:]
-    (du_ref,) = refs
-    width = up_ref.shape[1]
-    tile = FTILE if width % FTILE == 0 else FCHUNK
-    tiles = [(k, f) for k in range(chunks) for f in range(0, width, tile)]
-    first = lambda k, f: mm(sources[k][...], down_ref[f : f + tile], NT)
-    ready = first(*tiles[0])
-    for at, (k, f) in enumerate(tiles):
-        dh = ready
-        if at + 1 < len(tiles):
-            ready = first(*tiles[at + 1])
-        rows = slice(k * ROWS, (k + 1) * ROWS)
-        du_ref[rows, f : f + tile] = (dh * slope_ref[rows, f : f + tile].astype(F32)).astype(
-            BF16
-        )
-        if f + tile >= width:
-            returns[k][...] = mm(du_ref[rows], up_ref[...], NT).astype(BF16)
-
-
-def run_expert(kernel, name, sources, slopes, up, down, wides, time):
-    rows, width = ROWS * len(sources), up.shape[1]
-    results = pl.pallas_call(
-        partial(kernel, len(sources)),
-        out_shape=[jax.ShapeDtypeStruct((ROWS, D), BF16)] * len(sources)
-        + [jax.ShapeDtypeStruct((rows, width), BF16)] * wides,
-        compiler_params=pltpu.CompilerParams(vmem_limit_bytes=EXPERT_VMEM),
-        cost_estimate=cost(time),
-        name=name,
-    )(*sources, *slopes, up, down)
-    return results[: len(sources)], results[len(sources) :]
-
-
-def run_expert_forward(sources, up, down):
-    return run_expert(expert_forward_kernel, "expert_forward", sources, [], up, down, 2, 5.5)
-
-
-def run_expert_inner(sources, slope, up, down):
-    return run_expert(expert_inner_kernel, "expert_inner", sources, [slope], up, down, 1, 4)
-
-
-def expert_weights_kernel(chunks, parts, order, *refs):
+        hidden_ref[0, :, tile] = value.astype(BF16)
+        du_ref[0, :, tile] = (dh * slope).astype(BF16)
+    dn = mm(du_ref[0], up_ref[0], NT).astype(BF16)
+    if joint:
+        spread(out_ref, mm(hidden_ref[0], down_ref[0]).astype(BF16), slice(0, D))
+        spread(out_ref, dn, slice(D, 2 * D))
+    else:
+        spread(out_ref, dn)
+
+
+def run_expert_both(n, dy, up, down):
+    total, width, joint = up.shape[0], up.shape[2], dy is None
+    args = [n] if joint else [n, dy]
+    wide = jax.ShapeDtypeStruct((total, n.shape[0] * ROWS, width), BF16)
+    wide_spec = pl.BlockSpec((1, SOURCES * ROWS, width), lambda k, i: (k, i, 0))
+    return pl.pallas_call(
+        partial(expert_both_kernel, joint),
+        grid=(total, n.shape[0] // SOURCES),
+        in_specs=[by_sources(array) for array in args]
+        + [by_expert(up.shape), by_expert(down.shape)],
+        out_specs=[by_sources(n), wide_spec, wide_spec],
+        out_shape=[jax.ShapeDtypeStruct(n.shape, BF16), wide, wide],
+        compiler_params=pltpu.CompilerParams(vmem_limit_bytes=VMEM_BYTES),
+        cost_estimate=cost(6 * total),
+        name="expert_both",
+    )(*args, up, down)
+
+
+def expert_weights_kernel(joint, order, *refs):
     if order:
         order_ref, refs = refs[0], refs[1:]
-    ns, refs = refs[:chunks], refs[chunks:]
-    dys, refs = refs[:chunks], refs[chunks:]
-    hiddens, refs = refs[:parts], refs[parts:]
-    dus, refs = refs[:parts], refs[parts:]
+    n_ref, refs = refs[0], refs[1:]
+    dy_ref, dy_columns = n_ref, slice(D, 2 * D)
+    if not joint:
+        dy_ref, dy_columns, refs = refs[0], slice(0, D), refs[1:]
+    hidden_ref, du_ref, refs = refs[0], refs[1], refs[2:]
     if order:
         keep_ref, send_ref, n_rows, dy_rows, sum_ref = refs
     else:
         out_ref, n_rows, dy_rows = refs
-    for k in range(chunks):
-        n_rows[k * ROWS : (k + 1) * ROWS] = ns[k][...]
-        dy_rows[k * ROWS : (k + 1) * ROWS] = dys[k][...]
-    for f in range(0, hiddens[0].shape[1], FCHUNK):
-        columns = slice(f, f + FCHUNK)
-        up, down, at = 0.0, 0.0, 0
-        for hidden, du in zip(hiddens, dus):
-            rows = slice(at, at + du.shape[0])
-            at += du.shape[0]
-            up = up + mm(n_rows[rows], du[:, columns], TN)
-            down = down + mm(hidden[:, columns], dy_rows[rows], TN)
-        if order:
-            sum_ref[0:D] = up
-            sum_ref[D : 2 * D] = down
-            spread_blocks(order_ref, sum_ref, keep_ref, send_ref, columns)
-        else:
-            out_ref[0:D, columns] = up.astype(BF16)
-            out_ref[D : 2 * D, columns] = down.astype(BF16)
+
+    @pl.when(pl.program_id(1) == 0)
+    def _():
+        n_rows[...] = joined(n_ref, slice(0, D))
+        dy_rows[...] = joined(dy_ref, dy_columns)
+
+    up = mm(n_rows[...], du_ref[0], TN)
+    down = mm(hidden_ref[0], dy_rows[...], TN)
+    if order:
+        sum_ref[0:D] = up
+        sum_ref[D : 2 * D] = down
+        spread_experts(order_ref, sum_ref, keep_ref, send_ref)
+    else:
+        out_ref[0, 0:D] = up.astype(BF16)
+        out_ref[0, D : 2 * D] = down.astype(BF16)
+
+
+def spread_experts(order_ref, sum_ref, keep_ref, send_ref):
+    run = sum_ref.shape[0] // BLOCK // 4
+    for j in range(4 * run):
+        start = pl.multiple_of(jnp.bitwise_xor(order_ref[0], j) * BLOCK, BLOCK)
+        block = sum_ref[pl.ds(start, BLOCK)].astype(BF16)
+        ref = keep_ref if j < 2 * run else send_ref
+        at = j % run * BLOCK
+        ref[j // run % 2, 0, at : at + BLOCK] = block
 
 
 def spread_blocks(order_ref, sum_ref, keep_ref, send_ref, columns):
@@ -523,38 +536,50 @@
         ref[at : at + BLOCK, columns] = block
 
 
-def run_expert_weights(ns, dys, hiddens, dus, order=None):
-    width = hiddens[0].shape[1]
-    rows = ROWS * len(ns)
+def run_expert_weights(n, dy, hidden, du, order=None):
+    total, rows, width = hidden.shape
+    args = [n] if dy is None else [n, dy]
+    specs = [
+        pl.BlockSpec((array.shape[0], 1) + array.shape[2:], lambda k, f: (0, k, 0, 0))
+        for array in args
+    ]
     scratch = [pltpu.VMEM((rows, D), BF16)] * 2
-    shape, leading, specs = jax.ShapeDtypeStruct((2 * D, width), BF16), [], None
-    if order is not None:
-        shape = [jax.ShapeDtypeStruct((D, width), BF16)] * 2
+    if order is None:
+        shape = jax.ShapeDtypeStruct((total, 2 * D, width), BF16)
+        out_specs = pl.BlockSpec((1, 2 * D, FCHUNK), lambda k, f: (k, 0, f))
+        leading = []
+    else:
+        shape = [jax.ShapeDtypeStruct((2, total, D // 2, width), BF16)] * 2
+        out_specs = [pl.BlockSpec((2, 1, D // 2, FCHUNK), lambda k, f: (0, k, 0, f))] * 2
         leading = [order]
         scratch.append(pltpu.VMEM((2 * D, FCHUNK), F32))
-    vmem = pl.BlockSpec(memory_space=pltpu.VMEM)
-    return pl.pallas_call(
-        partial(expert_weights_kernel, len(ns), len(hiddens), order is not None),
+    wide_spec = pl.BlockSpec((1, rows, FCHUNK), lambda k, f: (k, 0, f))
+    results = pl.pallas_call(
+        partial(expert_weights_kernel, dy is None, order is not None),
+        grid=(total, width // FCHUNK),
         in_specs=[pl.BlockSpec(memory_space=pltpu.SMEM)] * len(leading)
-        + [vmem] * (2 * len(ns) + 2 * len(hiddens)),
+        + specs
+        + [wide_spec] * 2,
+        out_specs=out_specs,
         out_shape=shape,
         scratch_shapes=scratch,
         compiler_params=pltpu.CompilerParams(vmem_limit_bytes=EXPERT_VMEM),
-        cost_estimate=cost(6.5),
+        cost_estimate=cost(4 * total),
         name="expert_weights",
-    )(*leading, *ns, *dys, *hiddens, *dus)
-
-
-def backward_kernel(depth, images, chunks, order, *refs):
+    )(*leading, *args, hidden, du)
+    if order is None:
+        return results[0]
+    return [r.reshape(total * D, width) for r in results]
+
+
+def backward_kernel(depth, images, order, *refs):
     last = depth == LAYERS - 1
     refs = list(refs)
     take = lambda: refs.pop(0)
     if order:
         order_ref = take()
-    g_ref = take()
-    dn_back = [take() for _ in range(chunks)]
+    g_ref, back_ref = take(), take()
     if last:
-        y_back = [take() for _ in range(chunks)]
         before_gate_ref, before_target_ref = take(), take()
     else:
         picked_ref = take()
@@ -566,11 +591,10 @@
     mats_refs = [take() for _ in range(2 if order else 1)]
     vecs_ref, table_ref = take(), take()
     if last:
-        result_ref = take()
-        outgoing = [take() for _ in range(EXPERTS)]
-    attend_acc, out_acc, dqkv_ref, dz_ref, dn_ref = (take() for _ in range(5))
+        result_ref, dy_out_ref = take(), take()
+    attend_acc, out_acc, dqkv_ref, dz_ref = (take() for _ in range(4))
     if last:
-        y_ref, dy_rows_ref = take(), take()
+        dy_rows_ref = take()
 
     step = pl.program_id(0)
 
@@ -580,9 +604,7 @@
         out_acc[...] = jnp.zeros_like(out_acc)
         vecs_ref[...] = jnp.zeros_like(vecs_ref)
         table_ref[...] = jnp.zeros_like(table_ref)
-        join_chunks(dn_ref, dn_back)
         if last:
-            join_chunks(y_ref, y_back)
             dy_rows_ref[...] = jnp.zeros_like(dy_rows_ref)
 
     some = range(g_ref.shape[0])
@@ -592,8 +614,9 @@
         grad = g_ref[b].astype(F32)
         mid = mid_ref[b]
         gate = gate_ref[b][:, 0:1]
+        rows_back = pick_rows(target_ref[b], back_ref)
         if last:
-            picked = pick_rows(target_ref[b], y_ref)
+            picked, rows_back = rows_back[:, 0:D], rows_back[:, D : 2 * D]
             result_ref[b] = (mid + gate * picked).astype(BF16)
         else:
             picked = picked_ref[b].astype(F32)
@@ -601,7 +624,7 @@
         chosen = jnp.where(lane == as_column(route_ref[b], HW), 1.0, 0.0)
         logit_grad = ((gate * gate_grad) * (chosen - probs_ref[b])).astype(BF16)
         router_grad = mm(logit_grad, n_ref[b], TN)
-        grad_n = pick_rows(target_ref[b], dn_ref) + mm(logit_grad, router_ref[0], NT)
+        grad_n = rows_back + mm(logit_grad, router_ref[0], NT)
         unit, inverse = norm_parts(mid)
         vecs_ref[2:3] += jnp.sum(grad_n * unit, axis=0, keepdims=True)
         vecs_ref[3:4] += jnp.sum(grad_n, axis=0, keepdims=True)
@@ -677,7 +700,7 @@
                 mats_refs[0][:, columns] = acc[...].astype(BF16)
         if last:
             rows = dy_rows_ref[...].reshape(images * TPAD, D)
-            send_rows([outgoing], before_target_ref[...], rows)
+            send_rows(dy_out_ref, before_target_ref[...], rows)
 
 
 def run_backward(
@@ -689,12 +712,11 @@
     if order is not None:
         args.append(order)
         specs.append(pl.BlockSpec(memory_space=pltpu.SMEM))
-    args += [grad] + list(dn_back)
-    specs += [by_image(grad.shape)] + [whole(chunk.shape) for chunk in dn_back]
+    args += [grad, dn_back]
+    specs += [by_image(grad.shape), whole(dn_back.shape)]
     if last:
-        y_back, before_gate, before_target = extra
-        args += list(y_back) + [before_gate, before_target]
-        specs += [whole(chunk.shape) for chunk in y_back]
+        before_gate, before_target = extra
+        args += [before_gate, before_target]
         specs += [by_image(before_gate.shape), whole(before_target.shape)]
     else:
         args.append(extra)
@@ -725,20 +747,18 @@
     ]
     if last:
         outs.append((token_shape, BF16, by_image(token_shape)))
-        outs += [((ROWS, D), BF16, whole((ROWS, D)))] * EXPERTS
+        outs.append(((SLOTS, D), BF16, whole((SLOTS, D))))
     some = images_of(images)
     scratch = [
         pltpu.VMEM((D, 3 * D), F32),
         pltpu.VMEM((D, D), F32),
         pltpu.VMEM((some, WROWS, 3 * D), BF16),
         pltpu.VMEM((some, WROWS, D), BF16),
-        pltpu.VMEM((len(dn_back) // EXPERTS, SLOTS, D), BF16),
     ]
     if last:
-        scratch.append(pltpu.VMEM((len(y_back) // EXPERTS, SLOTS, D), BF16))
         scratch.append(pltpu.VMEM((images, TPAD, D), BF16))
     return pl.pallas_call(
-        partial(backward_kernel, depth, images, len(dn_back), order is not None),
+        partial(backward_kernel, depth, images, order is not None),
         grid=(images // images_of(images),),
         in_specs=specs,
         out_specs=[o[2] for o in outs],
@@ -810,20 +830,32 @@
     return x
 
 
-def exchange(chunks):
+def exchange(rows):
     groups = lax.axis_size("expert")
     if groups > EXPERTS:
-        rows = jnp.stack(chunks)
-        rows = lax.all_to_all(rows, "expert", split_axis=0, concat_axis=0, tiled=True)
-        return [rows[k] for k in range(groups)]
-    out = list(chunks)
-    for k in SEND_ORDER:
-        out[k] = lax.ppermute(chunks[k], "expert", [(i, i ^ k) for i in range(groups)])
-    return out
-
-
-def to_experts(chunks, slices):
-    return exchange([chunk for chunk in chunks for _ in range(slices)])
+        teams, size = None, groups
+    else:
+        teams = [list(range(first, first + TEAM)) for first in range(0, groups, TEAM)]
+        size = TEAM
+    width = rows.shape[-1]
+    runs = rows.reshape(size, -1, width)
+    runs = lax.all_to_all(
+        runs, "expert", split_axis=0, concat_axis=0, tiled=True, axis_index_groups=teams
+    )
+    return runs.reshape(size, -1, ROWS, width)
+
+
+def to_experts(rows, slices):
+    if slices > 1:
+        runs = rows.reshape(EXPERTS, ROWS, rows.shape[1])
+        rows = jnp.repeat(runs, slices, axis=0)
+    return exchange(rows)
+
+
+def from_experts(rows, slices):
+    width = rows.shape[-1]
+    rows = exchange(rows).reshape(EXPERTS, slices, ROWS, width)
+    return rows.transpose(1, 0, 2, 3).reshape(slices, SLOTS, width)
 
 
 def unpack_down(packed):
@@ -853,6 +885,31 @@
     )(keep, got)
 
 
+def add_last_kernel(keep_ref, got_ref, own_ref, partner_ref, low_ref, high_ref):
+    total = keep_ref[...].astype(F32) + got_ref[...].astype(F32)
+    half = total.shape[0] // 2
+    own, partner = total[0:half].astype(BF16), total[half:].astype(BF16)
+    own_ref[...] = own
+    partner_ref[...] = partner
+    both = (own.astype(F32) + partner.astype(F32)).astype(BF16)
+    low_ref[...] = both[0 : half // 2]
+    high_ref[...] = both[half // 2 :]
+
+
+def add_last(keep, got):
+    rows, width = got.shape
+    return pl.pallas_call(
+        add_last_kernel,
+        out_shape=[
+            jax.ShapeDtypeStruct((count, width), BF16)
+            for count in (rows // 2, rows // 2, rows // 4, rows // 4)
+        ],
+        compiler_params=pltpu.CompilerParams(vmem_limit_bytes=12 * 1024 * 1024),
+        cost_estimate=cost(1),
+        name="add_last",
+    )(keep, got)
+
+
 def join_kernel(first_ref, second_ref, out_ref):
     rows = first_ref.shape[0]
     out_ref[0:rows] = first_ref[...]
@@ -870,6 +927,72 @@
     )(first, second)
 
 
+def pack_kernel(order_ref, up_a, up_b, down_a, down_b, up_ref, down_ref, quarter_ref, rows_ref):
+    up = (up_a[0].astype(F32) + up_b[0].astype(F32)).astype(BF16)
+    down = (down_a[0].astype(F32) + down_b[0].astype(F32)).astype(BF16)
+    up_ref[...] = up
+    down_ref[...] = down
+    step, steps = pl.program_id(0), pl.num_programs(0)
+    some, width = up.shape
+    rows_ref[pl.ds(pl.multiple_of(step * some, some), some)] = up
+    for c in range(down.shape[0] // D):
+        rows_ref[D : 2 * D, c * D : (c + 1) * D] = down[c * D : (c + 1) * D]
+
+    @pl.when(step == steps - 1)
+    def _():
+        quarter = quarter_ref.shape[0]
+        start = pl.multiple_of(order_ref[0] * quarter, quarter)
+        quarter_ref[...] = rows_ref[pl.ds(start, quarter)]
+
+
+def pack_weights(depth, order, core_up, residual_up, core_down, residual_down):
+    width = residual_up.shape[2]
+    arrays = [core_up, residual_up, core_down, residual_down]
+    shapes = [(D, width), (width, D), (D // 2, width)]
+    return pl.pallas_call(
+        pack_kernel,
+        grid=(1,),
+        in_specs=[pl.BlockSpec(memory_space=pltpu.SMEM)]
+        + [layer_of(array.shape, depth) for array in arrays],
+        out_specs=[whole(shape) for shape in shapes],
+        out_shape=[jax.ShapeDtypeStruct(shape, BF16) for shape in shapes],
+        scratch_shapes=[pltpu.VMEM((2 * D, width), BF16)],
+        compiler_params=pltpu.CompilerParams(vmem_limit_bytes=VMEM_BYTES),
+        cost_estimate=cost(4),
+        name="pack_weights",
+    )(order, *arrays)
+
+
+def unpack_kernel(order_ref, *refs):
+    pieces, (own_up, own_down, up_ref, down_ref, rows_ref) = refs[:4], refs[4:]
+    quarter = pieces[0].shape[0]
+    for r, piece in enumerate(pieces):
+        start = pl.multiple_of(jnp.bitwise_xor(order_ref[0], r) * quarter, quarter)
+        rows_ref[pl.ds(start, quarter)] = piece[...]
+    up_ref[0] = own_up[...]
+    down_ref[0] = own_down[...]
+    up_ref[1] = rows_ref[0:D]
+    for c in range(down_ref.shape[1] // D):
+        down_ref[1, c * D : (c + 1) * D] = rows_ref[D : 2 * D, c * D : (c + 1) * D]
+
+
+def unpack_weights(order, pieces, own_up, own_down):
+    width = pieces[0].shape[1]
+    shapes = [(2, D, width), (2, width, D)]
+    args = [*pieces, own_up, own_down]
+    return pl.pallas_call(
+        unpack_kernel,
+        grid=(1,),
+        in_specs=[pl.BlockSpec(memory_space=pltpu.SMEM)] + [whole(a.shape) for a in args],
+        out_specs=[whole(shape) for shape in shapes],
+        out_shape=[jax.ShapeDtypeStruct(shape, BF16) for shape in shapes],
+        scratch_shapes=[pltpu.VMEM((2 * D, width), BF16)],
+        compiler_params=pltpu.CompilerParams(vmem_limit_bytes=EXPERT_VMEM),
+        cost_estimate=cost(3),
+        name="unpack_weights",
+    )(order, *args)
+
+
 def expert_outputs_kernel(earlier, order_ref, *refs):
     pieces, refs = refs[:8], refs[8:]
     refs = refs[4 if earlier else 0 :]
@@ -887,6 +1010,8 @@
     for kind in range(2):
         for part in range(2):
             place = jnp.bitwise_xor(order_ref[0], step + part * half)
+            if kind == 1:
+                place = place // 8 * 8 + place // 2 % 2 * 4 + place // 4 % 2 * 2 + place % 2
             start = pl.multiple_of(place * BLOCK, BLOCK)
             block = rows_ref[kind, pl.ds(start, BLOCK)].astype(F32)
             out = outs[kind * 2 + part]
@@ -931,8 +1056,9 @@
     for r in range(2):
         rows_ref[r * half : (r + 1) * half] = pieces[r][...].astype(F32)
     for j in range(D // BLOCK):
-        start = pl.multiple_of(jnp.bitwise_xor(order_ref[0], j) * BLOCK, BLOCK)
-        block = rows_ref[pl.ds(start, BLOCK)]
+        place = jnp.bitwise_xor(order_ref[0], j)
+        place = place // 4 * 4 + place % 2 * 2 + place // 2 % 2
+        block = rows_ref[pl.ds(pl.multiple_of(place * BLOCK, BLOCK), BLOCK)]
         attend_ref[0, j * BLOCK : (j + 1) * BLOCK] = block[:, : 3 * D]
         out_ref[0, j * BLOCK : (j + 1) * BLOCK] = block[:, 3 * D :]
 
@@ -970,66 +1096,70 @@
 class ExpertSum:
     def __init__(self, keep, send):
         self.keep, self.send = keep, send
-        self.steps = iter(
-            (self.core, self.row, self.near_x, self.near_z, self.far_z, self.back_z, self.back_x)
+
+    def core(self):
+        rows = self.keep.shape[0] // 2
+        cuts = ((0, rows), (rows, 2 * rows))
+        self.keep, self.send = add_rows(self.keep, swap(self.send, CORE), cuts)
+        return [self.keep, self.send]
+
+    def row(self):
+        self.own, self.partner, self.core_keep, self.core_send = add_last(
+            self.keep, swap(self.send, ROW)
         )
-
-    def run(self, count):
-        for _ in range(count):
-            next(self.steps)()
-        return self.done
-
-    def core(self):
-        quarter = self.keep.shape[0] // 2
-        cuts = ((0, quarter), (quarter, 2 * quarter))
-        self.keep, self.send = add_rows(self.keep, swap(self.send, CORE), cuts)
-        self.done = [self.keep, self.send]
-
-    def row(self):
-        quarter = self.keep.shape[0]
-        cuts = ((0, quarter), (quarter // 2, quarter))
-        self.mine, self.send = add_rows(self.keep, swap(self.send, ROW), cuts)
-        self.done = [self.mine, self.send]
+        return [self.own, self.partner, self.core_keep, self.core_send]
+
+    def join(self):
+        rows = self.own.shape[0]
+        (self.mine,) = add_rows(self.own, swap(self.partner, FAR_Z), ((0, rows),))
+        return [self.mine]
+
+    def residual_row(self):
+        self.mine_row = swap(self.mine, ROW)
+        return [self.mine_row]
+
+    def residual_core(self):
+        self.residual = [self.mine, self.mine_row, swap(self.mine, CORE), swap(self.mine_row, CORE)]
+        return self.residual
 
     def near_x(self):
-        rows = self.send.shape[0]
+        rows = self.core_send.shape[0]
         cuts = ((0, rows // 2), (rows // 2, rows))
-        self.keep, self.send = add_rows(self.mine, swap(self.send, NEAR_X), cuts)
-        self.done = [self.keep, self.send]
+        got = swap(self.core_send, NEAR_X)
+        self.core_keep, self.core_send = add_rows(self.core_keep, got, cuts)
+        return [self.core_keep, self.core_send]
 
     def near_z(self):
-        rows = self.send.shape[0]
-        (self.total,) = add_rows(self.keep, swap(self.send, NEAR_Z), ((0, rows),))
-        self.done = [self.total]
+        rows = self.core_send.shape[0]
+        (self.total,) = add_rows(self.core_keep, swap(self.core_send, NEAR_Z), ((0, rows),))
+        return [self.total]
 
     def far_z(self):
         rows = self.total.shape[0]
         (self.total,) = add_rows(self.total, swap(self.total, FAR_Z), ((0, rows),))
-        self.done = [self.total]
+        return [self.total]
 
     def back_z(self):
         self.total = join_rows(self.total, swap(self.total, NEAR_Z))
-        self.done = [self.total]
+        return [self.total]
+
+    def back_row(self):
+        self.total = join_rows(self.total, swap(self.total, ROW))
+        return [self.total]
 
     def back_x(self):
-        self.total = join_rows(self.total, swap(self.total, NEAR_X))
-        self.done = [self.total]
-
-    def residual_row(self):
-        self.mine_row = swap(self.mine, ROW)
-        return [self.mine_row]
-
-    def residual_core(self):
-        self.residual = [self.mine, self.mine_row, swap(self.mine, CORE), swap(self.mine_row, CORE)]
-        return self.residual[2:]
-
-    def core_row(self):
-        self.total_row = swap(self.total, ROW)
-        return [self.total_row]
-
-    def core_core(self):
-        self.whole = [self.total, self.total_row, swap(self.total, CORE), swap(self.total_row, CORE)]
-        return self.whole[2:]
+        self.total_x = swap(self.total, NEAR_X)
+        return [self.total_x]
+
+    def back_core(self):
+        self.whole = [self.total, self.total_x, swap(self.total, CORE), swap(self.total_x, CORE)]
+        return self.whole
+
+    def run(self, *steps):
+        done = []
+        for step in steps:
+            done = done + getattr(self, step)()
+        return done
 
 
 class AttendSum:
@@ -1038,7 +1168,7 @@
         self.steps = iter(
             [lambda step=step: self.halve(step) for step in (CORE, ROW, NEAR_X)]
             + [lambda step=step: self.add(step) for step in (NEAR_Z, FAR_Z)]
-            + [lambda step=step: self.join(step) for step in (NEAR_X, ROW)]
+            + [lambda step=step: self.join(step) for step in (ROW, NEAR_X)]
             + [self.last]
         )
 
@@ -1101,8 +1231,29 @@
     routes_rows = jnp.pad(
         routes.reshape(LAYERS, images, HW), ((0, 0), (0, 0), (0, TPAD - HW)), constant_values=-1
     )
-    flip = lax.axis_index("expert") if slices == 1 else 0
-    targets = run_routing(routes_rows, jnp.full((1,), flip, jnp.int32))
+    alone = slices == 1
+    half = lax.axis_index("expert") // TEAM
+    ups, downs, quarters = [], [], []
+    dp_order = place_order((CORE, ROW)) if alone else None
+    for d in range(LAYERS):
+        if not alone:
+            up = lax.dynamic_slice_in_dim(core_up[d], group_part * width, width, 1)
+            down = lax.dynamic_slice_in_dim(core_down[d], group_part * width, width, 0)
+            ups.append((up.astype(F32) + residual_up[d].astype(F32)).astype(BF16)[None])
+            downs.append((down.astype(F32) + residual_down[d].astype(F32)).astype(BF16)[None])
+
+    def pack(d, core_up):
+        up, down, quarter = pack_weights(
+            d, dp_order, core_up, residual_up, core_down, residual_down
+        )
+        ups.append(up)
+        downs.append(down)
+        quarters.append(quarter)
+
+    if alone:
+        pack(0, core_up)
+        routes_rows, bias_table = after((routes_rows, bias_table), quarters[0])
+    targets = run_routing(routes_rows, jnp.full((1,), half, jnp.int32), alone)
 
     table_index = jnp.asarray(offset_table(), jnp.int32)
     picker = (jnp.arange(OFFSETS, dtype=jnp.int32)[:, None] == table_index[None, :]).astype(F32)
@@ -1130,21 +1281,17 @@
     route_rows = [routes_rows[d].reshape(images, 1, TPAD) for d in range(LAYERS)]
     target_rows = [targets[d].reshape(images, 1, TPAD) for d in range(LAYERS)]
     target_all = [targets[d].reshape(1, images * TPAD) for d in range(LAYERS)]
-    ups, downs = [], []
-    for d in range(LAYERS):
-        up_core = lax.dynamic_slice_in_dim(core_up[d], group_part * width, width, 1)
-        down_core = lax.dynamic_slice_in_dim(core_down[d], group_part * width, width, 0)
-        ups.append((up_core.astype(F32) + residual_up[d].astype(F32)).astype(BF16))
-        downs.append((down_core.astype(F32) + residual_down[d].astype(F32)).astype(BF16))
-
     picked_type = BF16 if slices == 1 else F32
     saved, inner, gates, xs, picks = [], [], [], [block_input], []
     x, earlier = block_input, None
     dy_arrived = None
-    def in_parts(chunks):
-        return [chunks[i : i + PART] for i in range(0, len(chunks), PART)]
-
+    def in_parts(rows):
+        return [rows[i : i + PART] for i in range(0, rows.shape[0], PART)]
+
+    first = [swap(quarters[0], FAR_Z)] if alone else []
     for d in range(LAYERS):
+        if alone:
+            x = after(x, quarters[d])
         outs, outgoing = run_forward(
             d, x, earlier, cotangent, route_rows[d], target_rows[d], target_all[d], shared
         )
@@ -1152,59 +1299,60 @@
         if d:
             xs.append(outs[7])
             picks.append(outs[8])
-        arrived = to_experts(outgoing[0], slices)
-        if d == LAYERS - 1:
-            dy_arrived = to_experts(outgoing[1], slices)
-        ys, hiddens, slopes = [], [], []
-        for part in in_parts(arrived):
-            y, (hidden, slope) = run_expert_forward(part, ups[d], downs[d])
-            ys += y
-            hiddens.append(hidden)
-            slopes.append(slope)
-        back = exchange(ys)
-        earlier = (back, gate, target_rows[d], picked_type)
+        if alone:
+            outgoing = after(outgoing, first[d])
+            second = swap(first[d], ROW)
+            if d == 0:
+                pack(1, after(core_up, outgoing))
+        arrived = to_experts(outgoing, slices)
+        if alone:
+            if d == 0:
+                first.append(swap(after(quarters[1], second), FAR_Z))
+            pieces = [first[d], second, swap(first[d], CORE), swap(second, CORE)]
+            ups[d], downs[d] = unpack_weights(dp_order, pieces, ups[d], downs[d])
+        if d < LAYERS - 1:
+            y = run_expert_forward(arrived, ups[d], downs[d])
+            back = from_experts(y, slices)
+            earlier = (back, gate, target_rows[d], picked_type)
         x = mid
         gates.append(gate)
         saved.append([xs[d], qkv, a, mixed, mid, n, probs, gate])
-        inner.append((arrived, hiddens, slopes))
+        inner.append(arrived)
 
     grad = cotangent
     vecs, tables = [None] * 2, [None] * 2
     block_output = None
-    alone = slices == 1
     expert_order = place_order((CORE, ROW, NEAR_X, NEAR_Z)) if alone else None
     attend_order = place_order((CORE, ROW, NEAR_X)) if alone else None
     expert_sums, attend_sums = [None] * 2, [None] * 2
+    dy_arrived = None
     for d in reversed(range(LAYERS)):
-        arrived, hiddens, slopes = inner[d]
-        dns, dus = [], []
-        for at, (part, slope) in enumerate(zip(in_parts(dy_arrived), slopes)):
-            if alone and d == 0:
-                if at == 0:
-                    slope = after(slope, *expert_sums[1].run(1))
-                    expert_sums[1].residual_row()
-                else:
-                    slope = after(slope, *expert_sums[1].run(1), *attend_sums[1].run(1))
-            dn, (du,) = run_expert_inner(part, slope, ups[d], downs[d])
-            dns += dn
-            dus.append(du)
-        dn_back = exchange(dns)
-        grads = run_expert_weights(arrived, dy_arrived, hiddens, dus, expert_order)
-        expert_sums[d] = ExpertSum(*grads) if alone else grads
+        arrived = inner[d]
+        if alone and d == 0:
+            dy_arrived = after(dy_arrived, *attend_sums[1].run(1))
+        rows_out, hidden, du = run_expert_both(arrived, dy_arrived, ups[d], downs[d])
+        if alone and d == 0:
+            rows_out = after(
+                rows_out, *expert_sums[1].run("join", "near_x"), *attend_sums[1].run(1)
+            )
+        back = from_experts(rows_out, slices)
+        grads = run_expert_weights(arrived, dy_arrived, hidden, du, expert_order)
+        if alone:
+            expert_sums[d] = ExpertSum(*grads)
+            done = expert_sums[d].run("core")
+            if d == 0:
+                done = done + expert_sums[1].run("residual_row", "near_z", "far_z")
+            grad = after(grad, *done)
+        else:
+            expert_sums[d] = grads
         if d == LAYERS - 1:
-            extra = (earlier[0], gates[d - 1], target_all[d - 1])
+            extra = (gates[d - 1], target_all[d - 1])
         else:
             extra = picks[d]
-        if alone:
-            done = expert_sums[d].run(1 if d else 2)
-            if d == 0:
-                done = done + expert_sums[1].run(4) + [expert_sums[1].mine_row]
-                done = done + attend_sums[1].run(4)
-            grad = after(grad, *done)
         outs = run_backward(
             d,
             grad,
-            dn_back,
+            back,
             extra,
             saved[d],
             route_rows[d],
@@ -1220,8 +1368,10 @@
             grad, attend_sums[d], vecs[d], tables[d] = outs[:4]
             outs = outs[4:]
         if d == LAYERS - 1:
-            block_output = outs[0]
-            dy_arrived = to_experts(outs[1:], slices)
+            block_output, dy_out = outs
+            if alone:
+                dy_out = after(dy_out, *expert_sums[1].run("row"))
+            dy_arrived = to_experts(dy_out, slices)
     input_grad = grad
 
     dp_steps = bits_of("dp", 1, lax.axis_size("dp"))
@@ -1233,17 +1383,12 @@
         for d in reversed(range(LAYERS)):
             sums, attend = expert_sums[d], attend_sums[d]
             if d:
-                sums.residual_core()
-                sums.core_row()
-                sums.core_core()
-                attend.run(3)
+                sums.run("residual_core")
             else:
-                sums.residual_row()
-                sums.run(5)
-                sums.residual_core()
-                sums.core_row()
-                sums.core_core()
-                attend.run(8)
+                sums.run("row", "join", "near_x", "near_z", "far_z")
+                sums.run("residual_row", "residual_core")
+            sums.run("back_z", "back_row", "back_x", "back_core")
+            attend.run(6 if d else 8)
             experts = expert_outputs(d, expert_order, sums.residual, sums.whole, experts)
             full = attend_outputs(d, attend_order, attend.pieces, full)
         residual_up_grad, residual_down_grad, core_up_grad, core_down_grad = experts

time: 544 us -> 492 us (0.904)
  starting transfers between devices: 177 us -> 91.4 us
  Pallas kernels: 165 us -> 193 us
  local copies, waits for them, and re-layouts: 34.9 us -> 44.9 us
    ppermute x56 -> x0, starting transfers between devices: 106 us -> none  [exchange(): lax.ppermute(chunks[k], 'expert', [(i, i ^ k) for i in range(groups)])]
    ppermute x56 -> x0, waiting for transfers between devices: 102 us -> none  [exchange(): lax.ppermute(chunks[k], 'expert', [(i, i ^ k) for i in range(groups)])]
    ppermute x47 -> x57, waiting for transfers between devices: 47.6 us -> 106 us  [swap(): return lax.ppermute(x, axis, [(i, i ^ bit) for i in range(size)])]
    all_to_all x0 -> x6, waiting for transfers between devices: none -> 39.3 us  [exchange(): lax.all_to_all(runs, 'expert', split_axis=0, concat_axis=0, tiled=True, a...]
    all_to_all x0 -> x6, starting transfers between devices: none -> 24.2 us  [exchange(): lax.all_to_all(runs, 'expert', split_axis=0, concat_axis=0, tiled=True, a...]
    pallas_call x15 -> x16, Pallas kernels: 143 us -> 165 us  [the longest x2 55.2 us: run_backward(): pl.pallas_call(partial(backward_kernel, depth, images, order is not None)...]
    unnamed x168 -> x89, local copies, waits for them, and re-layouts: 17.8 us -> 33.8 us
    ppermute x47 -> x57, starting transfers between devices: 71.2 us -> 67.3 us  [swap(): return lax.ppermute(x, axis, [(i, i ^ bit) for i in range(size)])]
  transfers between devices with their start and end apart: 103 -> 63, of which waited for: 33 -> 24; matrix products, arithmetic and copies ran while one was open for 4% -> 5% of each run, Pallas kernels for 19% -> 33%
where the time goes in v3:
time: 492 us; the launch traced here: 483 us
  Pallas kernels  193 us (39%)
  waiting for transfers between devices  145 us (29%)
  starting transfers between devices  91.4 us (19%)
  local copies, waits for them, and re-layouts  44.9 us (9%)
  matrix products  5.42 us (1%)
    ppermute x57, waiting for transfers between devices, swap(): return lax.ppermute(x, axis, [(i, i ^ bit) for i in range(size)])  106 us
    ppermute x57, starting transfers between devices, swap(): return lax.ppermute(x, axis, [(i, i ^ bit) for i in range(size)])  67.3 us
    pallas_call x2, Pallas kernels, run_backward(): pl.pallas_call(partial(backward_kernel, depth, images, order is not None)...  55.2 us
    pallas_call x2, Pallas kernels, run_forward(): pl.pallas_call(partial(forward_kernel, depth, images), grid=(images // im...  41 us
    all_to_all x6, waiting for transfers between devices, exchange(): lax.all_to_all(runs, 'expert', split_axis=0, concat_axis=0, tiled=True, a...  39.3 us
    unnamed x89, local copies, waits for them, and re-layouts  33.8 us
    pallas_call x2, Pallas kernels, run_expert_both(): pl.pallas_call(partial(expert_both_kernel, joint), grid=(total, n.shape[0...  27.6 us
    all_to_all x6, starting transfers between devices, exchange(): lax.all_to_all(runs, 'expert', split_axis=0, concat_axis=0, tiled=True, a...  24.2 us
  transfers between devices with their start and end apart: 63, of which 24 were waited for; matrix products, arithmetic and copies ran while one was open for 5% of the time, Pallas kernels for 33%

profile of v3, /device:TPU:1, one launch (start us, length us, event | category | flops | bytes accessed | tf_op | source)
XLA Modules:
  0.0 482.5 jit_solution(1741151602798373119)
XLA Ops:
  0.7 4.8 pack_weights.2
  5.5 3.1 collective-permute-start
  10.1 1.9 routing.1
  13.4 3.0 fusion.6
  18.0 17.8 %forward_0.1 = (bf16[6,256,1152]{2,1,0:T(8,128)(2,1)}, bf16[6,256,384]{2,1,0:T(8,128)(2,1)}, bf16[6,256,384]{2,1,0:T(8,128)(2,1)}, f32[6,196,384]{2,1,0:T(8,128)...) custom-call(bf16[6,196,384]{2,1,0:T(8,128)(2,1)} %refs_4_.5, ...), custom_call_target="tpu_custom_call" | custom-call | flops 16199999488 | bytes 1000 | tf_op jit(solution)/shard_map/forward_0/pallas_call | solution.py:380
  35.8 4.1 all-to-all-start
  42.7 10.9 %collective-permute-done.1.refs_1_ = bf16[192,1536]{1,0:T(8,128)(2,1)S(1)} collective-permute-done((bf16[192,1536]{1,0:T(8,128)(2,1)S(1)}, bf16[192,1536]{1,0:T(8,128)(2,1)S(1)}, u32[]{:S(2)}, u32[]{:S(2)}) %collective-permute-start.1) | collective-permute-done | bytes 589856 | tf_op jit(solution)/shard_map/ppermute | solution.py:785
  53.6 2.1 collective-permute-start.3
  63.0 8.5 %expert_forward.1 = bf16[4,2,192,384]{3,2,1,0:T(8,128)(2,1)} custom-call(bf16[4,2,192,384]{3,2,1,0:T(8,128)(2,1)} %bitcast.71, bf16[2,384,1536]{2,1,0:T(8,128)(2,1)} %copy-done.16, bf16[2,1536,384]{2,1,0:T(8,128)(2,1)} %copy-done.17), custom_call_target="tpu_custom_call" | custom-call | flops 7200000000 | bytes 1000 | tf_op jit(solution)/shard_map/expert_forward/pallas_call | solution.py:430
  71.5 3.6 all-to-all-start.1
  77.1 4.8 pack_weights.3
  81.9 1.6 collective-permute-start.4
  83.5 12.5 %all-to-all-done.1 = bf16[4,384,384]{2,1,0:T(8,128)(2,1)S(1)} async-done(((bf16[4,384,384]{2,1,0:T(8,128)(2,1)}), bf16[4,384,384]{2,1,0:T(8,128)(2,1)S(1)}, u32[]{:S(2)}, u32[]{:S(2)}) %all-to-all-start.1) | async-done | bytes 1179680 | tf_op jit(solution)/shard_map/all_to_all | solution.py:842
  97.0 23.2 %forward_1.1 = (bf16[6,256,1152]{2,1,0:T(8,128)(2,1)}, bf16[6,256,384]{2,1,0:T(8,128)(2,1)}, bf16[6,256,384]{2,1,0:T(8,128)(2,1)}, f32[6,196,384]{2,1,0:T(8,128)...) custom-call(f32[6,196,384]{2,1,0:T(8,128)} %get-tuple-element.122.re, ...), custom_call_target="tpu_custom_call" | custom-call | flops 21600000000 | bytes 1000 | tf_op jit(solution)/shard_map/forward_1/pallas_call | solution.py:380
  120.3 3.8 all-to-all-start.2
  125.4 1.8 collective-permute-start.6
  127.1 10.4 %collective-permute-done.5.refs_1_ = bf16[192,1536]{1,0:T(8,128)(2,1)S(1)} collective-permute-done((bf16[192,1536]{1,0:T(8,128)(2,1)S(1)}, bf16[192,1536]{1,0:T(8,128)(2,1)S(1)}, u32[]{:S(2)}, u32[]{:S(2)}) %collective-permute-start.5) | collective-permute-done | bytes 589856 | tf_op jit(solution)/shard_map/ppermute | solution.py:785
  137.5 2.4 collective-permute-start.7
  147.6 3.6 all-to-all-done.2
  152.6 14.8 %expert_both.2 = (bf16[4,2,192,768]{3,2,1,0:T(8,128)(2,1)}, bf16[2,768,1536]{2,1,0:T(8,128)(2,1)}, bf16[2,768,1536]{2,1,0:T(8,128)(2,1)}) custom-call(bf16[4,2,192,768]{3,2,1,0:T(8,128)(2,1)} %bitcast.68, bf16[2,384,1536]{2,1,0:T(8,128)(2,1)} %copy-done.18, bf16[2,1536,384]{2,1,0:T(8,128)(2,1)} %copy-done.19), custom_call_target="tpu_custom_call" | custom-call | flops 10800000000 | bytes 1000 | tf_op jit(solution)/shard_map/expert_both/pallas_call | solution.py:477
  167.4 4.6 all-to-all-start.3
  172.1 2.3 copy-done.26
  174.4 2.3 copy-done.27
  176.8 9.0 %expert_weights.2 = (bf16[2,2,192,1536]{3,2,1,0:T(8,128)(2,1)S(1)}, bf16[2,2,192,1536]{3,2,1,0:T(8,128)(2,1)S(1)}) custom-call(s32[1]{0:T(128)} %bitcast.1.refs_0_.order_ref, bf16[4,2,192,768]{3,2,1,0:T(8,128)(2,1)S(1)} %bitcast.69, bf16[2,768,1536]{2,1,0:T(8,128)(2,1)S(1)} %copy-done.26, bf16[2,768,1536]{2,1,0:T(8,128)(2,1)S(1)} %copy-done.27), custom_call_target="tpu_custom_call" | custom-call | flops 7200000000 | bytes 1000 | tf_op jit(solution)/shard_map/expert_weights/pallas_call | solution.py:557
  188.0 3.6 collective-permute-done.8.got_ref
  193.4 6.4 %all-to-all-done.3 = bf16[4,384,768]{2,1,0:T(8,128)(2,1)} async-done(((bf16[4,384,768]{2,1,0:T(8,128)(2,1)}), bf16[4,384,768]{2,1,0:T(8,128)(2,1)}, u32[]{:S(2)}, u32[]{:S(2)}) %all-to-all-start.3) | async-done | bytes 2359328 | tf_op jit(solution)/shard_map/all_to_all | solution.py:842
  199.8 30.5 %backward_1.1 = (f32[6,196,384]{2,1,0:T(8,128)}, bf16[192,1536]{1,0:T(8,128)(2,1)}, bf16[192,1536]{1,0:T(8,128)(2,1)}, f32[16,384]{1,0:T(8,128)}, f32[64,768]{1,...) custom-call(s32[1]{0:T(128)} %bitcast.refs_0_.order_ref, bf16[6,196,384]{2,1,0:T(8,128)(2,1)} %refs_1_, ...), custom_call_target="tpu_custom_call" | custom-call | flops 29699999744 | bytes 1000 | tf_op jit(solution)/shard_map/backward_1/pallas_call | solution.py:760
  233.7 3.7 all-to-all-start.4
  237.4 1.7 collective-permute-start.10
  242.4 16.8 %all-to-all-done.4 = bf16[4,384,384]{2,1,0:T(8,128)(2,1)S(1)} async-done(((bf16[4,384,384]{2,1,0:T(8,128)(2,1)}), bf16[4,384,384]{2,1,0:T(8,128)(2,1)S(1)}, u32[]{:S(2)}, u32[]{:S(2)}) %all-to-all-start.4) | async-done | bytes 1179680 | tf_op jit(solution)/shard_map/all_to_all | solution.py:842
  260.2 12.8 %expert_both.3 = (bf16[4,2,192,384]{3,2,1,0:T(8,128)(2,1)}, bf16[2,768,1536]{2,1,0:T(8,128)(2,1)}, bf16[2,768,1536]{2,1,0:T(8,128)(2,1)}) custom-call(bf16[4,2,192,384]{3,2,1,0:T(8,128)(2,1)} %bitcast.72, bf16[4,2,192,384]{3,2,1,0:T(8,128)(2,1)} %bitcast.74, bf16[2,384,1536]{2,1,0:T(8,128)(2,1)} %copy-done.16, bf16[2,1536,384]{2,1,0:T(8,128)(2,1)} %copy-done.17), custom_call_target="tpu_custom_call" | custom-call | flops 10800000000 | bytes 1000 | tf_op jit(solution)/shard_map/expert_both/pallas_call | solution.py:477
  274.3 2.3 copy-done.28
  276.6 2.3 copy-done.29
  279.0 9.7 %expert_weights.3 = (bf16[2,2,192,1536]{3,2,1,0:T(8,128)(2,1)S(1)}, bf16[2,2,192,1536]{3,2,1,0:T(8,128)(2,1)}) custom-call(s32[1]{0:T(128)} %bitcast.1.refs_0_.order_ref, bf16[4,2,192,384]{3,2,1,0:T(8,128)(2,1)S(1)} %bitcast.73, bf16[4,2,192,384]{3,2,1,0:T(8,128)(2,1)S(1)} %bitcast.75, bf16[2,768,1536]{2,1,0:T(8,128)(2,1)S(1)} %copy-done.28, ...), custom_call_target="tpu_custom_call" | custom-call | flops 7200000000 | bytes 1000 | tf_op jit(solution)/shard_map/expert_weights/pallas_call | solution.py:557
  288.6 2.3 collective-permute-start.11
  292.7 6.8 %collective-permute-done.14.got_ref = bf16[96,1536]{1,0:T(8,128)(2,1)S(1)} collective-permute-done((bf16[96,1536]{1,0:T(8,128)(2,1)S(1)}, bf16[96,1536]{1,0:T(8,128)(2,1)S(1)}, u32[]{:S(2)}, u32[]{:S(2)}) %collective-permute-start.14) | collective-permute-done | bytes 294944 | tf_op jit(solution)/shard_map/ppermute | solution.py:785
  299.6 2.0 add_rows.23.refs_0_
  301.7 4.3 all-to-all-start.5
  308.6 14.8 %collective-permute-done.15.got_ref = bf16[48,1536]{1,0:T(8,128)(2,1)S(1)} collective-permute-done((bf16[48,1536]{1,0:T(8,128)(2,1)S(1)}, bf16[48,1536]{1,0:T(8,128)(2,1)S(1)}, u32[]{:S(2)}, u32[]{:S(2)}) %collective-permute-start.15) | collective-permute-done | bytes 147488 | tf_op jit(solution)/shard_map/ppermute | solution.py:785
  325.9 7.3 %collective-permute-done.16.got_ref = bf16[48,1536]{1,0:T(8,128)(2,1)S(1)} collective-permute-done((bf16[48,1536]{1,0:T(8,128)(2,1)S(1)}, bf16[48,1536]{1,0:T(8,128)(2,1)S(1)}, u32[]{:S(2)}, u32[]{:S(2)}) %collective-permute-start.16) | collective-permute-done | bytes 147488 | tf_op jit(solution)/shard_map/ppermute | solution.py:785
  333.4 5.9 %collective-permute-done.52.second_ref = bf16[48,1536]{1,0:T(8,128)(2,1)S(1)} collective-permute-done((bf16[48,1536]{1,0:T(8,128)(2,1)S(1)}, bf16[48,1536]{1,0:T(8,128)(2,1)S(1)}, u32[]{:S(2)}, u32[]{:S(2)}) %collective-permute-start.52) | collective-permute-done | bytes 147488 | tf_op jit(solution)/shard_map/ppermute | solution.py:785
  343.8 2.9 add_rows.22
  347.2 24.6 %backward_0.1 = (bf16[6,196,384]{2,1,0:T(8,128)(2,1)}, bf16[192,1536]{1,0:T(8,128)(2,1)}, bf16[192,1536]{1,0:T(8,128)(2,1)}, f32[16,384]{1,0:T(8,128)}, f32[64,768]{1,0:T(8,128)}) custom-call(s32[1]{0:T(128)} %bitcast.refs_0_.order_ref, f32[6,196,384]{2,1,0:T(8,128)} %get-tuple-element.172.refs_1_, bf16[1,1536,384]{2,1,0:T(8,128)(2,1)} %bitcast.30.refs_2_, ...), custom_call_target="tpu_custom_call" | custom-call | flops 21600000000 | bytes 1000 | tf_op jit(solution)/shard_map/backward_0/pallas_call | solution.py:760
  371.8 2.3 collective-permute-start.23
  376.9 1.7 join_rows.10.first_ref
  379.4 1.8 stack.21
  383.7 2.2 reshape.124
  385.8 2.4 fusion.3
  394.3 4.3 collective-permute-done.24.got_ref
  399.5 4.3 collective-permute-done.42.got_ref
  405.0 1.9 collective-permute-done.25.got_ref
  408.2 2.1 collective-permute-start.44
  410.3 2.9 collective-permute-start.50
  416.2 5.4 %collective-permute-done.27.got_ref = bf16[48,1536]{1,0:T(8,128)(2,1)S(1)} collective-permute-done((bf16[48,1536]{1,0:T(8,128)(2,1)S(1)}, bf16[48,1536]{1,0:T(8,128)(2,1)S(1)}, u32[]{:S(2)}, u32[]{:S(2)}) %collective-permute-start.27) | collective-permute-done | bytes 147488 | tf_op jit(solution)/shard_map/ppermute | solution.py:785
  422.7 4.3 collective-permute-done.45.second_ref
  427.1 5.5 %collective-permute-start.36 = (bf16[192,1536]{1,0:T(8,128)(2,1)S(1)}, bf16[192,1536]{1,0:T(8,128)(2,1)S(1)}, u32[]{:S(2)}, u32[]{:S(2)}) collective-permute-start(bf16[192,1536]{1,0:T(8,128)(2,1)S(1)} %join_rows.11.refs_0_), channel_id=1, source_target_pairs={{0,8},{8,0},{16,24},{24,16},{1,9},{9,1},{17,25},{25,17},{2,10},{10... | collective-permute-start | bytes 1769480 | tf_op jit(solution)/shard_map/ppermute | solution.py:785
  435.6 6.1 %expert_outputs.2 = (f32[2,384,1536]{2,1,0:T(8,128)}, f32[2,4,384,384]{3,2,1,0:T(8,128)}, f32[2,384,1536]{2,1,0:T(8,128)}, f32[2,4,384,384]{3,2,1,0:T(8,128)}) custom-call(s32[1]{0:T(128)} %bitcast.1.refs_0_.order_ref, bf16[192,1536]{1,0:T(8,128)(2,1)} %add_rows.23.refs_0_, bf16[192,1536]{1,0:T(8,128)(2,1)} %collective-permute-done.13.refs_1_, ...), custom_call_target="tpu_custom_call" | custom-call | flops 3600000000 | bytes 1000 | tf_op jit(solution)/shard_map/expert_outputs/pallas_call | solution.py:1035
  443.5 13.3 %collective-permute-done.38.got_ref = bf16[192,1536]{1,0:T(8,128)(2,1)S(1)} collective-permute-done((bf16[192,1536]{1,0:T(8,128)(2,1)S(1)}, bf16[192,1536]{1,0:T(8,128)(2,1)S(1)}, u32[]{:S(2)}, u32[]{:S(2)}) %collective-permute-start.38) | collective-permute-done | bytes 589856 | tf_op jit(solution)/shard_map/ppermute | solution.py:785
  456.9 1.7 collective-permute-start.39
  459.2 1.7 attend_outputs.2
  464.2 6.3 %collective-permute-done.39.refs_1_ = bf16[192,1536]{1,0:T(8,128)(2,1)S(1)} collective-permute-done((bf16[192,1536]{1,0:T(8,128)(2,1)S(1)}, bf16[192,1536]{1,0:T(8,128)(2,1)S(1)}, u32[]{:S(2)}, u32[]{:S(2)}) %collective-permute-start.39) | collective-permute-done | bytes 589856 | tf_op jit(solution)/shard_map/ppermute | solution.py:785
  470.5 2.3 collective-permute-start.41
  475.7 1.7 attend_outputs.3
  477.4 5.0 %expert_outputs.3 = (f32[2,384,1536]{2,1,0:T(8,128)}, f32[2,4,384,384]{3,2,1,0:T(8,128)}, f32[2,384,1536]{2,1,0:T(8,128)}, f32[2,4,384,384]{3,2,1,0:T(8,128)}) custom-call(s32[1]{0:T(128)} %bitcast.1.refs_0_.order_ref, bf16[192,1536]{1,0:T(8,128)(2,1)S(1)} %add_rows.36.refs_0_, ...), custom_call_target="tpu_custom_call", output_to_operand_aliasing={{0}: (9, {}), {1}: (10, {}), {2}: (11, {}), {3}: (12, {})} | custom-call | flops 3600000000 | bytes 1000 | tf_op jit(solution)/shard_map/expert_outputs/pallas_call | solution.py:1035
  (226 shorter events, 83.8 us)
Async XLA Ops:
  5.5 30.2 %collective-permute-start = (bf16[192,1536]{1,0:T(8,128)(2,1)}, bf16[192,1536]{1,0:T(8,128)(2,1)S(1)}, u32[]{:S(2)}, u32[]{:S(2)}) collective-permute-start(bf16[192,1536]{1,0:T(8,128)(2,1)} %get-tuple-element.113), channel_id=1, source_target_pairs={{0,4},{1,5},{2,6},{3,7},{4,0},{5,1},{6,2},{7,3},{8,12},{9,13},{10,... | collective-permute-start | bytes 1769480 | tf_op jit(solution)/shard_map/ppermute | solution.py:785
  35.8 26.2 %all-to-all-start = ((bf16[4,384,384]{2,1,0:T(8,128)(2,1)}), bf16[4,384,384]{2,1,0:T(8,128)(2,1)S(1)}, u32[]{:S(2)}, u32[]{:S(2)}) async-start(bf16[4,384,384]{2,1,0:T(8,128)(2,1)} %bitcast.83), calls=%async_computation | async-start | bytes 2359296 | tf_op jit(solution)/shard_map/all_to_all | solution.py:842
  39.9 13.7 %collective-permute-start.1 = (bf16[192,1536]{1,0:T(8,128)(2,1)S(1)}, bf16[192,1536]{1,0:T(8,128)(2,1)S(1)}, u32[]{:S(2)}, u32[]{:S(2)}) collective-permute-start(bf16[192,1536]{1,0:T(8,128)(2,1)S(1)} %collective-permute-done.refs_0_), channel_id=1, source_target_pairs={{0,16},{8,24},{16,0},{24,8},{1,17},{9,25},{17,1},{25,9},{2,18},{10... | collective-permute-start | bytes 1769480 | tf_op jit(solution)/shard_map/ppermute | solution.py:785
  41.2 14.5 %collective-permute-start.2 = (bf16[192,1536]{1,0:T(8,128)(2,1)S(1)}, bf16[192,1536]{1,0:T(8,128)(2,1)S(1)}, u32[]{:S(2)}, u32[]{:S(2)}) collective-permute-start(bf16[192,1536]{1,0:T(8,128)(2,1)S(1)} %collective-permute-done.refs_0_), channel_id=1, source_target_pairs={{0,8},{8,0},{16,24},{24,16},{1,9},{9,1},{17,25},{25,17},{2,10},{10... | collective-permute-start | bytes 1769480 | tf_op jit(solution)/shard_map/ppermute | solution.py:785
  53.6 3.8 collective-permute-start.3
  71.5 24.5 %all-to-all-start.1 = ((bf16[4,384,384]{2,1,0:T(8,128)(2,1)}), bf16[4,384,384]{2,1,0:T(8,128)(2,1)S(1)}, u32[]{:S(2)}, u32[]{:S(2)}) async-start(bf16[4,384,384]{2,1,0:T(8,128)(2,1)} %bitcast.85), calls=%async_computation.1 | async-start | bytes 2359296 | tf_op jit(solution)/shard_map/all_to_all | solution.py:842
  81.9 38.3 %collective-permute-start.4 = (bf16[192,1536]{1,0:T(8,128)(2,1)}, bf16[192,1536]{1,0:T(8,128)(2,1)S(1)}, u32[]{:S(2)}, u32[]{:S(2)}) collective-permute-start(bf16[192,1536]{1,0:T(8,128)(2,1)} %get-tuple-element.129), channel_id=1, source_target_pairs={{0,4},{1,5},{2,6},{3,7},{4,0},{5,1},{6,2},{7,3},{8,12},{9,13},{10,... | collective-permute-start | bytes 1769480 | tf_op jit(solution)/shard_map/ppermute | solution.py:785
  120.3 30.9 %all-to-all-start.2 = ((bf16[4,384,768]{2,1,0:T(8,128)(2,1)}), bf16[4,384,768]{2,1,0:T(8,128)(2,1)S(1)}, u32[]{:S(2)}, u32[]{:S(2)}) async-start(bf16[4,384,768]{2,1,0:T(8,128)(2,1)} %bitcast.80), calls=%async_computation.2 | async-start | bytes 4718592 | tf_op jit(solution)/shard_map/all_to_all | solution.py:842
  124.1 13.4 %collective-permute-start.5 = (bf16[192,1536]{1,0:T(8,128)(2,1)S(1)}, bf16[192,1536]{1,0:T(8,128)(2,1)S(1)}, u32[]{:S(2)}, u32[]{:S(2)}) collective-permute-start(bf16[192,1536]{1,0:T(8,128)(2,1)S(1)} %collective-permute-done.4.refs_0_), channel_id=1, source_target_pairs={{0,16},{8,24},{16,0},{24,8},{1,17},{9,25},{17,1},{25,9},{2,18},{10... | collective-permute-start | bytes 1769480 | tf_op jit(solution)/shard_map/ppermute | solution.py:785
  125.4 14.5 %collective-permute-start.6 = (bf16[192,1536]{1,0:T(8,128)(2,1)S(1)}, bf16[192,1536]{1,0:T(8,128)(2,1)S(1)}, u32[]{:S(2)}, u32[]{:S(2)}) collective-permute-start(bf16[192,1536]{1,0:T(8,128)(2,1)S(1)} %collective-permute-done.4.refs_0_), channel_id=1, source_target_pairs={{0,8},{8,0},{16,24},{24,16},{1,9},{9,1},{17,25},{25,17},{2,10},{10... | collective-permute-start | bytes 1769480 | tf_op jit(solution)/shard_map/ppermute | solution.py:785
  137.5 4.0 collective-permute-start.7
  167.4 32.4 %all-to-all-start.3 = ((bf16[4,384,768]{2,1,0:T(8,128)(2,1)}), bf16[4,384,768]{2,1,0:T(8,128)(2,1)}, u32[]{:S(2)}, u32[]{:S(2)}) async-start(bf16[4,384,768]{2,1,0:T(8,128)(2,1)} %bitcast.79), calls=%async_computation.3 | async-start | bytes 4718592 | tf_op jit(solution)/shard_map/all_to_all | solution.py:842
  185.8 5.7 %collective-permute-start.8 = (bf16[768,1536]{1,0:T(8,128)(2,1)S(1)}, bf16[768,1536]{1,0:T(8,128)(2,1)S(1)}, u32[]{:S(2)}, u32[]{:S(2)}) collective-permute-start(bf16[768,1536]{1,0:T(8,128)(2,1)S(1)} %bitcast.76), channel_id=1, source_target_pairs={{0,8},{8,0},{16,24},{24,16},{1,9},{9,1},{17,25},{25,17},{2,10},{10... | collective-permute-start | bytes 7077896 | tf_op jit(solution)/shard_map/ppermute | solution.py:785
  192.1 38.2 %collective-permute-start.9 = (bf16[384,1536]{1,0:T(8,128)(2,1)S(1)}, bf16[384,1536]{1,0:T(8,128)(2,1)S(1)}, u32[]{:S(2)}, u32[]{:S(2)}) collective-permute-start(bf16[384,1536]{1,0:T(8,128)(2,1)S(1)} %get-tuple-element.140), channel_id=1, source_target_pairs={{0,16},{8,24},{16,0},{24,8},{1,17},{9,25},{17,1},{25,9},{2,18},{10... | collective-permute-start | bytes 3538952 | tf_op jit(solution)/shard_map/ppermute | solution.py:785
  233.7 25.4 %all-to-all-start.4 = ((bf16[4,384,384]{2,1,0:T(8,128)(2,1)}), bf16[4,384,384]{2,1,0:T(8,128)(2,1)S(1)}, u32[]{:S(2)}, u32[]{:S(2)}) async-start(bf16[4,384,384]{2,1,0:T(8,128)(2,1)} %bitcast.82), calls=%async_computation.4 | async-start | bytes 2359296 | tf_op jit(solution)/shard_map/all_to_all | solution.py:842
  237.4 3.4 collective-permute-start.10
  239.2 60.4 %collective-permute-start.12 = (bf16[192,1536]{1,0:T(8,128)(2,1)}, bf16[192,1536]{1,0:T(8,128)(2,1)}, u32[]{:S(2)}, u32[]{:S(2)}) collective-permute-start(bf16[192,1536]{1,0:T(8,128)(2,1)} %get-tuple-element.155), channel_id=1, source_target_pairs={{0,4},{1,5},{2,6},{3,7},{4,0},{5,1},{6,2},{7,3},{8,12},{9,13},{10,... | collective-permute-start | bytes 1769480 | tf_op jit(solution)/shard_map/ppermute | solution.py:785
  288.6 55.1 %collective-permute-start.11 = (bf16[768,1536]{1,0:T(8,128)(2,1)}, bf16[768,1536]{1,0:T(8,128)(2,1)}, u32[]{:S(2)}, u32[]{:S(2)}) collective-permute-start(bf16[768,1536]{1,0:T(8,128)(2,1)} %bitcast.28), channel_id=1, source_target_pairs={{0,8},{8,0},{16,24},{24,16},{1,9},{9,1},{17,25},{25,17},{2,10},{10... | collective-permute-start | bytes 7077896 | tf_op jit(solution)/shard_map/ppermute | solution.py:785
  290.9 8.6 %collective-permute-start.14 = (bf16[96,1536]{1,0:T(8,128)(2,1)S(1)}, bf16[96,1536]{1,0:T(8,128)(2,1)S(1)}, u32[]{:S(2)}, u32[]{:S(2)}) collective-permute-start(bf16[96,1536]{1,0:T(8,128)(2,1)S(1)} %copy-done.7), channel_id=1, source_target_pairs={{0,1},{1,0},{2,3},{3,2},{4,5},{5,4},{6,7},{7,6},{8,9},{9,8},{10,11... | collective-permute-start | bytes 884744 | tf_op jit(solution)/shard_map/ppermute | solution.py:785
  291.5 10.1 %collective-permute-start.17 = (bf16[96,1536]{1,0:T(8,128)(2,1)S(1)}, bf16[96,1536]{1,0:T(8,128)(2,1)S(1)}, u32[]{:S(2)}, u32[]{:S(2)}) collective-permute-start(bf16[96,1536]{1,0:T(8,128)(2,1)S(1)} %copy-done.9), channel_id=1, source_target_pairs={{0,16},{8,24},{16,0},{24,8},{1,17},{9,25},{17,1},{25,9},{2,18},{10... | collective-permute-start | bytes 884744 | tf_op jit(solution)/shard_map/ppermute | solution.py:785
  301.7 45.5 %all-to-all-start.5 = ((bf16[4,384,384]{2,1,0:T(8,128)(2,1)}), bf16[4,384,384]{2,1,0:T(8,128)(2,1)}, u32[]{:S(2)}, u32[]{:S(2)}) async-start(bf16[4,384,384]{2,1,0:T(8,128)(2,1)} %bitcast.81), calls=%async_computation.5 | async-start | bytes 2359296 | tf_op jit(solution)/shard_map/all_to_all | solution.py:842
  306.0 17.4 %collective-permute-start.15 = (bf16[48,1536]{1,0:T(8,128)(2,1)S(1)}, bf16[48,1536]{1,0:T(8,128)(2,1)S(1)}, u32[]{:S(2)}, u32[]{:S(2)}) collective-permute-start(bf16[48,1536]{1,0:T(8,128)(2,1)S(1)} %get-tuple-element.171), channel_id=1, source_target_pairs={{0,2},{1,3},{2,0},{3,1},{4,6},{5,7},{6,4},{7,5},{8,10},{9,11},{10,... | collective-permute-start | bytes 442376 | tf_op jit(solution)/shard_map/ppermute | solution.py:785
  307.4 17.4 %collective-permute-start.31 = (bf16[48,1536]{1,0:T(8,128)(2,1)S(1)}, bf16[48,1536]{1,0:T(8,128)(2,1)S(1)}, u32[]{:S(2)}, u32[]{:S(2)}) collective-permute-start(bf16[48,1536]{1,0:T(8,128)(2,1)S(1)} %get-tuple-element.175), channel_id=1, source_target_pairs={{0,1},{1,0},{2,3},{3,2},{4,5},{5,4},{6,7},{7,6},{8,9},{9,8},{10,11... | collective-permute-start | bytes 442376 | tf_op jit(solution)/shard_map/ppermute | solution.py:785
  323.4 9.7 %collective-permute-start.16 = (bf16[48,1536]{1,0:T(8,128)(2,1)S(1)}, bf16[48,1536]{1,0:T(8,128)(2,1)S(1)}, u32[]{:S(2)}, u32[]{:S(2)}) collective-permute-start(bf16[48,1536]{1,0:T(8,128)(2,1)S(1)} %add_rows.25.keep_ref), channel_id=1, source_target_pairs={{0,4},{1,5},{2,6},{3,7},{4,0},{5,1},{6,2},{7,3},{8,12},{9,13},{10,... | collective-permute-start | bytes 442376 | tf_op jit(solution)/shard_map/ppermute | solution.py:785
  323.5 23.7 %collective-permute-start.13 = (bf16[192,1536]{1,0:T(8,128)(2,1)}, bf16[192,1536]{1,0:T(8,128)(2,1)}, u32[]{:S(2)}, u32[]{:S(2)}) collective-permute-start(bf16[192,1536]{1,0:T(8,128)(2,1)} %add_rows.23.refs_0_), channel_id=1, source_target_pairs={{0,16},{8,24},{16,0},{24,8},{1,17},{9,25},{17,1},{25,9},{2,18},{10... | collective-permute-start | bytes 1769480 | tf_op jit(solution)/shard_map/ppermute | solution.py:785
  324.9 8.4 %collective-permute-start.32 = (bf16[48,1536]{1,0:T(8,128)(2,1)S(1)}, bf16[48,1536]{1,0:T(8,128)(2,1)S(1)}, u32[]{:S(2)}, u32[]{:S(2)}) collective-permute-start(bf16[48,1536]{1,0:T(8,128)(2,1)S(1)} %add_rows.33.keep_ref), channel_id=1, source_target_pairs={{0,2},{1,3},{2,0},{3,1},{4,6},{5,7},{6,4},{7,5},{8,10},{9,11},{10,... | collective-permute-start | bytes 442376 | tf_op jit(solution)/shard_map/ppermute | solution.py:785
  333.2 6.1 %collective-permute-start.52 = (bf16[48,1536]{1,0:T(8,128)(2,1)S(1)}, bf16[48,1536]{1,0:T(8,128)(2,1)S(1)}, u32[]{:S(2)}, u32[]{:S(2)}) collective-permute-start(bf16[48,1536]{1,0:T(8,128)(2,1)S(1)} %add_rows.26.first_ref), channel_id=1, source_target_pairs={{0,2},{1,3},{2,0},{3,1},{4,6},{5,7},{6,4},{7,5},{8,10},{9,11},{10,... | collective-permute-start | bytes 442376 | tf_op jit(solution)/shard_map/ppermute | solution.py:785
  333.3 8.8 %collective-permute-start.33 = (bf16[48,1536]{1,0:T(8,128)(2,1)S(1)}, bf16[48,1536]{1,0:T(8,128)(2,1)S(1)}, u32[]{:S(2)}, u32[]{:S(2)}) collective-permute-start(bf16[48,1536]{1,0:T(8,128)(2,1)S(1)} %add_rows.34.keep_ref), channel_id=1, source_target_pairs={{0,4},{1,5},{2,6},{3,7},{4,0},{5,1},{6,2},{7,3},{8,12},{9,13},{10,... | collective-permute-start | bytes 442376 | tf_op jit(solution)/shard_map/ppermute | solution.py:785
  340.0 35.1 %collective-permute-start.53 = (bf16[96,1536]{1,0:T(8,128)(2,1)}, bf16[96,1536]{1,0:T(8,128)(2,1)}, u32[]{:S(2)}, u32[]{:S(2)}) collective-permute-start(bf16[96,1536]{1,0:T(8,128)(2,1)} %join_rows.14.first_ref), channel_id=1, source_target_pairs={{0,16},{8,24},{16,0},{24,8},{1,17},{9,25},{17,1},{25,9},{2,18},{10... | collective-permute-start | bytes 884744 | tf_op jit(solution)/shard_map/ppermute | solution.py:785
  342.8 34.2 %collective-permute-start.34 = (bf16[48,1536]{1,0:T(8,128)(2,1)}, bf16[48,1536]{1,0:T(8,128)(2,1)}, u32[]{:S(2)}, u32[]{:S(2)}) collective-permute-start(bf16[48,1536]{1,0:T(8,128)(2,1)} %add_rows.35.first_ref), channel_id=1, source_target_pairs={{0,16},{8,24},{16,0},{24,8},{1,17},{9,25},{17,1},{25,9},{2,18},{10... | collective-permute-start | bytes 442376 | tf_op jit(solution)/shard_map/ppermute | solution.py:785
  346.7 44.9 %collective-permute-start.37 = (bf16[384,1536]{1,0:T(8,128)(2,1)}, bf16[384,1536]{1,0:T(8,128)(2,1)S(1)}, u32[]{:S(2)}, u32[]{:S(2)}) collective-permute-start(bf16[384,1536]{1,0:T(8,128)(2,1)} %get-tuple-element.169), channel_id=1, source_target_pairs={{0,16},{8,24},{16,0},{24,8},{1,17},{9,25},{17,1},{25,9},{2,18},{10... | collective-permute-start | bytes 3538952 | tf_op jit(solution)/shard_map/ppermute | solution.py:785
  347.2 26.9 %copy-start.31 = (f32[64,768]{1,0:T(8,128)S(1)}, f32[64,768]{1,0:T(8,128)}, u32[]{:S(2)}) copy-start(f32[64,768]{1,0:T(8,128)} %get-tuple-element.187) | copy-start | bytes 589828
  371.8 16.4 %collective-permute-start.23 = (bf16[192,1536]{1,0:T(8,128)(2,1)}, bf16[192,1536]{1,0:T(8,128)(2,1)}, u32[]{:S(2)}, u32[]{:S(2)}) collective-permute-start(bf16[192,1536]{1,0:T(8,128)(2,1)} %get-tuple-element.189), channel_id=1, source_target_pairs={{0,8},{8,0},{16,24},{24,16},{1,9},{9,1},{17,25},{25,17},{2,10},{10... | collective-permute-start | bytes 1769480 | tf_op jit(solution)/shard_map/ppermute | solution.py:785
  376.2 34.1 %collective-permute-start.54 = (bf16[192,1536]{1,0:T(8,128)(2,1)S(1)}, bf16[192,1536]{1,0:T(8,128)(2,1)S(1)}, u32[]{:S(2)}, u32[]{:S(2)}) collective-permute-start(bf16[192,1536]{1,0:T(8,128)(2,1)S(1)} %join_rows.15.refs_4_), channel_id=1, source_target_pairs={{0,1},{1,0},{2,3},{3,2},{4,5},{5,4},{6,7},{7,6},{8,9},{9,8},{10,11... | collective-permute-start | bytes 1769480 | tf_op jit(solution)/shard_map/ppermute | solution.py:785
  378.7 34.5 %collective-permute-start.35 = (bf16[96,1536]{1,0:T(8,128)(2,1)}, bf16[96,1536]{1,0:T(8,128)(2,1)}, u32[]{:S(2)}, u32[]{:S(2)}) collective-permute-start(bf16[96,1536]{1,0:T(8,128)(2,1)} %join_rows.10.first_ref), channel_id=1, source_target_pairs={{0,1},{1,0},{2,3},{3,2},{4,5},{5,4},{6,7},{7,6},{8,9},{9,8},{10,11... | collective-permute-start | bytes 884744 | tf_op jit(solution)/shard_map/ppermute | solution.py:785
  390.6 8.0 %collective-permute-start.24 = (bf16[96,1536]{1,0:T(8,128)(2,1)S(1)}, bf16[96,1536]{1,0:T(8,128)(2,1)S(1)}, u32[]{:S(2)}, u32[]{:S(2)}) collective-permute-start(bf16[96,1536]{1,0:T(8,128)(2,1)S(1)} %get-tuple-element.191), channel_id=1, source_target_pairs={{0,16},{8,24},{16,0},{24,8},{1,17},{9,25},{17,1},{25,9},{2,18},{10... | collective-permute-start | bytes 884744 | tf_op jit(solution)/shard_map/ppermute | solution.py:785
  392.1 11.8 %collective-permute-start.42 = (bf16[96,1536]{1,0:T(8,128)(2,1)S(1)}, bf16[96,1536]{1,0:T(8,128)(2,1)S(1)}, u32[]{:S(2)}, u32[]{:S(2)}) collective-permute-start(bf16[96,1536]{1,0:T(8,128)(2,1)S(1)} %get-tuple-element.201), channel_id=1, source_target_pairs={{0,1},{1,0},{2,3},{3,2},{4,5},{5,4},{6,7},{7,6},{8,9},{9,8},{10,11... | collective-permute-start | bytes 884744 | tf_op jit(solution)/shard_map/ppermute | solution.py:785
  393.1 10.8 %collective-permute-start.18 = (f32[56,384]{1,0:T(8,128)S(1)}, f32[56,384]{1,0:T(8,128)S(1)}, u32[]{:S(2)}, u32[]{:S(2)}) collective-permute-start(f32[56,384]{1,0:T(8,128)S(1)} %select_maximum_fusion), channel_id=1, source_target_pairs={{0,8},{8,0},{16,24},{24,16},{1,9},{9,1},{17,25},{25,17},{2,10},{10... | collective-permute-start | bytes 258056 | tf_op jit(solution)/shard_map/ppermute | solution.py:785
  398.7 8.3 %collective-permute-start.25 = (bf16[48,1536]{1,0:T(8,128)(2,1)S(1)}, bf16[48,1536]{1,0:T(8,128)(2,1)S(1)}, u32[]{:S(2)}, u32[]{:S(2)}) collective-permute-start(bf16[48,1536]{1,0:T(8,128)(2,1)S(1)} %get-tuple-element.193), channel_id=1, source_target_pairs={{0,1},{1,0},{2,3},{3,2},{4,5},{5,4},{6,7},{7,6},{8,9},{9,8},{10,11... | collective-permute-start | bytes 442376 | tf_op jit(solution)/shard_map/ppermute | solution.py:785
  403.9 4.3 collective-permute-start.43
  404.0 3.4 collective-permute-start.19
  407.0 7.3 %collective-permute-start.26 = (bf16[48,1536]{1,0:T(8,128)(2,1)S(1)}, bf16[48,1536]{1,0:T(8,128)(2,1)S(1)}, u32[]{:S(2)}, u32[]{:S(2)}) collective-permute-start(bf16[48,1536]{1,0:T(8,128)(2,1)S(1)} %add_rows.30.keep_ref), channel_id=1, source_target_pairs={{0,2},{1,3},{2,0},{3,1},{4,6},{5,7},{6,4},{7,5},{8,10},{9,11},{10,... | collective-permute-start | bytes 442376 | tf_op jit(solution)/shard_map/ppermute | solution.py:785
  407.4 5.9 %collective-permute-start.20 = (f32[56,384]{1,0:T(8,128)S(1)}, f32[56,384]{1,0:T(8,128)S(1)}, u32[]{:S(2)}, u32[]{:S(2)}) collective-permute-start(f32[56,384]{1,0:T(8,128)S(1)} %add.64), channel_id=1, source_target_pairs={{0,1},{1,0},{2,3},{3,2},{4,5},{5,4},{6,7},{7,6},{8,9},{9,8},{10,11... | collective-permute-start | bytes 258056 | tf_op jit(solution)/shard_map/ppermute | solution.py:785
  408.2 6.9 %collective-permute-start.44 = (bf16[48,1536]{1,0:T(8,128)(2,1)S(1)}, bf16[48,1536]{1,0:T(8,128)(2,1)S(1)}, u32[]{:S(2)}, u32[]{:S(2)}) collective-permute-start(bf16[48,1536]{1,0:T(8,128)(2,1)S(1)} %add_rows.38.keep_ref), channel_id=1, source_target_pairs={{0,4},{1,5},{2,6},{3,7},{4,0},{5,1},{6,2},{7,3},{8,12},{9,13},{10,... | collective-permute-start | bytes 442376 | tf_op jit(solution)/shard_map/ppermute | solution.py:785
  410.3 16.8 %collective-permute-start.50 = (bf16[192,1536]{1,0:T(8,128)(2,1)}, bf16[192,1536]{1,0:T(8,128)(2,1)S(1)}, u32[]{:S(2)}, u32[]{:S(2)}) collective-permute-start(bf16[192,1536]{1,0:T(8,128)(2,1)} %add_rows.23.refs_0_), channel_id=1, source_target_pairs={{0,8},{8,0},{16,24},{24,16},{1,9},{9,1},{17,25},{25,17},{2,10},{10... | collective-permute-start | bytes 1769480 | tf_op jit(solution)/shard_map/ppermute | solution.py:785
  413.2 19.4 %collective-permute-start.55 = (bf16[192,1536]{1,0:T(8,128)(2,1)S(1)}, bf16[192,1536]{1,0:T(8,128)(2,1)S(1)}, u32[]{:S(2)}, u32[]{:S(2)}) collective-permute-start(bf16[192,1536]{1,0:T(8,128)(2,1)S(1)} %join_rows.15.refs_4_), channel_id=1, source_target_pairs={{0,8},{8,0},{16,24},{24,16},{1,9},{9,1},{17,25},{25,17},{2,10},{10... | collective-permute-start | bytes 1769480 | tf_op jit(solution)/shard_map/ppermute | solution.py:785
  413.3 20.8 %collective-permute-start.51 = (bf16[192,1536]{1,0:T(8,128)(2,1)}, bf16[192,1536]{1,0:T(8,128)(2,1)S(1)}, u32[]{:S(2)}, u32[]{:S(2)}) collective-permute-start(bf16[192,1536]{1,0:T(8,128)(2,1)} %collective-permute-done.13.refs_1_), channel_id=1, source_target_pairs={{0,8},{8,0},{16,24},{24,16},{1,9},{9,1},{17,25},{25,17},{2,10},{10... | collective-permute-start | bytes 1769480 | tf_op jit(solution)/shard_map/ppermute | solution.py:785
  414.3 20.6 %collective-permute-start.56 = (bf16[192,1536]{1,0:T(8,128)(2,1)S(1)}, bf16[192,1536]{1,0:T(8,128)(2,1)S(1)}, u32[]{:S(2)}, u32[]{:S(2)}) collective-permute-start(bf16[192,1536]{1,0:T(8,128)(2,1)S(1)} %collective-permute-done.54.refs_5_), channel_id=1, source_target_pairs={{0,8},{8,0},{16,24},{24,16},{1,9},{9,1},{17,25},{25,17},{2,10},{10... | collective-permute-start | bytes 1769480 | tf_op jit(solution)/shard_map/ppermute | solution.py:785
  415.1 6.5 %collective-permute-start.27 = (bf16[48,1536]{1,0:T(8,128)(2,1)S(1)}, bf16[48,1536]{1,0:T(8,128)(2,1)S(1)}, u32[]{:S(2)}, u32[]{:S(2)}) collective-permute-start(bf16[48,1536]{1,0:T(8,128)(2,1)S(1)} %add_rows.31.keep_ref), channel_id=1, source_target_pairs={{0,4},{1,5},{2,6},{3,7},{4,0},{5,1},{6,2},{7,3},{8,12},{9,13},{10,... | collective-permute-start | bytes 442376 | tf_op jit(solution)/shard_map/ppermute | solution.py:785
  421.6 5.4 %collective-permute-start.45 = (bf16[48,1536]{1,0:T(8,128)(2,1)S(1)}, bf16[48,1536]{1,0:T(8,128)(2,1)S(1)}, u32[]{:S(2)}, u32[]{:S(2)}) collective-permute-start(bf16[48,1536]{1,0:T(8,128)(2,1)S(1)} %add_rows.39.first_ref), channel_id=1, source_target_pairs={{0,2},{1,3},{2,0},{3,1},{4,6},{5,7},{6,4},{7,5},{8,10},{9,11},{10,... | collective-permute-start | bytes 442376 | tf_op jit(solution)/shard_map/ppermute | solution.py:785
  427.0 29.8 %collective-permute-start.38 = (bf16[192,1536]{1,0:T(8,128)(2,1)S(1)}, bf16[192,1536]{1,0:T(8,128)(2,1)S(1)}, u32[]{:S(2)}, u32[]{:S(2)}) collective-permute-start(bf16[192,1536]{1,0:T(8,128)(2,1)S(1)} %get-tuple-element.199), channel_id=1, source_target_pairs={{0,4},{1,5},{2,6},{3,7},{4,0},{5,1},{6,2},{7,3},{8,12},{9,13},{10,... | collective-permute-start | bytes 1769480 | tf_op jit(solution)/shard_map/ppermute | solution.py:785
  427.1 32.1 %collective-permute-start.36 = (bf16[192,1536]{1,0:T(8,128)(2,1)S(1)}, bf16[192,1536]{1,0:T(8,128)(2,1)S(1)}, u32[]{:S(2)}, u32[]{:S(2)}) collective-permute-start(bf16[192,1536]{1,0:T(8,128)(2,1)S(1)} %join_rows.11.refs_0_), channel_id=1, source_target_pairs={{0,8},{8,0},{16,24},{24,16},{1,9},{9,1},{17,25},{25,17},{2,10},{10... | collective-permute-start | bytes 1769480 | tf_op jit(solution)/shard_map/ppermute | solution.py:785
  432.6 9.1 %collective-permute-start.21 = (f32[56,384]{1,0:T(8,128)S(1)}, f32[56,384]{1,0:T(8,128)S(1)}, u32[]{:S(2)}, u32[]{:S(2)}) collective-permute-start(f32[56,384]{1,0:T(8,128)S(1)} %add.65), channel_id=1, source_target_pairs={{0,2},{1,3},{2,0},{3,1},{4,6},{5,7},{6,4},{7,5},{8,10},{9,11},{10,... | collective-permute-start | bytes 258056 | tf_op jit(solution)/shard_map/ppermute | solution.py:785
  434.1 8.5 %collective-permute-start.28 = (bf16[48,1536]{1,0:T(8,128)(2,1)S(1)}, bf16[48,1536]{1,0:T(8,128)(2,1)S(1)}, u32[]{:S(2)}, u32[]{:S(2)}) collective-permute-start(bf16[48,1536]{1,0:T(8,128)(2,1)S(1)} %add_rows.32.first_ref), channel_id=1, source_target_pairs={{0,16},{8,24},{16,0},{24,8},{1,17},{9,25},{17,1},{25,9},{2,18},{10... | collective-permute-start | bytes 442376 | tf_op jit(solution)/shard_map/ppermute | solution.py:785
  434.9 23.7 %collective-permute-start.46 = (bf16[96,1536]{1,0:T(8,128)(2,1)S(1)}, bf16[96,1536]{1,0:T(8,128)(2,1)S(1)}, u32[]{:S(2)}, u32[]{:S(2)}) collective-permute-start(bf16[96,1536]{1,0:T(8,128)(2,1)S(1)} %join_rows.12.first_ref), channel_id=1, source_target_pairs={{0,16},{8,24},{16,0},{24,8},{1,17},{9,25},{17,1},{25,9},{2,18},{10... | collective-permute-start | bytes 884744 | tf_op jit(solution)/shard_map/ppermute | solution.py:785
  441.7 19.2 %collective-permute-start.22 = (f32[56,384]{1,0:T(8,128)S(1)}, f32[56,384]{1,0:T(8,128)S(1)}, u32[]{:S(2)}, u32[]{:S(2)}) collective-permute-start(f32[56,384]{1,0:T(8,128)S(1)} %add.66), channel_id=1, source_target_pairs={{0,4},{1,5},{2,6},{3,7},{4,0},{5,1},{6,2},{7,3},{8,12},{9,13},{10,... | collective-permute-start | bytes 258056 | tf_op jit(solution)/shard_map/ppermute | solution.py:785
  442.7 19.0 %collective-permute-start.29 = (bf16[96,1536]{1,0:T(8,128)(2,1)S(1)}, bf16[96,1536]{1,0:T(8,128)(2,1)S(1)}, u32[]{:S(2)}, u32[]{:S(2)}) collective-permute-start(bf16[96,1536]{1,0:T(8,128)(2,1)S(1)} %join_rows.8.first_ref), channel_id=1, source_target_pairs={{0,1},{1,0},{2,3},{3,2},{4,5},{5,4},{6,7},{7,6},{8,9},{9,8},{10,11... | collective-permute-start | bytes 884744 | tf_op jit(solution)/shard_map/ppermute | solution.py:785
  456.9 13.6 %collective-permute-start.39 = (bf16[192,1536]{1,0:T(8,128)(2,1)S(1)}, bf16[192,1536]{1,0:T(8,128)(2,1)S(1)}, u32[]{:S(2)}, u32[]{:S(2)}) collective-permute-start(bf16[192,1536]{1,0:T(8,128)(2,1)S(1)} %add_rows.36.refs_0_), channel_id=1, source_target_pairs={{0,16},{8,24},{16,0},{24,8},{1,17},{9,25},{17,1},{25,9},{2,18},{10... | collective-permute-start | bytes 1769480 | tf_op jit(solution)/shard_map/ppermute | solution.py:785
  458.6 14.2 %collective-permute-start.47 = (bf16[192,1536]{1,0:T(8,128)(2,1)S(1)}, bf16[192,1536]{1,0:T(8,128)(2,1)S(1)}, u32[]{:S(2)}, u32[]{:S(2)}) collective-permute-start(bf16[192,1536]{1,0:T(8,128)(2,1)S(1)} %join_rows.13.refs_4_), channel_id=1, source_target_pairs={{0,1},{1,0},{2,3},{3,2},{4,5},{5,4},{6,7},{7,6},{8,9},{9,8},{10,11... | collective-permute-start | bytes 1769480 | tf_op jit(solution)/shard_map/ppermute | solution.py:785
  461.7 14.0 %collective-permute-start.30 = (bf16[192,1536]{1,0:T(8,128)(2,1)S(1)}, bf16[192,1536]{1,0:T(8,128)(2,1)S(1)}, u32[]{:S(2)}, u32[]{:S(2)}) collective-permute-start(bf16[192,1536]{1,0:T(8,128)(2,1)S(1)} %join_rows.9.refs_0_), channel_id=1, source_target_pairs={{0,8},{8,0},{16,24},{24,16},{1,9},{9,1},{17,25},{25,17},{2,10},{10... | collective-permute-start | bytes 1769480 | tf_op jit(solution)/shard_map/ppermute | solution.py:785
  463.7 13.6 %collective-permute-start.40 = (bf16[192,1536]{1,0:T(8,128)(2,1)S(1)}, bf16[192,1536]{1,0:T(8,128)(2,1)S(1)}, u32[]{:S(2)}, u32[]{:S(2)}) collective-permute-start(bf16[192,1536]{1,0:T(8,128)(2,1)S(1)} %add_rows.36.refs_0_), channel_id=1, source_target_pairs={{0,8},{8,0},{16,24},{24,16},{1,9},{9,1},{17,25},{25,17},{2,10},{10... | collective-permute-start | bytes 1769480 | tf_op jit(solution)/shard_map/ppermute | solution.py:785
  463.8 13.6 %collective-permute-start.48 = (bf16[192,1536]{1,0:T(8,128)(2,1)S(1)}, bf16[192,1536]{1,0:T(8,128)(2,1)S(1)}, u32[]{:S(2)}, u32[]{:S(2)}) collective-permute-start(bf16[192,1536]{1,0:T(8,128)(2,1)S(1)} %join_rows.13.refs_4_), channel_id=1, source_target_pairs={{0,8},{8,0},{16,24},{24,16},{1,9},{9,1},{17,25},{25,17},{2,10},{10... | collective-permute-start | bytes 1769480 | tf_op jit(solution)/shard_map/ppermute | solution.py:785
  470.5 6.8 %collective-permute-start.41 = (bf16[192,1536]{1,0:T(8,128)(2,1)S(1)}, bf16[192,1536]{1,0:T(8,128)(2,1)S(1)}, u32[]{:S(2)}, u32[]{:S(2)}) collective-permute-start(bf16[192,1536]{1,0:T(8,128)(2,1)S(1)} %collective-permute-done.39.refs_1_), channel_id=1, source_target_pairs={{0,8},{8,0},{16,24},{24,16},{1,9},{9,1},{17,25},{25,17},{2,10},{10... | collective-permute-start | bytes 1769480 | tf_op jit(solution)/shard_map/ppermute | solution.py:785
  472.9 4.5 collective-permute-start.49
  (39 other events, 189.5 us)
